TPU v7x, 128 devices: a whole 4x4x4 slice. The times are simulated.
128 devices in a mesh: row: 16 (over y, x), col: 8 (over z, core).
Axes of the slice: x: 4, y: 4, z: 4, core: 2. Of those that a mesh axis runs over, the one named last changes fastest.
Arguments:
- grad: bfloat16 [18432, 128, 128], P(('row', 'col')), may hold values from -6 to 6
- error: float32 [18432, 128, 128], P(('row', 'col')), may hold values from -4 to 4
- sel_blocks: int32 [128, 7], P(('row', 'col')), may hold values from 0 to 144, as said below
- row_bounds: int32 [17], replicated, may hold values from 0 to 24, as said below
- col_bounds: int32 [9], replicated, may hold values from 0 to 6, as said below
- master: float32 [256, 128, 128], P(('row', 'col')), may hold values from -6 to 6
- moment1: float32 [256, 128, 128], P(('row', 'col')), may hold values from -0.06 to 0.06
- moment2: float32 [256, 128, 128], P(('row', 'col')), may hold values from 1e-05 to 0.001
Outputs:
- error_out: float32 [18432, 128, 128], P(('row', 'col'))
- master_out: float32 [256, 128, 128], P(('row', 'col'))
- moment1_out: float32 [256, 128, 128], P(('row', 'col'))
- moment2_out: float32 [256, 128, 128], P(('row', 'col'))
- step_blocks: bfloat16 [144, 128, 128], replicated
Inputs may be any that keep to these rules, and one draw needn't show every extreme that they name: `sel_blocks`: each row lists distinct block numbers below 144, then pads with 144; some row lists 7 blocks. `row_bounds`: starts at 0, never falls, ends at 24; a band holds 1 to 2 block rows and some band holds 2. `col_bounds`: starts at 0, never falls, ends at 6; a band holds 0 to 1 block columns and some band holds 1.
All inputs are finite; a program needn't handle non-finite values.
Results may differ from a plain program's by a relative error of at most 0.001.
Values may be sent and summed in bfloat16 or wider, within the bound.
No kernel may reach another device: no remote copies, remote signals or barrier semaphores. Data moves between devices by JAX's collectives and lax.ppermute only.
A program may use at most 128 MiB of HBM per device.

v0:
```python
import jax
import jax.numpy as jnp
from jax import lax
from jax.sharding import PartitionSpec as P

CMAX = 1


BETA_ONE = 0.9
BETA_TWO = 0.95
EPSILON = 1e-08
DECAY_RATE = 0.1
LEARN_RATE = 0.01
CORRECT_ONE = 1.0 - 0.9**10
CORRECT_TWO = 1.0 - 0.95**10


def band_of(bounds, positions):
    inner_cuts = bounds[1:-1]
    return jnp.sum((inner_cuts[None, :] <= positions[:, None]).astype(jnp.int32), axis=1)


def adamw_update(totals, master, moment1, moment2, worker_sequence):
    averaged = totals / worker_sequence
    first = BETA_ONE * moment1 + (1.0 - BETA_ONE) * averaged
    second = BETA_TWO * moment2 + (1.0 - BETA_TWO) * averaged * averaged
    direction = (
        first / CORRECT_ONE / (jnp.sqrt(second / CORRECT_TWO) + EPSILON) + DECAY_RATE * master
    )
    return (master - LEARN_RATE * direction, first, second, direction)


def slot_positions(block_ids, row_bounds, col_bounds, grid_cols, owned_slots):
    grid_row = block_ids // grid_cols
    grid_col = block_ids % grid_cols
    row_band = band_of(row_bounds, grid_row)
    col_band = band_of(col_bounds, grid_col)
    offset_in = (grid_row - row_bounds[row_band]) * CMAX + (grid_col - col_bounds[col_band])
    return row_band * owned_slots + offset_in


def coalesce(got_vals, got_ids, positions, slots_total, blocks_all):
    block_ids = got_ids.reshape(-1)
    usable = block_ids < blocks_all
    block_side = got_vals.shape[-1]
    onehot_table = (
        (positions[None, :] == jnp.arange(slots_total)[:, None]) & usable[None, :]
    ).astype(jnp.float32)
    flat_vals = got_vals.reshape(block_ids.shape[0], block_side * block_side)
    summed = jnp.dot(onehot_table, flat_vals, precision=lax.Precision.HIGHEST)
    return (summed.reshape(slots_total, block_side, block_side), jnp.sum(onehot_table, axis=1))


def local(grad, error, sel_blocks, row_bounds, col_bounds, master, moment1, moment2):
    row_count = lax.axis_size("row")
    col_count = lax.axis_size("col")
    grid_cols = col_count - col_count // 4
    blocks_all = grad.shape[0]
    owned_slots = master.shape[0]
    accumulated = grad.astype(jnp.float32) + error
    picked = sel_blocks[0]
    usable = picked < blocks_all
    blocks = jnp.arange(blocks_all, dtype=jnp.int32)
    chosen = jnp.sum((picked[:, None] == blocks[None, :]).astype(jnp.float32), axis=0)
    error_out = accumulated * (1.0 - chosen)[:, None, None]
    values = (
        jnp.take(accumulated, jnp.minimum(picked, blocks_all - 1), axis=0)
        * usable.astype(jnp.float32)[:, None, None]
    )
    destination = band_of(col_bounds, picked % grid_cols)
    send_mask = (destination[None, :] == jnp.arange(col_count)[:, None]) & usable[None, :]
    send_vals = jnp.where(send_mask[:, :, None, None], values[None], 0.0)
    send_ids = jnp.where(send_mask, picked[None, :], blocks_all)
    got_vals, got_ids = (
        lax.all_to_all(send_vals, "col", split_axis=0, concat_axis=0, tiled=True),
        lax.all_to_all(send_ids, "col", split_axis=0, concat_axis=0, tiled=True),
    )
    safe_ids = jnp.minimum(got_ids.reshape(-1), blocks_all - 1)
    positions = slot_positions(safe_ids, row_bounds, col_bounds, grid_cols, owned_slots)
    summed, counts = coalesce(got_vals, got_ids, positions, row_count * owned_slots, blocks_all)
    owned_sums, owned_counts = (
        lax.psum_scatter(summed, "row", scatter_dimension=0, tiled=True),
        lax.psum_scatter(counts, "row", scatter_dimension=0, tiled=True),
    )
    changed = owned_counts > 0.5
    new_master, first, second, direction = adamw_update(
        owned_sums, master, moment1, moment2, row_count * col_count
    )
    flags = changed[:, None, None]
    master_out = jnp.where(flags, new_master, master)
    moment1_out = jnp.where(flags, first, moment1)
    moment2_out = jnp.where(flags, second, moment2)
    step_slots = jnp.where(flags, direction, 0.0).astype(jnp.bfloat16)
    block_row = blocks // grid_cols
    block_col = blocks % grid_cols
    row_band = band_of(row_bounds, block_row)
    every_step = lax.all_gather(step_slots, ("row", "col"), axis=0, tiled=True)
    col_band = band_of(col_bounds, block_col)
    slot_of = (
        (row_band * col_count + col_band) * owned_slots
        + (block_row - row_bounds[row_band]) * CMAX
        + (block_col - col_bounds[col_band])
    )
    step_blocks = jnp.take(every_step, slot_of, axis=0)
    return (error_out, master_out, moment1_out, moment2_out, step_blocks)


def solution(mesh):
    return jax.shard_map(
        local,
        mesh=mesh,
        in_specs=(
            P(("row", "col"), None, None),
            P(("row", "col"), None, None),
            P(("row", "col"), None),
            P(),
            P(),
            P(("row", "col"), None, None),
            P(("row", "col"), None, None),
            P(("row", "col"), None, None),
        ),
        out_specs=(
            P(("row", "col"), None, None),
            P(("row", "col"), None, None),
            P(("row", "col"), None, None),
            P(("row", "col"), None, None),
            P(),
        ),
        check_vma=False,
    )
```

profile of v0, /device:TPU:1, one launch (start us, length us, event | category | flops | bytes accessed | tf_op | source)
XLA Modules:
  0.0 263.8 jit_solution(576636188591537662)
XLA Ops:
  7.2 0.7 compare_bitcast_fusion
  7.8 0.7 and_select_fusion.7
  8.5 0.7 slice.10
  9.2 0.2 convert_reduce_fusion.6
  9.4 1.3 and_select_fusion
  10.7 6.8 %all-to-all-start = ((s32[8,1,7]{2,1,0:T(1,128)}), s32[8,1,7]{2,1,0:T(1,128)S(1)}, u32[]{:S(2)}, u32[]{:S(2)}) async-start(s32[8,1,7]{2,1,0:T(1,128)} %and_select_fusion), calls=%async_computation | async-start | bytes 8192 | tf_op jit(solution)/shard_map/all_to_all | solution.py:76
  17.5 0.7 fusion.21
  18.1 0.7 convert_reduce_fusion.4
  18.9 0.7 compare_and_fusion.1
  19.6 10.5 %broadcast_multiply_fusion = (f32[144,128,128]{2,1,0:T(8,128)}, f32[144,128,128]{2,1,0:T(8,128)}) fusion(f32[144]{0:T(256)S(1)} %broadcast_subtract_fusion, f32[144,128,128]{2,1,0:T(8,128)} %param.9, bf16[144,128,128]{2,1,0:T(8,128)(2,1)} %param.8), kind=kLoop, calls=%fused_computation.4 | loop fusion | flops 7077888 | bytes 33030720 | tf_op jit(solution)/shard_map/mul | solution.py:65
  30.0 4.3 %gather_fusion.1 = f32[7,128,128]{2,1,0:T(8,128)S(1)} fusion(f32[144,128,128]{2,1,0:T(8,128)} %get-tuple-element.39, s32[1024]{0:T(1024)S(1)} %pad_clamp_fusion.1), kind=kCustom, calls=%fused_computation.1 | custom fusion | bytes 917532 | tf_op jit(solution)/shard_map/jit(_take)/gather | solution.py:67
  34.3 0.1 select_multiply_fusion
  34.4 0.0 copy-start
  34.5 2.1 broadcast_select_fusion.1
  36.6 4.8 %all-to-all-start.1 = ((f32[8,7,128,128]{3,2,1,0:T(8,128)}), f32[8,7,128,128]{3,2,1,0:T(8,128)}, u32[]{:S(2)}, u32[]{:S(2)}) async-start(f32[8,7,128,128]{3,2,1,0:T(8,128)} %broadcast_select_fusion.1), calls=%async_computation.1 | async-start | bytes 7340032 | tf_op jit(solution)/shard_map/all_to_all | solution.py:75
  41.4 0.1 slice.4
  41.5 0.7 fusion.23
  42.2 0.1 lt.124
  42.3 0.1 ne.156
  42.5 0.1 rem.87
  42.5 0.1 div.61
  42.6 0.1 convert_reduce_fusion.3
  42.7 0.8 gather_fusion
  43.5 0.1 convert_reduce_fusion.5
  43.6 5.8 %multiply_add_fusion.3 = s32[56]{0:T(128)S(1)} fusion(s32[56]{0:T(128)S(1)} %convert_reduce_fusion.3, s32[56]{0:T(128)S(1)} %convert_reduce_fusion.5, s32[56]{0:T(128)S(1)} %get-tuple-element.72, s32[56]{0:T(128)S(1)} %gather_fusion, s32[]{:T(128)} %bitcast.9, s32[]{:T(128)} %bitcast.10, s32[]{:T(128)} %bitcast.11, s32[]{:T(128)} %bitcast.12, s32[]{:T(128)} %bitcast.13, ...), kind=kLoop, calls=%fused_computation.114 | loop fusion | flops 1624 | bytes 1380 | tf_op jit(solution)/shard_map/add | solution.py:39
  49.4 35.3 %all-to-all-done.1 = f32[8,7,128,128]{3,2,1,0:T(8,128)} async-done(((f32[8,7,128,128]{3,2,1,0:T(8,128)}), f32[8,7,128,128]{3,2,1,0:T(8,128)}, u32[]{:S(2)}, u32[]{:S(2)}) %all-to-all-start.1) | async-done | bytes 3670048 | tf_op jit(solution)/shard_map/all_to_all | solution.py:75
  84.7 5.7 %fusion = f32[32,128,128]{2,0,1:T(8,128)S(1)} fusion(s32[56]{0:T(128)S(1)} %multiply_add_fusion.3, pred[56]{0:T(512)(128)(4,1)S(1)} %lt.124, f32[7,8,128,128]{3,2,1,0:T(8,128)} %bitcast.49), kind=kOutput, calls=%fused_computation.7 | convolution fusion | flops 352325120 | bytes 5767448 | tf_op jit(solution)/shard_map/dot_general | solution.py:50
  90.4 2.5 copy.41
  92.9 0.0 reduce-scatter.2.cloned.1.call-update
  93.0 0.0 all-gather.2.cloned.1.call-start
  93.0 0.7 dynamic-slice
  94.4 0.1 convert_reduce_fusion.1
  94.5 33.5 %all-reduce = f32[32]{0:T(128)S(1)} all-reduce(f32[32]{0:T(128)S(1)} %convert_reduce_fusion.1), channel_id=2, replica_groups=mesh['row'=16,'col'=8] {'row'}, use_global_device_ids=true, to_apply=%region_5.6.clone | all-reduce | flops 32 | bytes 256
  127.9 0.1 dynamic-slice_compare_fusion
  128.0 37.4 %reduce-scatter.2.cloned.1.call-done = f32[2,128,128]{2,1,0:T(8,128)} async-done(((f32[32,128,128]{2,1,0:T(8,128)}), f32[2,128,128]{2,1,0:T(8,128)}) %reduce-scatter.2.cloned.1.call-update) | async-done | bytes 131088 | tf_op jit(solution)/shard_map/reduce_scatter | solution.py:82
  165.4 1.7 select_convert_fusion
  167.1 0.0 all-gather.2.cloned.1.call-update
  167.2 0.7 fusion.22
  167.9 0.1 convert_reduce_fusion
  168.0 0.1 convert_reduce_fusion.2
  168.1 4.5 %compare_select_fusion.9 = (s32[144,1]{0,1:T(1,128)S(1)}, s32[144,1]{0,1:T(1,128)S(1)}) fusion(s32[]{:T(128)} %bitcast.32, s32[]{:T(128)} %bitcast.33, s32[]{:T(128)} %bitcast.34, s32[]{:T(128)} %bitcast.35, s32[]{:T(128)} %bitcast.36, s32[]{:T(128)} %bitcast.38, s32[]{:T(128)} %bitcast.37, s32[144,1]{0,1:T(1,128)S(1)} %bitcast.100), kind=kLoop, calls=%fused_computation.63 | loop fusion | flops 2160 | bytes 1756 | tf_op jit(solution)/shard_map/gather | solution.py:101
  172.5 0.1 compare_reduce_fusion.3
  172.6 4.5 %compare_select_fusion.3 = s32[144,1]{0,1:T(1,128)S(1)} fusion(s32[]{:T(128)} %bitcast.9, s32[]{:T(128)} %bitcast.10, s32[]{:T(128)} %bitcast.11, s32[]{:T(128)} %bitcast.12, s32[]{:T(128)} %bitcast.13, s32[]{:T(128)} %bitcast.15, s32[]{:T(128)} %bitcast.14, s32[144,1]{0,1:T(1,128)S(1)} %bitcast.98), kind=kLoop, calls=%fused_computation.47 | loop fusion | flops 2160 | bytes 1180 | tf_op jit(solution)/shard_map/gather | solution.py:102
  177.1 7.4 %compare_and_fusion = (pred[144]{0:T(512)(128)(4,1)S(1)}, s32[144]{0:T(256)S(1)}, s32[144]{0:T(256)S(1)}) fusion(s32[144]{0:T(256)S(1)} %convert_reduce_fusion.2, s32[144]{0:T(256)S(1)} %convert_reduce_fusion, pred[144]{0:T(512)(128)(4,1)S(1)} %get-tuple-element.73, pred[144]{0:T(512)(128)(4,1)S(1)} %get-tuple-element.74, ...), kind=kLoop, calls=%fused_computation.91 | loop fusion | flops 5328 | bytes 5376 | tf_op jit(solution)/shard_map/jit(_take)/and | solution.py:104
  184.5 1.7 fusion.4
  186.2 54.8 %all-gather.2.cloned.1.call-done = bf16[256,128,128]{2,1,0:T(8,128)(2,1)} async-done(((bf16[2,128,128]{2,1,0:T(8,128)(2,1)}), bf16[256,128,128]{2,1,0:T(8,128)(2,1)}) %all-gather.2.cloned.1.call-update) | async-done | bytes 8388624 | tf_op jit(solution)/shard_map/all_gather | solution.py:97
  241.0 11.0 %gather_fusion.2 = bf16[144,128,128]{2,1,0:T(8,128)(2,1)} fusion(bf16[256,128,128]{2,1,0:T(8,128)(2,1)} %all-gather.2.cloned.1.call-done, s32[1024]{0:T(1024)S(1)} %pad_clamp_fusion), kind=kCustom, calls=%fused_computation.2 | custom fusion | bytes 9437760 | tf_op jit(solution)/shard_map/jit(_take)/gather | solution.py:104
  251.9 5.0 %broadcast_select_fusion = bf16[144,128,128]{2,1,0:T(8,128)(2,1)} fusion(bf16[144,128,128]{2,1,0:T(8,128)(2,1)} %gather_fusion.2, pred[144]{0:T(512)(128)(4,1)S(1)} %get-tuple-element.31), kind=kLoop, calls=%fused_computation.5 | loop fusion | flops 2359296 | bytes 9437328 | tf_op jit(solution)/shard_map/jit(_take)/select_n | solution.py:104
  (25 shorter events, 0.2 us)
Async XLA Ops:
  10.7 25.9 %all-to-all-start = ((s32[8,1,7]{2,1,0:T(1,128)}), s32[8,1,7]{2,1,0:T(1,128)S(1)}, u32[]{:S(2)}, u32[]{:S(2)}) async-start(s32[8,1,7]{2,1,0:T(1,128)} %and_select_fusion), calls=%async_computation | async-start | bytes 8192 | tf_op jit(solution)/shard_map/all_to_all | solution.py:76
  34.4 7.0 %copy-start = (s32[17]{0:T(128)S(1)}, s32[17]{0:T(128)}, u32[]{:S(2)}) copy-start(s32[17]{0:T(128)} %param.11) | copy-start | bytes 208
  34.4 7.0 %copy-start.4 = (s32[9]{0:T(128)S(1)}, s32[9]{0:T(128)}, u32[]{:S(2)}) copy-start(s32[9]{0:T(128)} %param.12) | copy-start | bytes 112
  36.6 48.1 %all-to-all-start.1 = ((f32[8,7,128,128]{3,2,1,0:T(8,128)}), f32[8,7,128,128]{3,2,1,0:T(8,128)}, u32[]{:S(2)}, u32[]{:S(2)}) async-start(f32[8,7,128,128]{3,2,1,0:T(8,128)} %broadcast_select_fusion.1), calls=%async_computation.1 | async-start | bytes 7340032 | tf_op jit(solution)/shard_map/all_to_all | solution.py:75
  41.4 124.0 %reduce-scatter.2.cloned.1.call-start = ((), (), s32[]{:S(2)}) async-start(), calls=%async_computation.3 | async-start | bytes 2228224 | tf_op jit(solution)/shard_map/reduce_scatter | solution.py:82
  84.7 8.3 %copy-start.5 = (u32[128]{0:T(128)S(1)}, u32[128]{0:T(128)}, u32[]{:S(2)}) copy-start(u32[128]{0:T(128)} %constant.159) | copy-start | bytes 1540
  84.7 80.7 %copy-start.1 = (f32[2,128,128]{2,1,0:T(8,128)S(1)}, f32[2,128,128]{2,1,0:T(8,128)}, u32[]{:S(2)}) copy-start(f32[2,128,128]{2,1,0:T(8,128)} %param.15) | copy-start | bytes 393220
  84.7 80.7 %copy-start.2 = (f32[2,128,128]{2,1,0:T(8,128)S(1)}, f32[2,128,128]{2,1,0:T(8,128)}, u32[]{:S(2)}) copy-start(f32[2,128,128]{2,1,0:T(8,128)} %param.14) | copy-start | bytes 393220
  84.7 80.7 %copy-start.3 = (f32[2,128,128]{2,1,0:T(8,128)S(1)}, f32[2,128,128]{2,1,0:T(8,128)}, u32[]{:S(2)}) copy-start(f32[2,128,128]{2,1,0:T(8,128)} %param.13) | copy-start | bytes 393220
  93.0 148.0 %all-gather.2.cloned.1.call-start = ((), (), s32[]{:S(2)}) async-start(), calls=%async_computation.4 | async-start | bytes 8454144 | tf_op jit(solution)/shard_map/all_gather | solution.py:97
Sparse Core Ops, SparseCore 0:
  93.1 72.3 reduce-scatter.1
  169.4 71.5 all-gather.1
where the time goes:
time: 265 us; the launch traced here: 264 us
  waiting for transfers between devices  127 us (48%)
  other arithmetic  48.8 us (18%)
  blocking collectives  33.5 us (13%)
  local copies, waits for them, and re-layouts  21.8 us (8%)
  between operations  14.9 us (6%)
  starting transfers between devices  11.7 us (4%)
  matrix products  5.67 us (2%)
    all_gather x1, waiting for transfers between devices, local(): every_step = lax.all_gather(step_slots, ('row', 'col'), axis=0, tiled=True)  54.8 us
    reduce_scatter x1, waiting for transfers between devices, local(): lax.psum_scatter(summed, 'row', scatter_dimension=0, tiled=True)  37.4 us
    all_to_all x1, waiting for transfers between devices, local(): lax.all_to_all(send_vals, 'col', split_axis=0, concat_axis=0, tiled=True)  35.3 us
    unnamed x1, blocking collectives  33.5 us
    gather x1, local copies, waits for them, and re-layouts, local(): step_blocks = jnp.take(every_step, slot_of, axis=0)  11 us
    mul x1, other arithmetic, local(): error_out = accumulated * (1.0 - chosen)[:, None, None]  10.5 us
    and x1, other arithmetic, local(): step_blocks = jnp.take(every_step, slot_of, axis=0)  7.37 us
    all_to_all x1, starting transfers between devices, local(): lax.all_to_all(send_ids, 'col', split_axis=0, concat_axis=0, tiled=True)  6.81 us
  transfers between devices with their start and end apart: 4, of which 3 were waited for; matrix products, arithmetic and copies ran while one was open for 18% of the time, Pallas kernels for 0%

commit v1 on v0

v1 whole, which is shorter than its diff:
```python
import jax
import jax.numpy as jnp
from jax import lax
from jax.experimental import pallas as pl
from jax.experimental.pallas import tpu as pltpu
from jax.sharding import Mesh
from jax.sharding import PartitionSpec as P

BS = 128
GC = 6
GR = 24
BLOCKS = 144
SEL = 7
OWNCAP = 2
N_ROW = 16
N_COL = 8
DEVICES = N_ROW * N_COL
CHIPS = DEVICES // 2
HALF = BS // 2

MSG = 16
ID_ROW = SEL
STATE_ROW = 8
EXT = 16
OUT_MSG = BLOCKS + EXT

BETA_ONE = 0.9
BETA_TWO = 0.95
EPSILON = 1e-08
DECAY_RATE = 0.1
LEARN_RATE = 0.01
CORRECT_ONE = 1.0 - 0.9**10
CORRECT_TWO = 1.0 - 0.95**10

F32 = jnp.float32
BF16 = jnp.bfloat16
I32 = jnp.int32
SMEM = pl.BlockSpec(memory_space=pltpu.SMEM)
VMEM = pl.BlockSpec(memory_space=pltpu.VMEM)
VMEM_LIMIT = 40 * 1024 * 1024


def adamw(totals, master, moment1, moment2):
    averaged = totals / DEVICES
    first = BETA_ONE * moment1 + (1.0 - BETA_ONE) * averaged
    second = BETA_TWO * moment2 + (1.0 - BETA_TWO) * averaged * averaged
    direction = first / CORRECT_ONE / (jnp.sqrt(second / CORRECT_TWO) + EPSILON) + DECAY_RATE * master
    return first, second, direction


def three_terms(x):
    high = x.astype(BF16)
    rest = x - high.astype(F32)
    middle = rest.astype(BF16)
    low = (rest - middle.astype(F32)).astype(BF16)
    return high, middle, low


def pack_kernel(sel_ref, *refs):
    grads, errors = refs[:SEL], refs[SEL : 2 * SEL]
    master, moment1, moment2, send = refs[2 * SEL :]

    def put(row, block):
        for core in range(2):
            send[pl.ds(core * MSG + row, CHIPS, stride=2 * MSG), :] = block[core * HALF : (core + 1) * HALF]

    for k in range(SEL):
        put(k, grads[k][0].astype(F32) + errors[k][0])
    lane = lax.broadcasted_iota(I32, (HALF, BS), 1)
    ids = jnp.zeros((HALF, BS), I32)
    for k in range(SEL):
        ids = jnp.where(lane == k, sel_ref[0, k], ids)
    ids = ids.astype(F32)
    put(ID_ROW, jnp.concatenate([ids, ids], axis=0))
    for s in range(OWNCAP):
        put(STATE_ROW + s, moment1[s])
        put(STATE_ROW + 2 + s, moment2[s])
        put(STATE_ROW + 4 + s, master[s])
    for row in (STATE_ROW + 6, STATE_ROW + 7):
        put(row, jnp.zeros((BS, BS), F32))


def pack(sel, grad, error, master, moment1, moment2):
    def chosen(k):
        return pl.BlockSpec((1, BS, BS), lambda i, sel_ref: (jnp.minimum(sel_ref[0, k], BLOCKS - 1), 0, 0))

    whole = pl.BlockSpec((OWNCAP, BS, BS), lambda i, sel_ref: (0, 0, 0))
    return pl.pallas_call(
        pack_kernel,
        grid_spec=pltpu.PrefetchScalarGridSpec(
            num_scalar_prefetch=1,
            grid=(1,),
            in_specs=[chosen(k) for k in range(SEL)] * 2 + [whole] * 3,
            out_specs=pl.BlockSpec((DEVICES * MSG, BS), lambda i, sel_ref: (0, 0)),
        ),
        out_shape=jax.ShapeDtypeStruct((DEVICES * MSG, BS), F32),
        compiler_params=pltpu.CompilerParams(vmem_limit_bytes=VMEM_LIMIT),
        cost_estimate=pl.CostEstimate(flops=200_000, bytes_accessed=2_200_000, transcendentals=0),
        name="pack_rows",
    )(sel, *[grad] * SEL, *[error] * SEL, master, moment1, moment2)


FEED = 8


def feedback_kernel(sel_ref, grad, error, out):
    first = pl.program_id(0) * FEED
    for b in range(FEED):
        hit = sel_ref[0, 0] == first + b
        for k in range(1, SEL):
            hit = jnp.logical_or(hit, sel_ref[0, k] == first + b)
        keep = 1.0 - hit.astype(F32)
        out[b] = (grad[b].astype(F32) + error[b]) * keep


def feedback(sel, grad, error):
    block = pl.BlockSpec((FEED, BS, BS), lambda i: (i, 0, 0))
    return pl.pallas_call(
        feedback_kernel,
        grid=(BLOCKS // FEED,),
        in_specs=[SMEM, block, block],
        out_specs=block,
        out_shape=jax.ShapeDtypeStruct((BLOCKS, BS, BS), F32),
        compiler_params=pltpu.CompilerParams(vmem_limit_bytes=VMEM_LIMIT),
        cost_estimate=pl.CostEstimate(flops=5_000_000, bytes_accessed=23_600_000, transcendentals=0),
        name="error_feedback",
    )(sel, grad, error)


def band(cuts, bands, positions):
    index = jnp.zeros_like(positions)
    start = jnp.zeros_like(positions)
    for k in range(1, bands):
        past = cuts[k] <= positions
        index = index + past.astype(I32)
        start = jnp.where(past, cuts[k], start)
    return index, start


def maps_kernel(place_ref, rows_ref, cols_ref, slot_map, block_map):
    block = lax.broadcasted_iota(I32, (BLOCKS, BS), 0)
    lane = lax.broadcasted_iota(I32, (BLOCKS, BS), 1)
    grid_row = block // GC
    grid_col = block - grid_row * GC
    row_band, row_start = band(rows_ref, N_ROW, grid_row)
    col_band, col_start = band(cols_ref, N_COL, grid_col)
    owner = row_band * N_COL + col_band
    slot = (grid_row - row_start) + (grid_col - col_start)
    for s in range(OWNCAP):
        slot_map[:, s * BS : (s + 1) * BS] = jnp.where((owner == lane) & (slot == s), 1.0, 0.0).astype(BF16)
    core = place_ref[0]
    chip = lax.broadcasted_iota(I32, (CHIPS, BS), 0)
    for t in range(2 * OWNCAP):
        holder = 2 * chip + (core if t < OWNCAP else 1 - core)
        band_row = holder // N_COL
        band_col = holder - band_row * N_COL
        top = jnp.zeros_like(chip)
        end = jnp.zeros_like(chip)
        for k in range(N_ROW):
            top = jnp.where(band_row == k, rows_ref[k], top)
            end = jnp.where(band_row == k, rows_ref[k + 1], end)
        left = jnp.zeros_like(chip)
        right = jnp.zeros_like(chip)
        for k in range(N_COL):
            left = jnp.where(band_col == k, cols_ref[k], left)
            right = jnp.where(band_col == k, cols_ref[k + 1], right)
        at_row = top + t % OWNCAP
        target = jnp.where((at_row < end) & (left < right), at_row * GC + left, -1)
        for part in range(2):
            lane = lax.broadcasted_iota(I32, (CHIPS, BS), 1) + part * BS
            block_map[t * CHIPS : (t + 1) * CHIPS, part * BS : (part + 1) * BS] = jnp.where(
                target == lane, 1.0, 0.0
            ).astype(BF16)


def maps(place, row_bounds, col_bounds):
    return pl.pallas_call(
        maps_kernel,
        in_specs=[SMEM] * 3,
        out_specs=[VMEM] * 2,
        out_shape=[
            jax.ShapeDtypeStruct((BLOCKS, OWNCAP * BS), BF16),
            jax.ShapeDtypeStruct((2 * OWNCAP * CHIPS, 2 * BS), BF16),
        ],
        cost_estimate=pl.CostEstimate(flops=500_000, bytes_accessed=300_000, transcendentals=0),
        name="slot_maps",
    )(place, row_bounds, col_bounds)


def directions_kernel(place_ref, rows_ref, cols_ref, got, slot_map, block_map, message, flags, tally_ref, ext):
    def rows(k):
        return got[pl.ds(k, DEVICES, stride=MSG), :]

    ids = jnp.transpose(rows(ID_ROW))
    block = lax.broadcasted_iota(I32, (BLOCKS, DEVICES), 0).astype(F32)
    picks = jnp.concatenate(
        [jnp.where(ids[k : k + 1] == block, 1.0, 0.0).astype(BF16) for k in range(SEL)], axis=1
    )
    values = jnp.concatenate([rows(k) for k in range(SEL)], axis=0)
    ones = jnp.ones((SEL * DEVICES, BS), BF16)
    sums = jnp.dot(picks, jnp.concatenate([*three_terms(values), ones], axis=1), preferred_element_type=F32)
    totals = (sums[:, :BS] + sums[:, BS : 2 * BS]) + sums[:, 2 * BS : 3 * BS]
    tallies = sums[:, 3 * BS :]
    tally_ref[...] = tallies

    states = []
    for array in range(3):
        held = jnp.concatenate([rows(STATE_ROW + 2 * array + s) for s in range(OWNCAP)], axis=0)
        states += three_terms(held)
    found = jnp.dot(slot_map[...], jnp.concatenate(states, axis=1), preferred_element_type=F32)
    term = [found[:, n * BS : (n + 1) * BS] for n in range(9)]
    moment1, moment2, master = [(term[3 * a] + term[3 * a + 1]) + term[3 * a + 2] for a in range(3)]

    direction = adamw(totals, master, moment1, moment2)[2]
    direction = jnp.where(tallies > 0.5, direction, 0.0).astype(BF16)
    for i in range(CHIPS):
        message[i, :BLOCKS] = direction

    padded = jnp.concatenate([totals, jnp.zeros((2 * BS - BLOCKS, BS), F32)], axis=0)
    owned = jnp.dot(block_map[...], jnp.concatenate(three_terms(padded), axis=1), preferred_element_type=F32)
    for p in range(3):
        for t in range(2 * OWNCAP):
            ext[pl.ds(2 * OWNCAP * p + t, CHIPS, stride=EXT), :] = owned[
                t * CHIPS : (t + 1) * CHIPS, p * BS : (p + 1) * BS
            ]
    for row in range(6 * OWNCAP, EXT):
        ext[pl.ds(row, CHIPS, stride=EXT), :] = jnp.zeros((CHIPS, BS), F32)
    for i in range(CHIPS):
        message[i, BLOCKS:] = ext[i * EXT : (i + 1) * EXT].astype(BF16)

    band_row = place_ref[1]
    band_col = place_ref[2]
    left = cols_ref[band_col]
    flags[...] = jnp.zeros_like(flags)
    for s in range(OWNCAP):
        at_row = rows_ref[band_row] + s
        inside = (at_row < rows_ref[band_row + 1]) & (left < cols_ref[band_col + 1])
        target = jnp.where(inside, at_row * GC + left, 0)
        flags[s : s + 1] = tally_ref[pl.ds(target, 1), :] * inside.astype(F32)


def directions(place, row_bounds, col_bounds, got, slot_map, block_map):
    return pl.pallas_call(
        directions_kernel,
        in_specs=[SMEM] * 3 + [VMEM] * 3,
        out_specs=[VMEM] * 2,
        out_shape=[
            jax.ShapeDtypeStruct((CHIPS, OUT_MSG, BS), BF16),
            jax.ShapeDtypeStruct((8, BS), F32),
        ],
        scratch_shapes=[pltpu.VMEM((BLOCKS, BS), F32), pltpu.VMEM((CHIPS * EXT, BS), F32)],
        compiler_params=pltpu.CompilerParams(vmem_limit_bytes=VMEM_LIMIT),
        cost_estimate=pl.CostEstimate(flops=200_000_000, bytes_accessed=4_000_000, transcendentals=20_000),
        name="directions",
    )(place, row_bounds, col_bounds, got, slot_map, block_map)


GROUP = 16


def turn(rows, out, scratch):
    scratch[...] = rows[...].astype(F32).reshape(CHIPS * GROUP, BS)
    for b in range(GROUP):
        out[b] = scratch[pl.ds(b, CHIPS, stride=GROUP), :].astype(BF16)


def own_half_kernel(place_ref, rows, out, scratch):
    turn(rows, out, scratch)


def own_half(place, mine):
    return pl.pallas_call(
        own_half_kernel,
        grid_spec=pltpu.PrefetchScalarGridSpec(
            num_scalar_prefetch=1,
            grid=(BLOCKS // GROUP,),
            in_specs=[pl.BlockSpec((CHIPS, GROUP, BS), lambda g, place_ref: (0, g, 0))],
            out_specs=pl.BlockSpec((GROUP, HALF, BS), lambda g, place_ref: (g, place_ref[0], 0)),
            scratch_shapes=[pltpu.VMEM((CHIPS * GROUP, BS), F32)],
        ),
        out_shape=jax.ShapeDtypeStruct((BLOCKS, BS, BS), BF16),
        compiler_params=pltpu.CompilerParams(vmem_limit_bytes=VMEM_LIMIT),
        cost_estimate=pl.CostEstimate(flops=2_000_000, bytes_accessed=4_700_000, transcendentals=0),
        name="own_half",
    )(place, mine)


def other_half_kernel(
    place_ref, steps, rows, mine_ext, theirs_ext, flags, master, moment1, moment2,
    out, master_out, moment1_out, moment2_out, scratch, totals,
):
    turn(rows, out, scratch)

    @pl.when(pl.program_id(0) == BLOCKS // GROUP - 1)
    def _():
        core = place_ref[0]
        for own, ext in ((True, mine_ext), (False, theirs_ext)):
            scratch[...] = ext[...].astype(F32).reshape(CHIPS * EXT, BS)
            at = pl.multiple_of((core if own else 1 - core) * HALF, HALF)
            for s in range(OWNCAP):
                first = s if own else OWNCAP + s
                part = [scratch[pl.ds(2 * OWNCAP * p + first, CHIPS, stride=EXT), :] for p in range(3)]
                totals[s, pl.ds(at, HALF), :] = (part[0] + part[1]) + part[2]
        for s in range(OWNCAP):
            changed = flags[s : s + 1] > 0.5
            new1, new2, direction = adamw(totals[s], master[s], moment1[s], moment2[s])
            master_out[s] = jnp.where(changed, master[s] - LEARN_RATE * direction, master[s])
            moment1_out[s] = jnp.where(changed, new1, moment1[s])
            moment2_out[s] = jnp.where(changed, new2, moment2[s])


def other_half(place, steps, mine, theirs, flags, master, moment1, moment2):
    ext = pl.BlockSpec((CHIPS, EXT, BS), lambda g, place_ref: (0, BLOCKS // EXT, 0))
    state = pl.BlockSpec((OWNCAP, BS, BS), lambda g, place_ref: (0, 0, 0))
    slots = jax.ShapeDtypeStruct((OWNCAP, BS, BS), F32)
    return pl.pallas_call(
        other_half_kernel,
        grid_spec=pltpu.PrefetchScalarGridSpec(
            num_scalar_prefetch=1,
            grid=(BLOCKS // GROUP,),
            in_specs=[
                pl.BlockSpec(memory_space=pl.ANY),
                pl.BlockSpec((CHIPS, GROUP, BS), lambda g, place_ref: (0, g, 0)),
                ext,
                ext,
                pl.BlockSpec((8, BS), lambda g, place_ref: (0, 0)),
                state,
                state,
                state,
            ],
            out_specs=[
                pl.BlockSpec((GROUP, HALF, BS), lambda g, place_ref: (g, 1 - place_ref[0], 0)),
                state,
                state,
                state,
            ],
            scratch_shapes=[pltpu.VMEM((CHIPS * GROUP, BS), F32), pltpu.VMEM((OWNCAP, BS, BS), F32)],
        ),
        out_shape=[jax.ShapeDtypeStruct((BLOCKS, BS, BS), BF16), slots, slots, slots],
        input_output_aliases={1: 0},
        compiler_params=pltpu.CompilerParams(vmem_limit_bytes=VMEM_LIMIT),
        cost_estimate=pl.CostEstimate(flops=3_000_000, bytes_accessed=6_500_000, transcendentals=0),
        name="other_half",
    )(place, steps, theirs, mine, theirs, flags, master, moment1, moment2)


def local(grad, error, sel_blocks, row_bounds, col_bounds, master, moment1, moment2):
    row, z, core = lax.axis_index("row"), lax.axis_index("z"), lax.axis_index("core")
    place = jnp.stack([core, row, 2 * z + core]).astype(I32)
    send = pack(sel_blocks, grad, error, master, moment1, moment2)
    got = lax.all_to_all(send, ("row", "z", "core"), split_axis=0, concat_axis=0, tiled=True)
    error_out = feedback(sel_blocks, grad, error)
    slot_map, block_map = maps(place, row_bounds, col_bounds)
    message, flags = directions(place, row_bounds, col_bounds, got, slot_map, block_map)
    mine = lax.all_to_all(
        message.reshape(CHIPS * OUT_MSG, BS), ("row", "z"), split_axis=0, concat_axis=0, tiled=True
    )
    theirs = lax.ppermute(mine, "core", [(0, 1), (1, 0)])
    mine = mine.reshape(CHIPS, OUT_MSG, BS)
    theirs = theirs.reshape(CHIPS, OUT_MSG, BS)
    steps = own_half(place, mine)
    steps, master_out, moment1_out, moment2_out = other_half(
        place, steps, mine, theirs, flags, master, moment1, moment2
    )
    return (error_out, master_out, moment1_out, moment2_out, steps)


def solution(mesh):
    cores = Mesh(mesh.devices.reshape(N_ROW, N_COL // 2, 2), ("row", "z", "core"))
    split = P(("row", "z", "core"))
    return jax.shard_map(
        local,
        mesh=cores,
        in_specs=(split, split, split, P(), P(), split, split, split),
        out_specs=(split, split, split, split, P()),
        check_vma=False,
    )
```

time: 265 us -> 110 us (0.42)
  waiting for transfers between devices: 127 us -> 16.5 us
  other arithmetic: 48.8 us -> 0.62 us
  Pallas kernels: 0 us -> 26.3 us
  between operations: 14.9 us -> 0.7 us
  local copies, waits for them, and re-layouts: 21.8 us -> 12.2 us
  matrix products: 5.67 us -> 0 us
  blocking collectives: 33.5 us -> 38.8 us
    all_gather x1 -> x0, waiting for transfers between devices: 54.8 us -> none  [local(): every_step = lax.all_gather(step_slots, ('row', 'col'), axis=0, tiled=True)]
    all_to_all x0 -> x1, blocking collectives: none -> 38.8 us  [local(): lax.all_to_all(message.reshape(CHIPS * OUT_MSG, BS), ('row', 'z'), split_...]
    reduce_scatter x1 -> x0, waiting for transfers between devices: 37.4 us -> none  [local(): lax.psum_scatter(summed, 'row', scatter_dimension=0, tiled=True)]
    unnamed x1 -> x0, blocking collectives: 33.5 us -> none
    pallas_call x0 -> x6, Pallas kernels: none -> 26.3 us  [the longest x1 8.41 us: feedback(): pl.pallas_call(feedback_kernel, grid=(BLOCKS // FEED,), in_specs=[SMEM, b...]
    all_to_all x2 -> x1, waiting for transfers between devices: 35.3 us -> 16.5 us  [local(): lax.all_to_all(send, ('row', 'z', 'core'), split_axis=0, concat_axis=0, t...]
    gather x5 -> x0, local copies, waits for them, and re-layouts: 17.4 us -> none  [the longest x1 11 us: local(): step_blocks = jnp.take(every_step, slot_of, axis=0)]
    unnamed x13 -> x34, local copies, waits for them, and re-layouts: 0.69 us -> 12.2 us
  transfers between devices with their start and end apart: 4 -> 2, of which waited for: 3 -> 1; matrix products, arithmetic and copies ran while one was open for 18% -> 1% of each run, Pallas kernels for 0% -> 14%
where the time goes in v1:
time: 110 us; the launch traced here: 109 us
  blocking collectives  38.8 us (35%)
  Pallas kernels  26.3 us (24%)
  waiting for transfers between devices  16.5 us (15%)
  starting transfers between devices  13.9 us (13%)
  local copies, waits for them, and re-layouts  12.2 us (11%)
    all_to_all x1, blocking collectives, local(): lax.all_to_all(message.reshape(CHIPS * OUT_MSG, BS), ('row', 'z'), split_...  38.8 us
    all_to_all x1, waiting for transfers between devices, local(): lax.all_to_all(send, ('row', 'z', 'core'), split_axis=0, concat_axis=0, t...  16.5 us
    unnamed x34, local copies, waits for them, and re-layouts  12.2 us
    all_to_all x1, starting transfers between devices, local(): lax.all_to_all(send, ('row', 'z', 'core'), split_axis=0, concat_axis=0, t...  11.5 us
    pallas_call x1, Pallas kernels, feedback(): pl.pallas_call(feedback_kernel, grid=(BLOCKS // FEED,), in_specs=[SMEM, b...  8.41 us
    pallas_call x1, Pallas kernels, other_half(): pl.pallas_call(other_half_kernel, grid_spec=pltpu.PrefetchScalarGridSpec(...  5.64 us
    pallas_call x1, Pallas kernels, own_half(): pl.pallas_call(own_half_kernel, grid_spec=pltpu.PrefetchScalarGridSpec(nu...  5.11 us
    pallas_call x1, Pallas kernels, pack(): pl.pallas_call(pack_kernel, grid_spec=pltpu.PrefetchScalarGridSpec(num_sc...  3.58 us
  transfers between devices with their start and end apart: 2, of which 1 were waited for; matrix products, arithmetic and copies ran while one was open for 1% of the time, Pallas kernels for 14%

profile of v1, /device:TPU:1, one launch (start us, length us, event | category | flops | bytes accessed | tf_op | source)
XLA Modules:
  0.0 109.1 jit_solution(6782862879086283962)
XLA Ops:
  0.6 0.0 copy-start.1
  0.6 2.3 %copy-done.1 = bf16[144,128,128]{2,1,0:T(8,128)(2,1)S(1)} copy-done((bf16[144,128,128]{2,1,0:T(8,128)(2,1)S(1)}, bf16[144,128,128]{2,1,0:T(8,128)(2,1)}, u32[]{:S(2)}) %copy-start.1) | copy-done | bytes 4718616
  3.0 0.0 copy-start.3
  3.0 0.9 copy-done.3
  3.9 0.0 copy-start.5
  3.9 0.9 copy-done.5
  4.8 0.0 copy-start.7
  4.8 0.9 copy-done.7
  5.7 0.0 copy-start.13
  5.7 0.7 copy-done.13
  6.3 0.0 copy-start.15
  6.3 0.0 copy-start.16
  6.3 3.6 %pack_rows.1 = f32[2048,128]{1,0:T(8,128)} custom-call(s32[1,7]{1,0:T(1,128)S(1)} %copy-done.13, bf16[144,128,128]{2,1,0:T(8,128)(2,1)S(1)} %copy-done.1, bf16[144,128,128]{2,1,0:T(8,128)(2,1)S(1)} %copy-done.1, bf16[144,128,128]{2,1,0:T(8,128)(2,1)S(1)} %copy-done.1, bf16[144,128,128]{2,1,0:T(8,128)(2,1)S(1)} %copy-done.1, ...), custom_call_target="tpu_custom_call" | custom-call | flops 200000 | bytes 2200000 | tf_op jit(solution)/shard_map/pack_rows/pallas_call | solution.py:88
  9.9 0.0 copy-start.14
  9.9 11.5 %all-to-all-start = ((f32[128,16,128]{2,1,0:T(8,128)}), f32[128,16,128]{2,1,0:T(8,128)S(1)}, u32[]{:S(2)}, u32[]{:S(2)}) async-start(f32[128,16,128]{2,1,0:T(8,128)} %bitcast.3), calls=%async_computation | async-start | bytes 2097152 | tf_op jit(solution)/shard_map/all_to_all | solution.py:351
  21.4 0.6 pad_add_fusion.place_ref
  22.1 2.0 %slot_maps.1 = (bf16[144,256]{1,0:T(8,128)(2,1)}, bf16[256,256]{1,0:T(8,128)(2,1)}) custom-call(s32[3]{0:T(128)} %pad_add_fusion.place_ref, s32[17]{0:T(128)} %rows_ref.3, s32[9]{0:T(128)} %cols_ref.3), custom_call_target="tpu_custom_call" | custom-call | flops 500000 | bytes 300000 | tf_op jit(solution)/shard_map/slot_maps/pallas_call | solution.py:177
  24.1 16.5 %all-to-all-done = f32[128,16,128]{2,1,0:T(8,128)S(1)} async-done(((f32[128,16,128]{2,1,0:T(8,128)}), f32[128,16,128]{2,1,0:T(8,128)S(1)}, u32[]{:S(2)}, u32[]{:S(2)}) %all-to-all-start) | async-done | bytes 1048608 | tf_op jit(solution)/shard_map/all_to_all | solution.py:351
  40.6 0.0 copy-start.2
  40.6 0.0 copy-done.15
  40.6 0.0 copy-done.16
  40.6 0.0 copy-start.9
  40.6 1.0 copy-done.9
  41.7 0.0 copy-start.10
  41.7 1.1 %copy-done.10 = bf16[144,256]{1,0:T(8,128)(2,1)S(1)} copy-done((bf16[144,256]{1,0:T(8,128)(2,1)S(1)}, bf16[144,256]{1,0:T(8,128)(2,1)}, u32[]{:S(2)}) %copy-start.10) | copy-done | bytes 73752
  42.8 0.0 copy-start.11
  42.8 0.6 copy-done.11
  43.4 1.5 %directions.1 = (bf16[64,160,128]{2,1,0:T(8,128)(2,1)S(1)}, f32[8,128]{1,0:T(8,128)S(1)}) custom-call(s32[3]{0:T(128)S(1)} %copy-done.11, s32[17]{0:T(128)S(1)} %copy-done.15, s32[9]{0:T(128)S(1)} %copy-done.16, f32[2048,128]{1,0:T(8,128)S(1)} %bitcast.10, bf16[144,256]{1,0:T(8,128)(2,1)S(1)} %copy-done.10, bf16[256,256]{1,0:T(8,128)(2,1)S(1)} %copy-done.9), custom_call_target="tpu_custom_call" | custom-call | flops 200000000 | bytes 4000000 | tf_op jit(solution)/shard_map/directions/pallas_call | solution.py:243
  45.0 38.8 %all_to_all.20.rows.mine_ext = bf16[64,160,128]{2,1,0:T(8,128)(2,1)S(1)} all-to-all(bf16[64,160,128]{2,1,0:T(8,128)(2,1)S(1)} %get-tuple-element.15), channel_id=1, replica_groups=mesh['row'=16,'z'=4,'core'=2] {'row','z'}, dimensions={0} | all-to-all | bytes 5242880 | tf_op jit(solution)/shard_map/all_to_all | solution.py:355
  83.8 2.4 %collective-permute-start = (bf16[10240,128]{1,0:T(8,128)(2,1)S(1)}, bf16[10240,128]{1,0:T(8,128)(2,1)S(1)}, u32[]{:S(2)}, u32[]{:S(2)}) collective-permute-start(bf16[10240,128]{1,0:T(8,128)(2,1)S(1)} %bitcast.7), channel_id=1, source_target_pairs={{0,1},{1,0},{2,3},{3,2},{4,5},{5,4},{6,7},{7,6},{8,9},{9,8},{10,11... | collective-permute-start | bytes 7864328 | tf_op jit(solution)/shard_map/ppermute | solution.py:358
  86.2 0.0 copy-done.14
  86.2 0.0 copy-done.2
  86.2 0.0 copy-start
  86.2 3.7 %copy-done = f32[144,128,128]{2,1,0:T(8,128)S(1)} copy-done((f32[144,128,128]{2,1,0:T(8,128)S(1)}, f32[144,128,128]{2,1,0:T(8,128)}, u32[]{:S(2)}) %copy-start) | copy-done | bytes 9437208
  89.9 0.0 copy-start.12
  89.9 8.4 %error_feedback.1 = f32[144,128,128]{2,1,0:T(8,128)} custom-call(s32[1,7]{1,0:T(1,128)S(1)} %copy-done.14, bf16[144,128,128]{2,1,0:T(8,128)(2,1)S(1)} %copy-done.2, f32[144,128,128]{2,1,0:T(8,128)S(1)} %copy-done), custom_call_target="tpu_custom_call" | custom-call | flops 5000000 | bytes 23600000 | tf_op jit(solution)/shard_map/error_feedback/pallas_call | solution.py:118
  98.3 0.0 copy-done.12
  98.3 0.0 copy-start.4
  98.3 0.0 copy-start.6
  98.3 0.0 copy-start.8
  98.4 5.1 %own_half.1.steps = bf16[144,128,128]{2,1,0:T(8,128)(2,1)} custom-call(s32[3]{0:T(128)S(1)} %copy-done.12, bf16[64,160,128]{2,1,0:T(8,128)(2,1)S(1)} %all_to_all.20.rows.mine_ext), custom_call_target="tpu_custom_call" | custom-call | flops 2000000 | bytes 4700000 | tf_op jit(solution)/shard_map/own_half/pallas_call | solution.py:272
  103.5 0.0 collective-permute-done
  103.5 0.0 copy-done.4
  103.5 0.0 copy-done.6
  103.5 0.0 copy-done.8
  103.5 5.6 %other_half.1 = (bf16[144,128,128]{2,1,0:T(8,128)(2,1)}, f32[2,128,128]{2,1,0:T(8,128)}, f32[2,128,128]{2,1,0:T(8,128)}, f32[2,128,128]{2,1,0:T(8,128)}) custom-call(s32[3]{0:T(128)S(1)} %copy-done.12, bf16[144,128,128]{2,1,0:T(8,128)(2,1)} %own_half.1.steps, bf16[64,160,128]{2,1,0:T(8,128)(2,1)S(1)} %bitcast.8, ...), custom_call_target="tpu_custom_call", output_to_operand_aliasing={{0}: (1, {})} | custom-call | flops 3000000 | bytes 6500000 | tf_op jit(solution)/shard_map/other_half/pallas_call | solution.py:316
Async XLA Ops:
  0.6 2.3 %copy-start.1 = (bf16[144,128,128]{2,1,0:T(8,128)(2,1)S(1)}, bf16[144,128,128]{2,1,0:T(8,128)(2,1)}, u32[]{:S(2)}) copy-start(bf16[144,128,128]{2,1,0:T(8,128)(2,1)} %refs_6_.1) | copy-start | bytes 14155780
  3.0 0.9 copy-start.3
  3.9 0.9 copy-start.5
  4.8 0.9 copy-start.7
  5.7 0.7 copy-start.13
  6.3 34.3 %copy-start.15 = (s32[17]{0:T(128)S(1)}, s32[17]{0:T(128)}, u32[]{:S(2)}) copy-start(s32[17]{0:T(128)} %rows_ref.3) | copy-start | bytes 208
  6.3 34.3 %copy-start.16 = (s32[9]{0:T(128)S(1)}, s32[9]{0:T(128)}, u32[]{:S(2)}) copy-start(s32[9]{0:T(128)} %cols_ref.3) | copy-start | bytes 112
  9.9 76.3 %copy-start.14 = (s32[1,7]{1,0:T(1,128)S(1)}, s32[1,7]{1,0:T(1,128)}, u32[]{:S(2)}) copy-start(s32[1,7]{1,0:T(1,128)} %sel_ref.3) | copy-start | bytes 88
  9.9 30.7 %all-to-all-start = ((f32[128,16,128]{2,1,0:T(8,128)}), f32[128,16,128]{2,1,0:T(8,128)S(1)}, u32[]{:S(2)}, u32[]{:S(2)}) async-start(f32[128,16,128]{2,1,0:T(8,128)} %bitcast.3), calls=%async_computation | async-start | bytes 2097152 | tf_op jit(solution)/shard_map/all_to_all | solution.py:351
  40.6 45.6 %copy-start.2 = (bf16[144,128,128]{2,1,0:T(8,128)(2,1)S(1)}, bf16[144,128,128]{2,1,0:T(8,128)(2,1)}, u32[]{:S(2)}) copy-start(bf16[144,128,128]{2,1,0:T(8,128)(2,1)} %refs_6_.1) | copy-start | bytes 14155780
  40.6 1.1 copy-start.9
  41.7 1.1 %copy-start.10 = (bf16[144,256]{1,0:T(8,128)(2,1)S(1)}, bf16[144,256]{1,0:T(8,128)(2,1)}, u32[]{:S(2)}) copy-start(bf16[144,256]{1,0:T(8,128)(2,1)} %get-tuple-element.13.slot_map) | copy-start | bytes 221188
  42.8 0.6 copy-start.11
  83.8 19.7 %collective-permute-start = (bf16[10240,128]{1,0:T(8,128)(2,1)S(1)}, bf16[10240,128]{1,0:T(8,128)(2,1)S(1)}, u32[]{:S(2)}, u32[]{:S(2)}) collective-permute-start(bf16[10240,128]{1,0:T(8,128)(2,1)S(1)} %bitcast.7), channel_id=1, source_target_pairs={{0,1},{1,0},{2,3},{3,2},{4,5},{5,4},{6,7},{7,6},{8,9},{9,8},{10,11... | collective-permute-start | bytes 7864328 | tf_op jit(solution)/shard_map/ppermute | solution.py:358
  86.2 3.7 %copy-start = (f32[144,128,128]{2,1,0:T(8,128)S(1)}, f32[144,128,128]{2,1,0:T(8,128)}, u32[]{:S(2)}) copy-start(f32[144,128,128]{2,1,0:T(8,128)} %refs_13_.1) | copy-start | bytes 28311556
  89.9 8.4 %copy-start.12 = (s32[3]{0:T(128)S(1)}, s32[3]{0:T(128)}, u32[]{:S(2)}) copy-start(s32[3]{0:T(128)} %pad_add_fusion.place_ref) | copy-start | bytes 40
  98.3 5.1 %copy-start.4 = (f32[2,128,128]{2,1,0:T(8,128)S(1)}, f32[2,128,128]{2,1,0:T(8,128)}, u32[]{:S(2)}) copy-start(f32[2,128,128]{2,1,0:T(8,128)} %master.1) | copy-start | bytes 393220
  98.3 5.1 %copy-start.6 = (f32[2,128,128]{2,1,0:T(8,128)S(1)}, f32[2,128,128]{2,1,0:T(8,128)}, u32[]{:S(2)}) copy-start(f32[2,128,128]{2,1,0:T(8,128)} %moment1.1) | copy-start | bytes 393220
  98.3 5.1 %copy-start.8 = (f32[2,128,128]{2,1,0:T(8,128)S(1)}, f32[2,128,128]{2,1,0:T(8,128)}, u32[]{:S(2)}) copy-start(f32[2,128,128]{2,1,0:T(8,128)} %moment2.1) | copy-start | bytes 393220

commit v2 on v0

v2 whole, which is shorter than its diff:
```python
import jax
import jax.numpy as jnp
from jax import lax
from jax.experimental import pallas as pl
from jax.experimental.pallas import tpu as pltpu
from jax.sharding import Mesh
from jax.sharding import PartitionSpec as P

BS = 128
GC = 6
GR = 24
BLOCKS = 144
SEL = 7
OWNCAP = 2
N_ROW = 16
N_COL = 8
DEVICES = N_ROW * N_COL
PLANE = N_ROW

MSG = 8
STATE_ROW = 4
INFO_ROW = 7
SCALE_LANE = 8
UNIT = 2.0**26
STEPS = 32767.0
ROOT_STEPS = 65535.0
ROOT_LOW = 32768.0

BETA_ONE = 0.9
BETA_TWO = 0.95
EPSILON = 1e-08
DECAY_RATE = 0.1
LEARN_RATE = 0.01
CORRECT_ONE = 1.0 - 0.9**10
CORRECT_TWO = 1.0 - 0.95**10

F32 = jnp.float32
BF16 = jnp.bfloat16
I32 = jnp.int32
SMEM = pl.BlockSpec(memory_space=pltpu.SMEM)
VMEM = pl.BlockSpec(memory_space=pltpu.VMEM)
HBM = pl.BlockSpec(memory_space=pltpu.HBM)
ANY = pl.BlockSpec(memory_space=pl.ANY)
MIB = 1024 * 1024
PARAMS = pltpu.CompilerParams(vmem_limit_bytes=16 * MIB)
ALONE = pltpu.CompilerParams(vmem_limit_bytes=64 * MIB)
NEARLY_ALONE = pltpu.CompilerParams(vmem_limit_bytes=61 * MIB)


def adamw(totals, master, moment1, moment2):
    averaged = totals / DEVICES
    first = BETA_ONE * moment1 + (1.0 - BETA_ONE) * averaged
    second = BETA_TWO * moment2 + (1.0 - BETA_TWO) * averaged * averaged
    direction = first / CORRECT_ONE / (jnp.sqrt(second / CORRECT_TWO) + EPSILON) + DECAY_RATE * master
    return first, second, direction


def three_terms(x):
    high = x.astype(BF16)
    rest = x - high.astype(F32)
    middle = rest.astype(BF16)
    low = (rest - middle.astype(F32)).astype(BF16)
    return high, middle, low


def first_row(z, core):
    return core * (BS // 2) + z * PLANE


def pack_kernel(sel_hbm, grad, error, master, moment1, moment2, send, sel, grads, errors, states, sel_sem, sems):
    fetch_sel = pltpu.make_async_copy(sel_hbm, sel, sel_sem)
    fetch_sel.start()
    held = [
        pltpu.make_async_copy(array, states.at[n], sems.at[2 * SEL + n])
        for n, array in enumerate((moment1, moment2, master))
    ]
    for copy in held:
        copy.start()
    fetch_sel.wait()
    chosen = []
    for k in range(SEL):
        at = jnp.minimum(sel[0, k], BLOCKS - 1)
        chosen.append(pltpu.make_async_copy(grad.at[at], grads.at[k], sems.at[k]))
        chosen.append(pltpu.make_async_copy(error.at[at], errors.at[k], sems.at[SEL + k]))
    for copy in chosen:
        copy.start()

    def put(row, block):
        for col in range(N_COL):
            at = first_row(col // 2, col % 2)
            send[pl.ds(col * MSG + row, PLANE, stride=N_COL * MSG), :] = block[at : at + PLANE]

    lane = lax.broadcasted_iota(I32, (BS, BS), 1)
    info = jnp.zeros((BS, BS), I32)
    for k in range(SEL):
        info = jnp.where(lane == k, sel[0, k], info)

    def coded(n, info, block, root=False):
        scale = jnp.maximum(jnp.ceil(jnp.max(jnp.abs(block), axis=1, keepdims=True) * UNIT), 1.0)
        info = jnp.where(lane == SCALE_LANE + n, scale.astype(I32), info)
        if root:
            return jnp.round(block * (ROOT_STEPS * UNIT / scale) - ROOT_LOW).astype(I32), info
        return jnp.round(block * (STEPS * UNIT / scale)).astype(I32), info

    def put_pair(row, first, second):
        put(row, lax.shift_left(first, 16) | (second & 0xFFFF))

    for n in range(3):
        held[n].wait()
        pair = []
        for s in range(OWNCAP):
            block = states[n, s]
            code, info = coded(SEL + OWNCAP * n + s, info, jnp.sqrt(block) if n == 1 else block, n == 1)
            pair.append(code)
        put_pair(STATE_ROW + n, *pair)
    pair = []
    for k in range(SEL):
        chosen[2 * k].wait()
        chosen[2 * k + 1].wait()
        code, info = coded(k, info, grads[k].astype(F32) + errors[k])
        pair.append(code)
        if len(pair) == 2:
            put_pair(k // 2, *pair)
            pair = []
    put_pair(SEL // 2, pair[0], jnp.zeros((BS, BS), I32))
    put(INFO_ROW, info)


def pack(sel, grad, error, master, moment1, moment2):
    return pl.pallas_call(
        pack_kernel,
        in_specs=[HBM] * 6,
        out_specs=VMEM,
        out_shape=jax.ShapeDtypeStruct((DEVICES * MSG, BS), I32),
        scratch_shapes=[
            pltpu.SMEM((1, SEL), I32),
            pltpu.VMEM((SEL, BS, BS), BF16),
            pltpu.VMEM((SEL, BS, BS), F32),
            pltpu.VMEM((3, OWNCAP, BS, BS), F32),
            pltpu.SemaphoreType.DMA,
            pltpu.SemaphoreType.DMA((2 * SEL + 3,)),
        ],
        compiler_params=ALONE,
        cost_estimate=pl.CostEstimate(flops=200_000, bytes_accessed=2_200_000, transcendentals=0),
        name="pack_rows",
    )(sel, grad, error, master, moment1, moment2)


def band(cuts, bands, positions):
    index = jnp.zeros_like(positions)
    start = jnp.zeros_like(positions)
    for k in range(1, bands):
        past = cuts[k] <= positions
        index = index + past.astype(I32)
        start = jnp.where(past, cuts[k], start)
    return index, start


FEED = 18


def feedback(sel, grad, error, part, before):
    steps = BLOCKS // FEED // 2

    def kernel(*refs):
        sel, grad, error, out = *refs[:3], refs[-1]

        def step(grad_blocks, error_blocks, out_blocks):
            first = (part * steps + pl.program_id(0)) * FEED
            for b in range(FEED):
                hit = sel[0, 0] == first + b
                for k in range(1, SEL):
                    hit = jnp.logical_or(hit, sel[0, k] == first + b)
                keep = 1.0 - hit.astype(F32)
                out_blocks[b] = (grad_blocks[b].astype(F32) + error_blocks[b]) * keep

        block = pl.BlockSpec((FEED, BS, BS), lambda i: (part * steps + i, 0, 0))
        pltpu.emit_pipeline(step, grid=(steps,), in_specs=[block, block], out_specs=[block])(grad, error, out)

    more = [] if before is None else [before]
    return pl.pallas_call(
        kernel,
        in_specs=[SMEM] + [HBM] * 2 + [HBM] * len(more),
        out_specs=HBM,
        out_shape=jax.ShapeDtypeStruct((BLOCKS, BS, BS), F32),
        input_output_aliases={3: 0} if more else {},
        compiler_params=NEARLY_ALONE,
        cost_estimate=pl.CostEstimate(flops=2_500_000, bytes_accessed=11_800_000, transcendentals=0),
        name="error_feedback",
    )(sel, grad, error, *more)


def maps_kernel(rows_ref, cols_ref, slot_map, block_map, own_map):
    block = lax.broadcasted_iota(I32, (BLOCKS, BS), 0)
    lane = lax.broadcasted_iota(I32, (BLOCKS, BS), 1)
    grid_row = block // GC
    grid_col = block - grid_row * GC
    row_band, row_start = band(rows_ref, N_ROW, grid_row)
    col_band, col_start = band(cols_ref, N_COL, grid_col)
    owner = row_band * N_COL + col_band
    slot = (grid_row - row_start) + (grid_col - col_start)
    for s in range(OWNCAP):
        slot_map[:, s * BS : (s + 1) * BS] = jnp.where((owner == lane) & (slot == s), 1.0, 0.0).astype(BF16)
    holder = lax.broadcasted_iota(I32, (DEVICES * OWNCAP, BS), 0)
    slot = holder % OWNCAP
    holder = holder // OWNCAP
    band_row = holder // N_COL
    band_col = holder - band_row * N_COL
    top = jnp.zeros_like(holder)
    end = jnp.zeros_like(holder)
    for k in range(N_ROW):
        top = jnp.where(band_row == k, rows_ref[k], top)
        end = jnp.where(band_row == k, rows_ref[k + 1], end)
    left = jnp.zeros_like(holder)
    right = jnp.zeros_like(holder)
    for k in range(N_COL):
        left = jnp.where(band_col == k, cols_ref[k], left)
        right = jnp.where(band_col == k, cols_ref[k + 1], right)
    at_row = top + slot
    target = jnp.where((at_row < end) & (left < right), at_row * GC + left, -1)
    lane = lax.broadcasted_iota(I32, (DEVICES * OWNCAP, BS), 1)
    for part in range(2):
        block_map[:, part * BS : (part + 1) * BS] = jnp.where(target == lane + part * BS, 1.0, 0.0).astype(BF16)
    band_row = lax.axis_index("row")
    band_col = 2 * lax.axis_index("z") + lax.axis_index("core")
    slot = lax.broadcasted_iota(I32, (16, 2 * BS), 0)
    at_row = rows_ref[band_row] + slot
    left = cols_ref[band_col]
    inside = (slot < OWNCAP) & (at_row < rows_ref[band_row + 1]) & (left < cols_ref[band_col + 1])
    lane = lax.broadcasted_iota(I32, (16, 2 * BS), 1)
    own_map[...] = jnp.where(inside & (at_row * GC + left == lane), 1.0, 0.0).astype(BF16)


def maps(row_bounds, col_bounds):
    return pl.pallas_call(
        maps_kernel,
        in_specs=[SMEM] * 2,
        out_specs=[VMEM] * 3,
        out_shape=[
            jax.ShapeDtypeStruct((BLOCKS, OWNCAP * BS), BF16),
            jax.ShapeDtypeStruct((OWNCAP * DEVICES, 2 * BS), BF16),
            jax.ShapeDtypeStruct((16, 2 * BS), BF16),
        ],
        compiler_params=PARAMS,
        cost_estimate=pl.CostEstimate(flops=500_000, bytes_accessed=300_000, transcendentals=0),
        name="slot_maps",
    )(row_bounds, col_bounds)


def directions_kernel(got, slot_map, block_map, own_map, message, owned, flags):
    def rows(k):
        return got[pl.ds(k, DEVICES, stride=MSG), :]

    info = rows(INFO_ROW)

    def decoded(row, n):
        words = rows(row)
        for half in (lax.shift_right_arithmetic(words, 16), lax.shift_right_arithmetic(lax.shift_left(words, 16), 16)):
            if n < SEL or row > SEL // 2:
                scale = info[:, SCALE_LANE + n : SCALE_LANE + n + 1].astype(F32)
                if row == STATE_ROW + 1:
                    yield (half.astype(F32) + ROOT_LOW) * (scale * (1.0 / (ROOT_STEPS * UNIT)))
                else:
                    yield half.astype(F32) * (scale * (1.0 / (STEPS * UNIT)))
            n += 1

    ids = jnp.transpose(info.astype(F32))
    block = lax.broadcasted_iota(I32, (BLOCKS, DEVICES), 0).astype(F32)
    picks = jnp.concatenate(
        [jnp.where(ids[k : k + 1] == block, 1.0, 0.0).astype(BF16) for k in range(SEL)], axis=1
    )
    values = jnp.concatenate([value for row in range(STATE_ROW) for value in decoded(row, 2 * row)], axis=0)
    ones = jnp.ones((SEL * DEVICES, BS), BF16)
    sums = jnp.dot(picks, jnp.concatenate([*three_terms(values), ones], axis=1), preferred_element_type=F32)
    totals = (sums[:, :BS] + sums[:, BS : 2 * BS]) + sums[:, 2 * BS : 3 * BS]
    tallies = sums[:, 3 * BS :]

    states = []
    for array in range(3):
        held = jnp.concatenate(list(decoded(STATE_ROW + array, SEL + OWNCAP * array)), axis=0)
        states += three_terms(held)
    found = jnp.dot(slot_map[...], jnp.concatenate(states, axis=1), preferred_element_type=F32)
    term = [found[:, n * BS : (n + 1) * BS] for n in range(9)]
    moment1, root2, master = [(term[3 * a] + term[3 * a + 1]) + term[3 * a + 2] for a in range(3)]

    direction = adamw(totals, master, moment1, root2 * root2)[2]
    direction = jnp.where(tallies > 0.5, direction, 0.0).astype(BF16)
    for i in range(PLANE):
        message[i] = direction

    padded = jnp.concatenate([totals, jnp.zeros((2 * BS - BLOCKS, BS), F32)], axis=0)
    sums = jnp.dot(block_map[...], jnp.concatenate(three_terms(padded), axis=1), preferred_element_type=F32)
    owned[...] = (sums[:, :BS] + sums[:, BS : 2 * BS]) + sums[:, 2 * BS :]

    padded = jnp.concatenate([tallies, jnp.zeros((2 * BS - BLOCKS, BS), F32)], axis=0).astype(BF16)
    flags[...] = jnp.dot(own_map[...], padded, preferred_element_type=F32)


def directions(got, slot_map, block_map, own_map):
    return pl.pallas_call(
        directions_kernel,
        in_specs=[VMEM] * 4,
        out_specs=[VMEM] * 3,
        out_shape=[
            jax.ShapeDtypeStruct((PLANE, BLOCKS, BS), BF16),
            jax.ShapeDtypeStruct((OWNCAP * DEVICES, BS), F32),
            jax.ShapeDtypeStruct((16, BS), F32),
        ],
        compiler_params=PARAMS,
        cost_estimate=pl.CostEstimate(flops=200_000_000, bytes_accessed=2_000_000, transcendentals=20_000),
        name="directions",
    )(got, slot_map, block_map, own_map)


PITCH = BLOCKS + 1


def turn_kernel(rows, out, scratch):
    for chip in range(PLANE):
        scratch[pl.ds(chip * PITCH, BLOCKS), :] = rows[chip].astype(F32)
    for b in range(BLOCKS):
        out[b] = scratch[pl.ds(b, PLANE, stride=PITCH), :].astype(BF16)


def turn(rows):
    return pl.pallas_call(
        turn_kernel,
        in_specs=[VMEM],
        out_specs=VMEM,
        out_shape=jax.ShapeDtypeStruct((BLOCKS, PLANE, BS), BF16),
        scratch_shapes=[pltpu.VMEM((PLANE * PITCH, BS), F32)],
        compiler_params=PARAMS,
        cost_estimate=pl.CostEstimate(flops=600_000, bytes_accessed=1_200_000, transcendentals=0),
        name="turn",
    )(rows)


def place(steps, pieces):
    arrays = [a for piece in pieces for a in piece[2:]]

    def kernel(*refs):
        inputs, out, sems = refs[: len(arrays)], refs[-2], refs[-1]
        z, core = lax.axis_index("z"), lax.axis_index("core")
        copies = []
        for n, ref in enumerate(inputs):
            first, away = pieces[n // 2][:2]
            at = first_row(lax.rem(z + away, N_COL // 2), core if n % 2 == 0 else 1 - core)
            target = out.at[pl.ds(first, ref.shape[0]), pl.ds(pl.multiple_of(at, PLANE), PLANE)]
            copies.append(pltpu.make_async_copy(ref, target, sems.at[n]))
        for copy in copies:
            copy.start()
        for copy in copies:
            copy.wait()

    return pl.pallas_call(
        kernel,
        in_specs=[VMEM] * len(arrays) + ([] if steps is None else [HBM]),
        out_specs=HBM,
        out_shape=jax.ShapeDtypeStruct((BLOCKS, BS, BS), BF16),
        scratch_shapes=[pltpu.SemaphoreType.DMA((len(arrays),))],
        input_output_aliases={} if steps is None else {len(arrays): 0},
        compiler_params=PARAMS,
        cost_estimate=pl.CostEstimate(flops=0, bytes_accessed=2_400_000, transcendentals=0),
        name="place",
    )(*arrays, *([] if steps is None else [steps]))


def update_kernel(owned, flags, master, moment1, moment2, master_out, moment1_out, moment2_out, totals):
    for s in range(OWNCAP):
        for col in range(N_COL):
            at = first_row(col // 2, col % 2)
            totals[s, at : at + PLANE] = owned[pl.ds(col * OWNCAP + s, PLANE, stride=N_COL * OWNCAP), :]
        changed = flags[s : s + 1] > 0.5
        new1, new2, direction = adamw(totals[s], master[s], moment1[s], moment2[s])
        master_out[s] = jnp.where(changed, master[s] - LEARN_RATE * direction, master[s])
        moment1_out[s] = jnp.where(changed, new1, moment1[s])
        moment2_out[s] = jnp.where(changed, new2, moment2[s])


def update(owned, flags, master, moment1, moment2):
    slots = jax.ShapeDtypeStruct((OWNCAP, BS, BS), F32)
    return pl.pallas_call(
        update_kernel,
        in_specs=[VMEM] * 5,
        out_specs=[VMEM] * 3,
        out_shape=[slots] * 3,
        scratch_shapes=[pltpu.VMEM((OWNCAP, BS, BS), F32)],
        compiler_params=PARAMS,
        cost_estimate=pl.CostEstimate(flops=600_000, bytes_accessed=900_000, transcendentals=33_000),
        name="update",
    )(owned, flags, master, moment1, moment2)


RIGHT = [(i, (i + 1) % 4) for i in range(4)]
LEFT = [(i, (i + 3) % 4) for i in range(4)]


def local(grad, error, sel_blocks, row_bounds, col_bounds, master, moment1, moment2):
    send = pack(sel_blocks, grad, error, master, moment1, moment2)
    got = lax.all_to_all(send, ("row", "z", "core"), split_axis=0, concat_axis=0, tiled=True)
    slot_map, block_map, own_map = maps(row_bounds, col_bounds)
    error_out = feedback(sel_blocks, grad, error, 0, None)
    got, error_out = lax.optimization_barrier((got, error_out))
    message, owned, flags = directions(got, slot_map, block_map, own_map)

    message, error_out = lax.optimization_barrier((message, error_out))
    plane = lax.all_to_all(message.reshape(PLANE * BLOCKS, BS), "row", split_axis=0, concat_axis=0, tiled=True)
    error_out = feedback(sel_blocks, grad, error, 1, error_out)
    plane, error_out = lax.optimization_barrier((plane, error_out))
    mine = turn(plane.reshape(PLANE, BLOCKS, BS))
    mine, owned = lax.optimization_barrier((mine, owned))

    def swap(piece):
        return lax.ppermute(piece, "core", [(0, 1), (1, 0)])

    half = BLOCKS // 2
    before = lax.ppermute(mine, "z", RIGHT)
    after = lax.ppermute(mine, "z", LEFT)
    mine_too = swap(mine)
    owned = lax.all_to_all(owned, ("row", "z", "core"), split_axis=0, concat_axis=0, tiled=True)
    before, after, mine_too, owned = lax.optimization_barrier((before, after, mine_too, owned))
    far_first = lax.ppermute(before[:half], "z", RIGHT)
    far_last = lax.ppermute(after[half:], "z", LEFT)
    steps = place(None, [(0, 0, mine, mine_too), (0, 3, before, swap(before)), (0, 1, after, swap(after))])
    states = update(owned, flags, master, moment1, moment2)
    far_first, far_last, steps, states = lax.optimization_barrier((far_first, far_last, steps, states))
    steps = place(steps, [(0, 2, far_first, swap(far_first)), (half, 2, far_last, swap(far_last))])
    return (error_out, *states, steps)


def solution(mesh):
    cores = Mesh(mesh.devices.reshape(N_ROW, N_COL // 2, 2), ("row", "z", "core"))
    split = P(("row", "z", "core"))
    return jax.shard_map(
        local,
        mesh=cores,
        in_specs=(split, split, split, P(), P(), split, split, split),
        out_specs=(split, split, split, split, P()),
        check_vma=False,
    )
```

time: 265 us -> 81.7 us (0.31)
  waiting for transfers between devices: 127 us -> 16.3 us
  other arithmetic: 48.8 us -> 0 us
  Pallas kernels: 0 us -> 22.6 us
  local copies, waits for them, and re-layouts: 21.8 us -> 1.37 us
  blocking collectives: 33.5 us -> 17.8 us
  between operations: 14.9 us -> 0.74 us
  starting transfers between devices: 11.7 us -> 22.3 us
  matrix products: 5.67 us -> 0 us
    all_gather x1 -> x0, waiting for transfers between devices: 54.8 us -> none  [local(): every_step = lax.all_gather(step_slots, ('row', 'col'), axis=0, tiled=True)]
    reduce_scatter x1 -> x0, waiting for transfers between devices: 37.4 us -> none  [local(): lax.psum_scatter(summed, 'row', scatter_dimension=0, tiled=True)]
    unnamed x1 -> x0, blocking collectives: 33.5 us -> none
    all_to_all x2, waiting for transfers between devices: 35.3 us -> 9.63 us  [the longest x1 4.99 us: local(): lax.all_to_all(send, ('row', 'z', 'core'), split_axis=0, concat_axis=0, t...]
    pallas_call x0 -> x9, Pallas kernels: none -> 22.6 us  [the longest x2 12.6 us: feedback(): pl.pallas_call(kernel, in_specs=[SMEM] + [HBM] * 2 + [HBM] * len(more), o...]
    all_to_all x0 -> x1, blocking collectives: none -> 17.8 us  [local(): lax.all_to_all(owned, ('row', 'z', 'core'), split_axis=0, concat_axis=0,...]
    gather x5 -> x0, local copies, waits for them, and re-layouts: 17.4 us -> none  [the longest x1 11 us: local(): step_blocks = jnp.take(every_step, slot_of, axis=0)]
    select_n x11 -> x0, other arithmetic: 11.5 us -> none  [the longest x2 5.03 us: local(): step_blocks = jnp.take(every_step, slot_of, axis=0)]
  transfers between devices with their start and end apart: 4 -> 11, of which waited for: 3 -> 6; matrix products, arithmetic and copies ran while one was open for 18% -> 0% of each run, Pallas kernels for 0% -> 20%
where the time goes in v2:
time: 81.7 us; the launch traced here: 81.2 us
  Pallas kernels  22.6 us (28%)
  starting transfers between devices  22.3 us (27%)
  blocking collectives  17.8 us (22%)
  waiting for transfers between devices  16.3 us (20%)
  local copies, waits for them, and re-layouts  1.37 us (2%)
    all_to_all x1, blocking collectives, local(): lax.all_to_all(owned, ('row', 'z', 'core'), split_axis=0, concat_axis=0,...  17.8 us
    pallas_call x2, Pallas kernels, feedback(): pl.pallas_call(kernel, in_specs=[SMEM] + [HBM] * 2 + [HBM] * len(more), o...  12.6 us
    all_to_all x1, starting transfers between devices, local(): lax.all_to_all(send, ('row', 'z', 'core'), split_axis=0, concat_axis=0, t...  11.5 us
    all_to_all x1, waiting for transfers between devices, local(): lax.all_to_all(send, ('row', 'z', 'core'), split_axis=0, concat_axis=0, t...  4.99 us
    all_to_all x1, waiting for transfers between devices, local(): lax.all_to_all(message.reshape(PLANE * BLOCKS, BS), 'row', split_axis=0,...  4.64 us
    ppermute x5, starting transfers between devices, swap(): return lax.ppermute(piece, 'core', [(0, 1), (1, 0)])  4.25 us
    ppermute x1, waiting for transfers between devices, local(): far_last = lax.ppermute(after[half:], 'z', LEFT)  3.96 us
    pallas_call x1, Pallas kernels, pack(): pl.pallas_call(pack_kernel, in_specs=[HBM] * 6, out_specs=VMEM, out_shape...  3.63 us
  transfers between devices with their start and end apart: 11, of which 6 were waited for; matrix products, arithmetic and copies ran while one was open for 0% of the time, Pallas kernels for 20%

profile of v2, /device:TPU:1, one launch (start us, length us, event | category | flops | bytes accessed | tf_op | source)
XLA Modules:
  0.0 81.2 jit_solution(10090544920787647972)
XLA Ops:
  0.6 3.6 %pack_rows.1 = s32[1024,128]{1,0:T(8,128)} custom-call(s32[1,7]{1,0:T(1,128)} %refs_0_.3, bf16[144,128,128]{2,1,0:T(8,128)(2,1)} %refs_1_.3, f32[144,128,128]{2,1,0:T(8,128)} %refs_2_.3, f32[2,128,128]{2,1,0:T(8,128)} %master.3, f32[2,128,128]{2,1,0:T(8,128)} %moment1.3, f32[2,128,128]{2,1,0:T(8,128)} %moment2.3), custom_call_target="tpu_custom_call" | custom-call | flops 200000 | bytes 2200000 | tf_op jit(solution)/shard_map/pack_rows/pallas_call | solution.py:130
  4.3 11.5 %all-to-all-start = ((s32[128,8,128]{2,1,0:T(8,128)}), s32[128,8,128]{2,1,0:T(8,128)S(1)}, u32[]{:S(2)}, u32[]{:S(2)}) async-start(s32[128,8,128]{2,1,0:T(8,128)} %bitcast.9), calls=%async_computation | async-start | bytes 1048576 | tf_op jit(solution)/shard_map/all_to_all | solution.py:400
  15.8 0.0 copy-start.3
  15.8 0.6 copy-done.3
  16.4 0.0 copy-start.4
  16.4 0.7 copy-done.4
  17.1 1.0 %slot_maps.1 = (bf16[144,256]{1,0:T(8,128)(2,1)S(1)}, bf16[256,256]{1,0:T(8,128)(2,1)S(1)}, bf16[16,256]{1,0:T(8,128)(2,1)S(1)}) custom-call(s32[17]{0:T(128)S(1)} %copy-done.3, s32[9]{0:T(128)S(1)} %copy-done.4), custom_call_target="tpu_custom_call" | custom-call | flops 500000 | bytes 300000 | tf_op jit(solution)/shard_map/slot_maps/pallas_call | solution.py:235
  18.1 6.3 %error_feedback.2.refs_3_ = f32[144,128,128]{2,1,0:T(8,128)} custom-call(s32[1,7]{1,0:T(1,128)} %refs_0_.3, bf16[144,128,128]{2,1,0:T(8,128)(2,1)} %refs_1_.3, f32[144,128,128]{2,1,0:T(8,128)} %refs_2_.3), custom_call_target="tpu_custom_call" | custom-call | flops 2500000 | bytes 11800000 | tf_op jit(solution)/shard_map/error_feedback/pallas_call | solution.py:181
  24.4 5.0 %all-to-all-done = s32[128,8,128]{2,1,0:T(8,128)S(1)} async-done(((s32[128,8,128]{2,1,0:T(8,128)}), s32[128,8,128]{2,1,0:T(8,128)S(1)}, u32[]{:S(2)}, u32[]{:S(2)}) %all-to-all-start) | async-done | bytes 524320 | tf_op jit(solution)/shard_map/all_to_all | solution.py:400
  29.4 1.4 %directions.1 = (bf16[16,144,128]{2,1,0:T(8,128)(2,1)}, f32[256,128]{1,0:T(8,128)S(1)}, f32[16,128]{1,0:T(8,128)S(1)}) custom-call(s32[1024,128]{1,0:T(8,128)S(1)} %bitcast.6, bf16[144,256]{1,0:T(8,128)(2,1)S(1)} %get-tuple-element.33.slot_map, bf16[256,256]{1,0:T(8,128)(2,1)S(1)} %get-tuple-element.34.block_map, bf16[16,256]{1,0:T(8,128)(2,1)S(1)} %get-tuple-element.35.own_map), custom_call_target="tpu_custom_call" | custom-call | flops 200000000 | bytes 2000000 | tf_op jit(solution)/shard_map/directions/pallas_call | solution.py:300
  30.8 3.6 %all-to-all-start.1 = ((bf16[16,144,128]{2,1,0:T(8,128)(2,1)}), bf16[16,144,128]{2,1,0:T(8,128)(2,1)S(1)}, u32[]{:S(2)}, u32[]{:S(2)}) async-start(bf16[16,144,128]{2,1,0:T(8,128)(2,1)} %get-tuple-element.38), calls=%async_computation.1 | async-start | bytes 1179648 | tf_op jit(solution)/shard_map/all_to_all | solution.py:407
  34.4 0.0 copy-start
  34.4 0.0 copy-start.1
  34.4 0.0 copy-start.2
  34.4 6.4 %error_feedback.3 = f32[144,128,128]{2,1,0:T(8,128)} custom-call(s32[1,7]{1,0:T(1,128)} %refs_0_.3, bf16[144,128,128]{2,1,0:T(8,128)(2,1)} %refs_1_.3, f32[144,128,128]{2,1,0:T(8,128)} %refs_2_.3, f32[144,128,128]{2,1,0:T(8,128)} %error_feedback.2.refs_3_), custom_call_target="tpu_custom_call", output_to_operand_aliasing={{}: (3, {})} | custom-call | flops 2500000 | bytes 11800000 | tf_op jit(solution)/shard_map/error_feedback/pallas_call | solution.py:181
  40.8 4.6 %all-to-all-done.1 = bf16[16,144,128]{2,1,0:T(8,128)(2,1)S(1)} async-done(((bf16[16,144,128]{2,1,0:T(8,128)(2,1)}), bf16[16,144,128]{2,1,0:T(8,128)(2,1)S(1)}, u32[]{:S(2)}, u32[]{:S(2)}) %all-to-all-start.1) | async-done | bytes 589856 | tf_op jit(solution)/shard_map/all_to_all | solution.py:407
  45.5 0.1 turn.1.refs_0_
  45.6 2.2 %collective-permute-start.2 = (bf16[144,16,128]{2,1,0:T(8,128)(2,1)S(1)}, bf16[144,16,128]{2,1,0:T(8,128)(2,1)S(1)}, u32[]{:S(2)}, u32[]{:S(2)}) collective-permute-start(bf16[144,16,128]{2,1,0:T(8,128)(2,1)S(1)} %turn.1.refs_0_), channel_id=1, source_target_pairs={{0,1},{1,0},{2,3},{3,2},{4,5},{5,4},{6,7},{7,6},{8,9},{9,8},{10,11... | collective-permute-start | bytes 1769480 | tf_op jit(solution)/shard_map/ppermute | solution.py:414
  47.8 1.4 %collective-permute-start.1 = (bf16[144,16,128]{2,1,0:T(8,128)(2,1)S(1)}, bf16[144,16,128]{2,1,0:T(8,128)(2,1)S(1)}, u32[]{:S(2)}, u32[]{:S(2)}) collective-permute-start(bf16[144,16,128]{2,1,0:T(8,128)(2,1)S(1)} %turn.1.refs_0_), channel_id=1, source_target_pairs={{0,6},{2,0},{4,2},{6,4},{1,7},{3,1},{5,3},{7,5},{8,14},{10,8},{12,... | collective-permute-start | bytes 1769480 | tf_op jit(solution)/shard_map/ppermute | solution.py:418
  49.1 0.1 collective-permute-start
  49.2 17.8 %all_to_all.33 = f32[128,2,128]{2,1,0:T(2,128)S(1)} all-to-all(f32[128,2,128]{2,1,0:T(2,128)S(1)} %bitcast.8), channel_id=1, replica_groups=mesh['row'=16,'z'=4,'core'=2] {'row','z','core'}, dimensions={0} | all-to-all | bytes 262144 | tf_op jit(solution)/shard_map/all_to_all | solution.py:420
  67.1 0.0 collective-permute-done.2.refs_1_
  67.1 0.0 collective-permute-done.1.refs_4_
  67.1 0.0 collective-permute-done.refs_2_
  67.1 0.5 collective-permute-start.5
  67.6 0.1 collective-permute-start.6
  67.8 0.1 collective-permute-start.4
  67.8 1.5 %collective-permute-start.3 = (bf16[72,16,128]{2,1,0:T(8,128)(2,1)S(1)}, bf16[72,16,128]{2,1,0:T(8,128)(2,1)S(1)}, u32[]{:S(2)}, u32[]{:S(2)}) collective-permute-start(bf16[72,16,128]{2,1,0:T(8,128)(2,1)S(1)} %slice.6), channel_id=1, source_target_pairs={{0,2},{2,4},{4,6},{6,0},{1,3},{3,5},{5,7},{7,1},{8,10},{10,12},{12... | collective-permute-start | bytes 884744 | tf_op jit(solution)/shard_map/ppermute | solution.py:422
  69.3 0.0 copy-done
  69.3 0.0 copy-done.1
  69.3 0.0 copy-done.2
  69.3 0.9 %update.1 = (f32[2,128,128]{2,1,0:T(8,128)}, f32[2,128,128]{2,1,0:T(8,128)}, f32[2,128,128]{2,1,0:T(8,128)}) custom-call(f32[256,128]{1,0:T(8,128)S(1)} %bitcast.7, f32[16,128]{1,0:T(8,128)S(1)} %get-tuple-element.49.flags, f32[2,128,128]{2,1,0:T(8,128)S(1)} %copy-done, f32[2,128,128]{2,1,0:T(8,128)S(1)} %copy-done.1, f32[2,128,128]{2,1,0:T(8,128)S(1)} %copy-done.2), custom_call_target="tpu_custom_call" | custom-call | flops 600000 | bytes 900000 | tf_op jit(solution)/shard_map/update/pallas_call | solution.py:382
  70.2 0.0 collective-permute-done.5.refs_3_
  70.2 0.0 collective-permute-done.6.refs_5_
  70.2 1.8 %place.2.refs_4_ = bf16[144,128,128]{2,1,0:T(8,128)(2,1)} custom-call(bf16[144,16,128]{2,1,0:T(8,128)(2,1)S(1)} %turn.1.refs_0_, bf16[144,16,128]{2,1,0:T(8,128)(2,1)S(1)} %collective-permute-done.2.refs_1_, bf16[144,16,128]{2,1,0:T(8,128)(2,1)S(1)} %collective-permute-done.refs_2_, bf16[144,16,128]{2,1,0:T(8,128)(2,1)S(1)} %collective-permute-done.5.refs_3_, ...), custom_call_target="tpu_custom_call" | custom-call | bytes 2400000 | tf_op jit(solution)/shard_map/place/pallas_call | solution.py:355
  72.0 4.0 %collective-permute-done.4.refs_2_ = bf16[72,16,128]{2,1,0:T(8,128)(2,1)S(1)} collective-permute-done((bf16[72,16,128]{2,1,0:T(8,128)(2,1)S(1)}, bf16[72,16,128]{2,1,0:T(8,128)(2,1)S(1)}, u32[]{:S(2)}, u32[]{:S(2)}) %collective-permute-start.4) | collective-permute-done | bytes 294944 | tf_op jit(solution)/shard_map/ppermute | solution.py:423
  76.0 1.1 %collective-permute-done.3.refs_0_ = bf16[72,16,128]{2,1,0:T(8,128)(2,1)S(1)} collective-permute-done((bf16[72,16,128]{2,1,0:T(8,128)(2,1)S(1)}, bf16[72,16,128]{2,1,0:T(8,128)(2,1)S(1)}, u32[]{:S(2)}, u32[]{:S(2)}) %collective-permute-start.3) | collective-permute-done | bytes 294944 | tf_op jit(solution)/shard_map/ppermute | solution.py:422
  77.1 1.5 %collective-permute-start.7 = (bf16[72,16,128]{2,1,0:T(8,128)(2,1)S(1)}, bf16[72,16,128]{2,1,0:T(8,128)(2,1)S(1)}, u32[]{:S(2)}, u32[]{:S(2)}) collective-permute-start(bf16[72,16,128]{2,1,0:T(8,128)(2,1)S(1)} %collective-permute-done.3.refs_0_), channel_id=1, source_target_pairs={{0,1},{1,0},{2,3},{3,2},{4,5},{5,4},{6,7},{7,6},{8,9},{9,8},{10,11... | collective-permute-start | bytes 884744 | tf_op jit(solution)/shard_map/ppermute | solution.py:414
  78.6 0.0 collective-permute-start.8
  78.6 1.2 %collective-permute-done.7.refs_1_ = bf16[72,16,128]{2,1,0:T(8,128)(2,1)S(1)} collective-permute-done((bf16[72,16,128]{2,1,0:T(8,128)(2,1)S(1)}, bf16[72,16,128]{2,1,0:T(8,128)(2,1)S(1)}, u32[]{:S(2)}, u32[]{:S(2)}) %collective-permute-start.7) | collective-permute-done | bytes 294944 | tf_op jit(solution)/shard_map/ppermute | solution.py:414
  79.8 0.4 collective-permute-done.8.refs_3_
  80.2 1.0 %place.3 = bf16[144,128,128]{2,1,0:T(8,128)(2,1)} custom-call(bf16[72,16,128]{2,1,0:T(8,128)(2,1)S(1)} %collective-permute-done.3.refs_0_, bf16[72,16,128]{2,1,0:T(8,128)(2,1)S(1)} %collective-permute-done.7.refs_1_, bf16[72,16,128]{2,1,0:T(8,128)(2,1)S(1)} %collective-permute-done.4.refs_2_, ...), custom_call_target="tpu_custom_call", output_to_operand_aliasing={{}: (4, {})} | custom-call | bytes 2400000 | tf_op jit(solution)/shard_map/place/pallas_call | solution.py:355
  (2 shorter events, 0.0 us)
Async XLA Ops:
  4.3 25.1 %all-to-all-start = ((s32[128,8,128]{2,1,0:T(8,128)}), s32[128,8,128]{2,1,0:T(8,128)S(1)}, u32[]{:S(2)}, u32[]{:S(2)}) async-start(s32[128,8,128]{2,1,0:T(8,128)} %bitcast.9), calls=%async_computation | async-start | bytes 1048576 | tf_op jit(solution)/shard_map/all_to_all | solution.py:400
  15.8 0.7 copy-start.3
  16.4 0.7 copy-start.4
  30.8 14.7 %all-to-all-start.1 = ((bf16[16,144,128]{2,1,0:T(8,128)(2,1)}), bf16[16,144,128]{2,1,0:T(8,128)(2,1)S(1)}, u32[]{:S(2)}, u32[]{:S(2)}) async-start(bf16[16,144,128]{2,1,0:T(8,128)(2,1)} %get-tuple-element.38), calls=%async_computation.1 | async-start | bytes 1179648 | tf_op jit(solution)/shard_map/all_to_all | solution.py:407
  34.4 34.9 %copy-start = (f32[2,128,128]{2,1,0:T(8,128)S(1)}, f32[2,128,128]{2,1,0:T(8,128)}, u32[]{:S(2)}) copy-start(f32[2,128,128]{2,1,0:T(8,128)} %master.3) | copy-start | bytes 393220
  34.4 34.9 %copy-start.1 = (f32[2,128,128]{2,1,0:T(8,128)S(1)}, f32[2,128,128]{2,1,0:T(8,128)}, u32[]{:S(2)}) copy-start(f32[2,128,128]{2,1,0:T(8,128)} %moment1.3) | copy-start | bytes 393220
  34.4 34.9 %copy-start.2 = (f32[2,128,128]{2,1,0:T(8,128)S(1)}, f32[2,128,128]{2,1,0:T(8,128)}, u32[]{:S(2)}) copy-start(f32[2,128,128]{2,1,0:T(8,128)} %moment2.3) | copy-start | bytes 393220
  45.6 21.5 %collective-permute-start.2 = (bf16[144,16,128]{2,1,0:T(8,128)(2,1)S(1)}, bf16[144,16,128]{2,1,0:T(8,128)(2,1)S(1)}, u32[]{:S(2)}, u32[]{:S(2)}) collective-permute-start(bf16[144,16,128]{2,1,0:T(8,128)(2,1)S(1)} %turn.1.refs_0_), channel_id=1, source_target_pairs={{0,1},{1,0},{2,3},{3,2},{4,5},{5,4},{6,7},{7,6},{8,9},{9,8},{10,11... | collective-permute-start | bytes 1769480 | tf_op jit(solution)/shard_map/ppermute | solution.py:414
  47.8 19.3 %collective-permute-start.1 = (bf16[144,16,128]{2,1,0:T(8,128)(2,1)S(1)}, bf16[144,16,128]{2,1,0:T(8,128)(2,1)S(1)}, u32[]{:S(2)}, u32[]{:S(2)}) collective-permute-start(bf16[144,16,128]{2,1,0:T(8,128)(2,1)S(1)} %turn.1.refs_0_), channel_id=1, source_target_pairs={{0,6},{2,0},{4,2},{6,4},{1,7},{3,1},{5,3},{7,5},{8,14},{10,8},{12,... | collective-permute-start | bytes 1769480 | tf_op jit(solution)/shard_map/ppermute | solution.py:418
  49.1 18.0 %collective-permute-start = (bf16[144,16,128]{2,1,0:T(8,128)(2,1)S(1)}, bf16[144,16,128]{2,1,0:T(8,128)(2,1)S(1)}, u32[]{:S(2)}, u32[]{:S(2)}) collective-permute-start(bf16[144,16,128]{2,1,0:T(8,128)(2,1)S(1)} %turn.1.refs_0_), channel_id=1, source_target_pairs={{0,2},{2,4},{4,6},{6,0},{1,3},{3,5},{5,7},{7,1},{8,10},{10,12},{12... | collective-permute-start | bytes 1769480 | tf_op jit(solution)/shard_map/ppermute | solution.py:417
  67.1 3.1 %collective-permute-start.5 = (bf16[144,16,128]{2,1,0:T(8,128)(2,1)S(1)}, bf16[144,16,128]{2,1,0:T(8,128)(2,1)S(1)}, u32[]{:S(2)}, u32[]{:S(2)}) collective-permute-start(bf16[144,16,128]{2,1,0:T(8,128)(2,1)S(1)} %collective-permute-done.refs_2_), channel_id=1, source_target_pairs={{0,1},{1,0},{2,3},{3,2},{4,5},{5,4},{6,7},{7,6},{8,9},{9,8},{10,11... | collective-permute-start | bytes 1769480 | tf_op jit(solution)/shard_map/ppermute | solution.py:414
  67.6 2.6 %collective-permute-start.6 = (bf16[144,16,128]{2,1,0:T(8,128)(2,1)S(1)}, bf16[144,16,128]{2,1,0:T(8,128)(2,1)S(1)}, u32[]{:S(2)}, u32[]{:S(2)}) collective-permute-start(bf16[144,16,128]{2,1,0:T(8,128)(2,1)S(1)} %collective-permute-done.1.refs_4_), channel_id=1, source_target_pairs={{0,1},{1,0},{2,3},{3,2},{4,5},{5,4},{6,7},{7,6},{8,9},{9,8},{10,11... | collective-permute-start | bytes 1769480 | tf_op jit(solution)/shard_map/ppermute | solution.py:414
  67.8 8.2 %collective-permute-start.4 = (bf16[72,16,128]{2,1,0:T(8,128)(2,1)S(1)}, bf16[72,16,128]{2,1,0:T(8,128)(2,1)S(1)}, u32[]{:S(2)}, u32[]{:S(2)}) collective-permute-start(bf16[72,16,128]{2,1,0:T(8,128)(2,1)S(1)} %slice.7), channel_id=1, source_target_pairs={{0,6},{2,0},{4,2},{6,4},{1,7},{3,1},{5,3},{7,5},{8,14},{10,8},{12,... | collective-permute-start | bytes 884744 | tf_op jit(solution)/shard_map/ppermute | solution.py:423
  67.8 9.2 %collective-permute-start.3 = (bf16[72,16,128]{2,1,0:T(8,128)(2,1)S(1)}, bf16[72,16,128]{2,1,0:T(8,128)(2,1)S(1)}, u32[]{:S(2)}, u32[]{:S(2)}) collective-permute-start(bf16[72,16,128]{2,1,0:T(8,128)(2,1)S(1)} %slice.6), channel_id=1, source_target_pairs={{0,2},{2,4},{4,6},{6,0},{1,3},{3,5},{5,7},{7,1},{8,10},{10,12},{12... | collective-permute-start | bytes 884744 | tf_op jit(solution)/shard_map/ppermute | solution.py:422
  77.1 2.7 %collective-permute-start.7 = (bf16[72,16,128]{2,1,0:T(8,128)(2,1)S(1)}, bf16[72,16,128]{2,1,0:T(8,128)(2,1)S(1)}, u32[]{:S(2)}, u32[]{:S(2)}) collective-permute-start(bf16[72,16,128]{2,1,0:T(8,128)(2,1)S(1)} %collective-permute-done.3.refs_0_), channel_id=1, source_target_pairs={{0,1},{1,0},{2,3},{3,2},{4,5},{5,4},{6,7},{7,6},{8,9},{9,8},{10,11... | collective-permute-start | bytes 884744 | tf_op jit(solution)/shard_map/ppermute | solution.py:414
  78.6 1.6 %collective-permute-start.8 = (bf16[72,16,128]{2,1,0:T(8,128)(2,1)S(1)}, bf16[72,16,128]{2,1,0:T(8,128)(2,1)S(1)}, u32[]{:S(2)}, u32[]{:S(2)}) collective-permute-start(bf16[72,16,128]{2,1,0:T(8,128)(2,1)S(1)} %collective-permute-done.4.refs_2_), channel_id=1, source_target_pairs={{0,1},{1,0},{2,3},{3,2},{4,5},{5,4},{6,7},{7,6},{8,9},{9,8},{10,11... | collective-permute-start | bytes 884744 | tf_op jit(solution)/shard_map/ppermute | solution.py:414

commit v3 on v2

--- a/solution.py
+++ b/solution.py
@@ -16,11 +16,14 @@
 N_COL = 8
 DEVICES = N_ROW * N_COL
 PLANE = N_ROW
+CHIPS = 4 * PLANE
+HALF = BS // 2
 
 MSG = 8
 STATE_ROW = 4
 INFO_ROW = 7
 SCALE_LANE = 8
+EXT = 8
 UNIT = 2.0**26
 STEPS = 32767.0
 ROOT_STEPS = 65535.0
@@ -44,7 +47,6 @@
 MIB = 1024 * 1024
 PARAMS = pltpu.CompilerParams(vmem_limit_bytes=16 * MIB)
 ALONE = pltpu.CompilerParams(vmem_limit_bytes=64 * MIB)
-NEARLY_ALONE = pltpu.CompilerParams(vmem_limit_bytes=61 * MIB)
 
 
 def adamw(totals, master, moment1, moment2):
@@ -64,7 +66,7 @@
 
 
 def first_row(z, core):
-    return core * (BS // 2) + z * PLANE
+    return core * HALF + z * PLANE
 
 
 def pack_kernel(sel_hbm, grad, error, master, moment1, moment2, send, sel, grads, errors, states, sel_sem, sems):
@@ -159,35 +161,30 @@
 FEED = 18
 
 
-def feedback(sel, grad, error, part, before):
-    steps = BLOCKS // FEED // 2
-
-    def kernel(*refs):
-        sel, grad, error, out = *refs[:3], refs[-1]
-
-        def step(grad_blocks, error_blocks, out_blocks):
-            first = (part * steps + pl.program_id(0)) * FEED
-            for b in range(FEED):
-                hit = sel[0, 0] == first + b
-                for k in range(1, SEL):
-                    hit = jnp.logical_or(hit, sel[0, k] == first + b)
-                keep = 1.0 - hit.astype(F32)
-                out_blocks[b] = (grad_blocks[b].astype(F32) + error_blocks[b]) * keep
-
-        block = pl.BlockSpec((FEED, BS, BS), lambda i: (part * steps + i, 0, 0))
-        pltpu.emit_pipeline(step, grid=(steps,), in_specs=[block, block], out_specs=[block])(grad, error, out)
-
-    more = [] if before is None else [before]
-    return pl.pallas_call(
-        kernel,
-        in_specs=[SMEM] + [HBM] * 2 + [HBM] * len(more),
+def feedback_kernel(sel, grad, error, out):
+    def step(grad_blocks, error_blocks, out_blocks):
+        first = pl.program_id(0) * FEED
+        for b in range(FEED):
+            hit = sel[0, 0] == first + b
+            for k in range(1, SEL):
+                hit = jnp.logical_or(hit, sel[0, k] == first + b)
+            keep = 1.0 - hit.astype(F32)
+            out_blocks[b] = (grad_blocks[b].astype(F32) + error_blocks[b]) * keep
+
+    block = pl.BlockSpec((FEED, BS, BS), lambda i: (i, 0, 0))
+    pltpu.emit_pipeline(step, grid=(BLOCKS // FEED,), in_specs=[block, block], out_specs=[block])(grad, error, out)
+
+
+def feedback(sel, grad, error):
+    return pl.pallas_call(
+        feedback_kernel,
+        in_specs=[SMEM] + [HBM] * 2,
         out_specs=HBM,
         out_shape=jax.ShapeDtypeStruct((BLOCKS, BS, BS), F32),
-        input_output_aliases={3: 0} if more else {},
-        compiler_params=NEARLY_ALONE,
-        cost_estimate=pl.CostEstimate(flops=2_500_000, bytes_accessed=11_800_000, transcendentals=0),
+        compiler_params=PARAMS,
+        cost_estimate=pl.CostEstimate(flops=5_000_000, bytes_accessed=23_600_000, transcendentals=0),
         name="error_feedback",
-    )(sel, grad, error, *more)
+    )(sel, grad, error)
 
 
 def maps_kernel(rows_ref, cols_ref, slot_map, block_map, own_map):
@@ -201,11 +198,12 @@
     slot = (grid_row - row_start) + (grid_col - col_start)
     for s in range(OWNCAP):
         slot_map[:, s * BS : (s + 1) * BS] = jnp.where((owner == lane) & (slot == s), 1.0, 0.0).astype(BF16)
-    holder = lax.broadcasted_iota(I32, (DEVICES * OWNCAP, BS), 0)
+    holder = lax.broadcasted_iota(I32, (EXT * CHIPS, BS), 0)
+    chip = holder // EXT
     slot = holder % OWNCAP
-    holder = holder // OWNCAP
-    band_row = holder // N_COL
-    band_col = holder - band_row * N_COL
+    core = lax.axis_index("core")
+    band_row = chip // 4
+    band_col = chip % 4 * 2 + jnp.where(holder % 4 < OWNCAP, core, 1 - core)
     top = jnp.zeros_like(holder)
     end = jnp.zeros_like(holder)
     for k in range(N_ROW):
@@ -218,7 +216,7 @@
         right = jnp.where(band_col == k, cols_ref[k + 1], right)
     at_row = top + slot
     target = jnp.where((at_row < end) & (left < right), at_row * GC + left, -1)
-    lane = lax.broadcasted_iota(I32, (DEVICES * OWNCAP, BS), 1)
+    lane = lax.broadcasted_iota(I32, (EXT * CHIPS, BS), 1)
     for part in range(2):
         block_map[:, part * BS : (part + 1) * BS] = jnp.where(target == lane + part * BS, 1.0, 0.0).astype(BF16)
     band_row = lax.axis_index("row")
@@ -238,7 +236,7 @@
         out_specs=[VMEM] * 3,
         out_shape=[
             jax.ShapeDtypeStruct((BLOCKS, OWNCAP * BS), BF16),
-            jax.ShapeDtypeStruct((OWNCAP * DEVICES, 2 * BS), BF16),
+            jax.ShapeDtypeStruct((EXT * CHIPS, 2 * BS), BF16),
             jax.ShapeDtypeStruct((16, 2 * BS), BF16),
         ],
         compiler_params=PARAMS,
@@ -247,7 +245,7 @@
     )(row_bounds, col_bounds)
 
 
-def directions_kernel(got, slot_map, block_map, own_map, message, owned, flags):
+def directions_kernel(got, slot_map, block_map, own_map, message, flags):
     def rows(k):
         return got[pl.ds(k, DEVICES, stride=MSG), :]
 
@@ -285,12 +283,14 @@
 
     direction = adamw(totals, master, moment1, root2 * root2)[2]
     direction = jnp.where(tallies > 0.5, direction, 0.0).astype(BF16)
-    for i in range(PLANE):
-        message[i] = direction
-
     padded = jnp.concatenate([totals, jnp.zeros((2 * BS - BLOCKS, BS), F32)], axis=0)
     sums = jnp.dot(block_map[...], jnp.concatenate(three_terms(padded), axis=1), preferred_element_type=F32)
-    owned[...] = (sums[:, :BS] + sums[:, BS : 2 * BS]) + sums[:, 2 * BS :]
+    high, low, _ = three_terms((sums[:, :BS] + sums[:, BS : 2 * BS]) + sums[:, 2 * BS :])
+    term = lax.broadcasted_iota(I32, (EXT * CHIPS, BS), 0) % EXT < EXT // 2
+    both = jnp.where(term, high.astype(F32), low.astype(F32)).astype(BF16).reshape(CHIPS, EXT, BS)
+    for i in range(CHIPS):
+        message[i, :BLOCKS] = direction
+        message[i, BLOCKS:] = both[i]
 
     padded = jnp.concatenate([tallies, jnp.zeros((2 * BS - BLOCKS, BS), F32)], axis=0).astype(BF16)
     flags[...] = jnp.dot(own_map[...], padded, preferred_element_type=F32)
@@ -300,10 +300,9 @@
     return pl.pallas_call(
         directions_kernel,
         in_specs=[VMEM] * 4,
-        out_specs=[VMEM] * 3,
+        out_specs=[VMEM] * 2,
         out_shape=[
-            jax.ShapeDtypeStruct((PLANE, BLOCKS, BS), BF16),
-            jax.ShapeDtypeStruct((OWNCAP * DEVICES, BS), F32),
+            jax.ShapeDtypeStruct((CHIPS, BLOCKS + EXT, BS), BF16),
             jax.ShapeDtypeStruct((16, BS), F32),
         ],
         compiler_params=PARAMS,
@@ -315,116 +314,142 @@
 PITCH = BLOCKS + 1
 
 
-def turn_kernel(rows, out, scratch):
-    for chip in range(PLANE):
-        scratch[pl.ds(chip * PITCH, BLOCKS), :] = rows[chip].astype(F32)
-    for b in range(BLOCKS):
-        out[b] = scratch[pl.ds(b, PLANE, stride=PITCH), :].astype(BF16)
+EXT_PITCH = EXT + 1
+
+
+def turn_kernel(rows, first, last, own, other, scratch, ext):
+    for z in range(4):
+        for y in range(PLANE):
+            chip = 4 * y + z
+            scratch[pl.ds(y * PITCH, BLOCKS), :] = rows[chip, :BLOCKS].astype(F32)
+            ext[pl.ds((z * PLANE + y) * EXT_PITCH, EXT), :] = rows[chip, BLOCKS:].astype(F32)
+        for b in range(BLOCKS):
+            (first, last)[z // 2][z % 2, b] = scratch[pl.ds(b, PLANE, stride=PITCH), :].astype(BF16)
+    for t in range(2 * OWNCAP):
+        high, low = [ext[pl.ds(t + 4 * n, CHIPS, stride=EXT_PITCH), :] for n in range(2)]
+        (own, other)[t // OWNCAP][t % OWNCAP] = high + low
 
 
 def turn(rows):
+    planes = jax.ShapeDtypeStruct((2, BLOCKS, PLANE, BS), BF16)
+    owned = jax.ShapeDtypeStruct((OWNCAP, HALF, BS), F32)
     return pl.pallas_call(
         turn_kernel,
         in_specs=[VMEM],
-        out_specs=VMEM,
-        out_shape=jax.ShapeDtypeStruct((BLOCKS, PLANE, BS), BF16),
-        scratch_shapes=[pltpu.VMEM((PLANE * PITCH, BS), F32)],
-        compiler_params=PARAMS,
-        cost_estimate=pl.CostEstimate(flops=600_000, bytes_accessed=1_200_000, transcendentals=0),
+        out_specs=[VMEM] * 4,
+        out_shape=[planes, planes, owned, owned],
+        scratch_shapes=[pltpu.VMEM((PLANE * PITCH, BS), F32), pltpu.VMEM((CHIPS * EXT_PITCH, BS), F32)],
+        compiler_params=PARAMS,
+        cost_estimate=pl.CostEstimate(flops=2_400_000, bytes_accessed=5_000_000, transcendentals=0),
         name="turn",
     )(rows)
 
 
-def place(steps, pieces):
-    arrays = [a for piece in pieces for a in piece[2:]]
-
-    def kernel(*refs):
-        inputs, out, sems = refs[: len(arrays)], refs[-2], refs[-1]
-        z, core = lax.axis_index("z"), lax.axis_index("core")
-        copies = []
-        for n, ref in enumerate(inputs):
-            first, away = pieces[n // 2][:2]
-            at = first_row(lax.rem(z + away, N_COL // 2), core if n % 2 == 0 else 1 - core)
-            target = out.at[pl.ds(first, ref.shape[0]), pl.ds(pl.multiple_of(at, PLANE), PLANE)]
-            copies.append(pltpu.make_async_copy(ref, target, sems.at[n]))
-        for copy in copies:
-            copy.start()
-        for copy in copies:
+def place(pieces, steps, sems, half):
+    copies = []
+    for first, planes in pieces:
+        for z in range(first, first + 2):
+            rows = pl.ds(pl.multiple_of(first_row(z, half), PLANE), PLANE)
+            copies.append(pltpu.make_async_copy(planes.at[z - first], steps.at[:, rows], sems.at[z]))
+            copies[-1].start()
+    return copies
+
+
+def place_own(first, last):
+    def kernel(first, last, steps, sems):
+        for copy in place([(0, first), (2, last)], steps, sems, lax.axis_index("core")):
             copy.wait()
 
     return pl.pallas_call(
         kernel,
-        in_specs=[VMEM] * len(arrays) + ([] if steps is None else [HBM]),
+        in_specs=[VMEM] * 2,
         out_specs=HBM,
         out_shape=jax.ShapeDtypeStruct((BLOCKS, BS, BS), BF16),
-        scratch_shapes=[pltpu.SemaphoreType.DMA((len(arrays),))],
-        input_output_aliases={} if steps is None else {len(arrays): 0},
+        scratch_shapes=[pltpu.SemaphoreType.DMA((4,))],
+        compiler_params=PARAMS,
+        cost_estimate=pl.CostEstimate(flops=0, bytes_accessed=4_800_000, transcendentals=0),
+        name="place_own",
+    )(first, last)
+
+
+def place_first(planes, steps):
+    def kernel(planes, before, steps, sems):
+        for copy in place([(0, planes)], steps, sems, 1 - lax.axis_index("core")):
+            copy.wait()
+
+    return pl.pallas_call(
+        kernel,
+        in_specs=[VMEM, HBM],
+        out_specs=HBM,
+        out_shape=jax.ShapeDtypeStruct((BLOCKS, BS, BS), BF16),
+        scratch_shapes=[pltpu.SemaphoreType.DMA((4,))],
+        input_output_aliases={1: 0},
         compiler_params=PARAMS,
         cost_estimate=pl.CostEstimate(flops=0, bytes_accessed=2_400_000, transcendentals=0),
-        name="place",
-    )(*arrays, *([] if steps is None else [steps]))
-
-
-def update_kernel(owned, flags, master, moment1, moment2, master_out, moment1_out, moment2_out, totals):
+        name="place_first",
+    )(planes, steps)
+
+
+def finish_kernel(
+    planes, before, own, other, flags, master, moment1, moment2, steps, master_out, moment1_out, moment2_out,
+    totals, new, sems, new_sems,
+):
+    core = lax.axis_index("core")
+    copies = place([(2, planes)], steps, sems, 1 - core)
+    totals[:, pl.ds(pl.multiple_of(core * HALF, HALF), HALF), :] = own[...]
+    totals[:, pl.ds(pl.multiple_of((1 - core) * HALF, HALF), HALF), :] = other[...]
     for s in range(OWNCAP):
-        for col in range(N_COL):
-            at = first_row(col // 2, col % 2)
-            totals[s, at : at + PLANE] = owned[pl.ds(col * OWNCAP + s, PLANE, stride=N_COL * OWNCAP), :]
         changed = flags[s : s + 1] > 0.5
         new1, new2, direction = adamw(totals[s], master[s], moment1[s], moment2[s])
-        master_out[s] = jnp.where(changed, master[s] - LEARN_RATE * direction, master[s])
-        moment1_out[s] = jnp.where(changed, new1, moment1[s])
-        moment2_out[s] = jnp.where(changed, new2, moment2[s])
-
-
-def update(owned, flags, master, moment1, moment2):
+        new[0, s] = jnp.where(changed, master[s] - LEARN_RATE * direction, master[s])
+        new[1, s] = jnp.where(changed, new1, moment1[s])
+        new[2, s] = jnp.where(changed, new2, moment2[s])
+        for n, array in enumerate((master_out, moment1_out, moment2_out)):
+            copies.append(pltpu.make_async_copy(new.at[n, s], array.at[s], new_sems.at[n, s]))
+            copies[-1].start()
+    for copy in copies:
+        copy.wait()
+
+
+def finish(planes, steps, own, other, flags, master, moment1, moment2):
     slots = jax.ShapeDtypeStruct((OWNCAP, BS, BS), F32)
     return pl.pallas_call(
-        update_kernel,
-        in_specs=[VMEM] * 5,
-        out_specs=[VMEM] * 3,
-        out_shape=[slots] * 3,
-        scratch_shapes=[pltpu.VMEM((OWNCAP, BS, BS), F32)],
-        compiler_params=PARAMS,
-        cost_estimate=pl.CostEstimate(flops=600_000, bytes_accessed=900_000, transcendentals=33_000),
-        name="update",
-    )(owned, flags, master, moment1, moment2)
-
-
-RIGHT = [(i, (i + 1) % 4) for i in range(4)]
-LEFT = [(i, (i + 3) % 4) for i in range(4)]
+        finish_kernel,
+        in_specs=[VMEM, HBM] + [VMEM] * 6,
+        out_specs=[HBM] * 4,
+        out_shape=[jax.ShapeDtypeStruct((BLOCKS, BS, BS), BF16), slots, slots, slots],
+        scratch_shapes=[
+            pltpu.VMEM((OWNCAP, BS, BS), F32),
+            pltpu.VMEM((3, OWNCAP, BS, BS), F32),
+            pltpu.SemaphoreType.DMA((4,)),
+            pltpu.SemaphoreType.DMA((3, OWNCAP)),
+        ],
+        input_output_aliases={1: 0},
+        compiler_params=PARAMS,
+        cost_estimate=pl.CostEstimate(flops=600_000, bytes_accessed=3_600_000, transcendentals=33_000),
+        name="finish",
+    )(planes, steps, own, other, flags, master, moment1, moment2)
+
+
+def swap(piece):
+    return lax.ppermute(piece, "core", [(0, 1), (1, 0)])
 
 
 def local(grad, error, sel_blocks, row_bounds, col_bounds, master, moment1, moment2):
     send = pack(sel_blocks, grad, error, master, moment1, moment2)
     got = lax.all_to_all(send, ("row", "z", "core"), split_axis=0, concat_axis=0, tiled=True)
     slot_map, block_map, own_map = maps(row_bounds, col_bounds)
-    error_out = feedback(sel_blocks, grad, error, 0, None)
-    got, error_out = lax.optimization_barrier((got, error_out))
-    message, owned, flags = directions(got, slot_map, block_map, own_map)
-
-    message, error_out = lax.optimization_barrier((message, error_out))
-    plane = lax.all_to_all(message.reshape(PLANE * BLOCKS, BS), "row", split_axis=0, concat_axis=0, tiled=True)
-    error_out = feedback(sel_blocks, grad, error, 1, error_out)
-    plane, error_out = lax.optimization_barrier((plane, error_out))
-    mine = turn(plane.reshape(PLANE, BLOCKS, BS))
-    mine, owned = lax.optimization_barrier((mine, owned))
-
-    def swap(piece):
-        return lax.ppermute(piece, "core", [(0, 1), (1, 0)])
-
-    half = BLOCKS // 2
-    before = lax.ppermute(mine, "z", RIGHT)
-    after = lax.ppermute(mine, "z", LEFT)
-    mine_too = swap(mine)
-    owned = lax.all_to_all(owned, ("row", "z", "core"), split_axis=0, concat_axis=0, tiled=True)
-    before, after, mine_too, owned = lax.optimization_barrier((before, after, mine_too, owned))
-    far_first = lax.ppermute(before[:half], "z", RIGHT)
-    far_last = lax.ppermute(after[half:], "z", LEFT)
-    steps = place(None, [(0, 0, mine, mine_too), (0, 3, before, swap(before)), (0, 1, after, swap(after))])
-    states = update(owned, flags, master, moment1, moment2)
-    far_first, far_last, steps, states = lax.optimization_barrier((far_first, far_last, steps, states))
-    steps = place(steps, [(0, 2, far_first, swap(far_first)), (half, 2, far_last, swap(far_last))])
+    message, flags = directions(got, slot_map, block_map, own_map)
+    rows = BLOCKS + EXT
+    chips = lax.all_to_all(message.reshape(CHIPS * rows, BS), ("row", "z"), split_axis=0, concat_axis=0, tiled=True)
+    error_out = feedback(sel_blocks, grad, error)
+    chips, error_out = lax.optimization_barrier((chips, error_out))
+    first, last, own, other = turn(chips.reshape(CHIPS, rows, BS))
+    first_too, last_too, other = swap(first), swap(last), swap(other)
+    steps = place_own(first, last)
+    first_too, steps = lax.optimization_barrier((first_too, steps))
+    steps = place_first(first_too, steps)
+    steps, *states = finish(last_too, steps, own, other, flags, master, moment1, moment2)
     return (error_out, *states, steps)
 
 

time: 81.7 us -> 78 us (0.955)
  blocking collectives: 17.8 us -> 0 us
  waiting for transfers between devices: 16.3 us -> 30.6 us
  local copies, waits for them, and re-layouts: 1.37 us -> 8.79 us
  Pallas kernels: 22.6 us -> 17.3 us
  starting transfers between devices: 22.3 us -> 20.1 us
    all_to_all x1 -> x0, blocking collectives: 17.8 us -> none  [local(): lax.all_to_all(owned, ('row', 'z', 'core'), split_axis=0, concat_axis=0,...]
    all_to_all x1, waiting for transfers between devices: 4.64 us -> 18.4 us  [local(): lax.all_to_all(message.reshape(CHIPS * rows, BS), ('row', 'z'), split_axi...]
    unnamed x10 -> x18, local copies, waits for them, and re-layouts: 1.32 us -> 8.79 us
    all_to_all x1, waiting for transfers between devices: 4.99 us -> 11 us  [local(): lax.all_to_all(send, ('row', 'z', 'core'), split_axis=0, concat_axis=0, t...]
    ppermute x4 -> x0, waiting for transfers between devices: 5.03 us -> none  [the longest x1 3.96 us: local(): far_last = lax.ppermute(after[half:], 'z', LEFT)]
    pallas_call x6 -> x5, Pallas kernels: 16.6 us -> 11.5 us  [the longest x1 7.25 us: feedback(): pl.pallas_call(feedback_kernel, in_specs=[SMEM] + [HBM] * 2, out_specs=HB...]
    ppermute x4 -> x0, starting transfers between devices: 3.01 us -> none  [the longest x1 1.45 us: local(): far_first = lax.ppermute(before[:half], 'z', RIGHT)]
    all_to_all x1, starting transfers between devices: 3.58 us -> 5.06 us  [local(): lax.all_to_all(message.reshape(CHIPS * rows, BS), ('row', 'z'), split_axi...]
  transfers between devices with their start and end apart: 11 -> 5, of which waited for: 6 -> 4; matrix products, arithmetic and copies ran while one was open for 0% -> 0% of each run, Pallas kernels for 20% -> 14%
where the time goes in v3:
time: 78 us; the launch traced here: 77.6 us
  waiting for transfers between devices  30.6 us (39%)
  starting transfers between devices  20.1 us (26%)
  Pallas kernels  17.3 us (22%)
  local copies, waits for them, and re-layouts  8.79 us (11%)
    all_to_all x1, waiting for transfers between devices, local(): lax.all_to_all(message.reshape(CHIPS * rows, BS), ('row', 'z'), split_axi...  18.4 us
    all_to_all x1, starting transfers between devices, local(): lax.all_to_all(send, ('row', 'z', 'core'), split_axis=0, concat_axis=0, t...  11.5 us
    all_to_all x1, waiting for transfers between devices, local(): lax.all_to_all(send, ('row', 'z', 'core'), split_axis=0, concat_axis=0, t...  11 us
    unnamed x18, local copies, waits for them, and re-layouts  8.79 us
    pallas_call x1, Pallas kernels, feedback(): pl.pallas_call(feedback_kernel, in_specs=[SMEM] + [HBM] * 2, out_specs=HB...  7.25 us
    all_to_all x1, starting transfers between devices, local(): lax.all_to_all(message.reshape(CHIPS * rows, BS), ('row', 'z'), split_axi...  5.06 us
    pallas_call x1, Pallas kernels, pack(): pl.pallas_call(pack_kernel, in_specs=[HBM] * 6, out_specs=VMEM, out_shape...  3.63 us
    ppermute x3, starting transfers between devices, swap(): return lax.ppermute(piece, 'core', [(0, 1), (1, 0)])  3.55 us
  transfers between devices with their start and end apart: 5, of which 4 were waited for; matrix products, arithmetic and copies ran while one was open for 0% of the time, Pallas kernels for 14%

profile of v3, /device:TPU:1, one launch (start us, length us, event | category | flops | bytes accessed | tf_op | source)
XLA Modules:
  0.0 77.6 jit_solution(7805750101795452925)
XLA Ops:
  0.6 3.6 %pack_rows.1 = s32[1024,128]{1,0:T(8,128)} custom-call(s32[1,7]{1,0:T(1,128)} %sel.1, bf16[144,128,128]{2,1,0:T(8,128)(2,1)} %grad.3, f32[144,128,128]{2,1,0:T(8,128)} %error.3, f32[2,128,128]{2,1,0:T(8,128)} %master.3, f32[2,128,128]{2,1,0:T(8,128)} %moment1.3, f32[2,128,128]{2,1,0:T(8,128)} %moment2.3), custom_call_target="tpu_custom_call" | custom-call | flops 200000 | bytes 2200000 | tf_op jit(solution)/shard_map/pack_rows/pallas_call | solution.py:132
  4.3 0.0 copy-start.6
  4.3 11.5 %all-to-all-start = ((s32[128,8,128]{2,1,0:T(8,128)}), s32[128,8,128]{2,1,0:T(8,128)S(1)}, u32[]{:S(2)}, u32[]{:S(2)}) async-start(s32[128,8,128]{2,1,0:T(8,128)} %bitcast.5), calls=%async_computation | async-start | bytes 1048576 | tf_op jit(solution)/shard_map/all_to_all | solution.py:440
  15.8 0.0 copy-start.7
  15.8 0.6 copy-done.7
  16.5 0.0 copy-start.8
  16.5 0.7 copy-done.8
  17.1 1.2 %slot_maps.1 = (bf16[144,256]{1,0:T(8,128)(2,1)S(1)}, bf16[512,256]{1,0:T(8,128)(2,1)S(1)}, bf16[16,256]{1,0:T(8,128)(2,1)S(1)}) custom-call(s32[17]{0:T(128)S(1)} %copy-done.7, s32[9]{0:T(128)S(1)} %copy-done.8), custom_call_target="tpu_custom_call" | custom-call | flops 500000 | bytes 300000 | tf_op jit(solution)/shard_map/slot_maps/pallas_call | solution.py:233
  18.3 11.0 %all-to-all-done = s32[128,8,128]{2,1,0:T(8,128)S(1)} async-done(((s32[128,8,128]{2,1,0:T(8,128)}), s32[128,8,128]{2,1,0:T(8,128)S(1)}, u32[]{:S(2)}, u32[]{:S(2)}) %all-to-all-start) | async-done | bytes 524320 | tf_op jit(solution)/shard_map/all_to_all | solution.py:440
  29.4 0.9 %directions.1 = (bf16[64,152,128]{2,1,0:T(8,128)(2,1)S(1)}, f32[16,128]{1,0:T(8,128)S(1)}) custom-call(s32[1024,128]{1,0:T(8,128)S(1)} %bitcast.4, bf16[144,256]{1,0:T(8,128)(2,1)S(1)} %get-tuple-element.22.slot_map, bf16[512,256]{1,0:T(8,128)(2,1)S(1)} %get-tuple-element.23.block_map, bf16[16,256]{1,0:T(8,128)(2,1)S(1)} %get-tuple-element.24.own_map), custom_call_target="tpu_custom_call" | custom-call | flops 200000000 | bytes 2000000 | tf_op jit(solution)/shard_map/directions/pallas_call | solution.py:300
  30.2 0.0 copy-start.2
  30.2 1.4 %copy-done.2 = bf16[64,152,128]{2,1,0:T(8,128)(2,1)} copy-done((bf16[64,152,128]{2,1,0:T(8,128)(2,1)}, bf16[64,152,128]{2,1,0:T(8,128)(2,1)S(1)}, u32[]{:S(2)}) %copy-start.2) | copy-done | bytes 2490392
  31.7 5.1 %all-to-all-start.1 = ((bf16[64,152,128]{2,1,0:T(8,128)(2,1)}), bf16[64,152,128]{2,1,0:T(8,128)(2,1)S(1)}, u32[]{:S(2)}, u32[]{:S(2)}) async-start(bf16[64,152,128]{2,1,0:T(8,128)(2,1)} %copy-done.2), calls=%async_computation.1 | async-start | bytes 4980736 | tf_op jit(solution)/shard_map/all_to_all | solution.py:444
  36.8 0.0 copy-done.6
  36.8 0.0 copy-start
  36.8 3.7 %copy-done = f32[144,128,128]{2,1,0:T(8,128)S(1)} copy-done((f32[144,128,128]{2,1,0:T(8,128)S(1)}, f32[144,128,128]{2,1,0:T(8,128)}, u32[]{:S(2)}) %copy-start) | copy-done | bytes 9437208
  40.4 0.0 copy-start.1
  40.4 2.3 %copy-done.1 = bf16[144,128,128]{2,1,0:T(8,128)(2,1)S(1)} copy-done((bf16[144,128,128]{2,1,0:T(8,128)(2,1)S(1)}, bf16[144,128,128]{2,1,0:T(8,128)(2,1)}, u32[]{:S(2)}) %copy-start.1) | copy-done | bytes 4718616
  42.8 7.3 %error_feedback.1 = f32[144,128,128]{2,1,0:T(8,128)} custom-call(s32[1,7]{1,0:T(1,128)S(1)} %copy-done.6, bf16[144,128,128]{2,1,0:T(8,128)(2,1)S(1)} %copy-done.1, f32[144,128,128]{2,1,0:T(8,128)S(1)} %copy-done), custom_call_target="tpu_custom_call" | custom-call | flops 5000000 | bytes 23600000 | tf_op jit(solution)/shard_map/error_feedback/pallas_call | solution.py:179
  50.0 18.4 %all-to-all-done.1 = bf16[64,152,128]{2,1,0:T(8,128)(2,1)S(1)} async-done(((bf16[64,152,128]{2,1,0:T(8,128)(2,1)}), bf16[64,152,128]{2,1,0:T(8,128)(2,1)S(1)}, u32[]{:S(2)}, u32[]{:S(2)}) %all-to-all-start.1) | async-done | bytes 2490400 | tf_op jit(solution)/shard_map/all_to_all | solution.py:444
  68.4 0.6 turn.1
  69.0 3.0 %collective-permute-start.1 = (bf16[2,144,16,128]{3,2,1,0:T(8,128)(2,1)S(1)}, bf16[2,144,16,128]{3,2,1,0:T(8,128)(2,1)S(1)}, u32[]{:S(2)}, u32[]{:S(2)}) collective-permute-start(bf16[2,144,16,128]{3,2,1,0:T(8,128)(2,1)S(1)} %get-tuple-element.29.first), channel_id=1, source_target_pairs={{0,1},{1,0},{2,3},{3,2},{4,5},{5,4},{6,7},{7,6},{8,9},{9,8},{10,11... | collective-permute-start | bytes 3538952 | tf_op jit(solution)/shard_map/ppermute | solution.py:435
  72.1 0.1 collective-permute-start
  72.2 0.4 collective-permute-start.2
  72.6 1.4 %place_own.1.before = bf16[144,128,128]{2,1,0:T(8,128)(2,1)} custom-call(bf16[2,144,16,128]{3,2,1,0:T(8,128)(2,1)S(1)} %get-tuple-element.29.first, bf16[2,144,16,128]{3,2,1,0:T(8,128)(2,1)S(1)} %get-tuple-element.28.last), custom_call_target="tpu_custom_call" | custom-call | bytes 4800000 | tf_op jit(solution)/shard_map/place_own/pallas_call | solution.py:363
  74.0 0.0 copy-start.3
  74.0 0.0 copy-start.4
  74.0 0.0 copy-start.5
  74.1 0.5 collective-permute-done.1.planes
  74.5 1.0 %place_first.1.before = bf16[144,128,128]{2,1,0:T(8,128)(2,1)} custom-call(bf16[2,144,16,128]{3,2,1,0:T(8,128)(2,1)S(1)} %collective-permute-done.1.planes, bf16[144,128,128]{2,1,0:T(8,128)(2,1)} %place_own.1.before), custom_call_target="tpu_custom_call", output_to_operand_aliasing={{}: (1, {})} | custom-call | bytes 2400000 | tf_op jit(solution)/shard_map/place_first/pallas_call | solution.py:380
  75.6 0.7 collective-permute-done.2.other
  76.3 0.0 collective-permute-done.planes
  76.3 0.0 copy-done.3
  76.3 0.0 copy-done.4
  76.3 0.0 copy-done.5
  76.3 1.2 %finish.1 = (bf16[144,128,128]{2,1,0:T(8,128)(2,1)}, f32[2,128,128]{2,1,0:T(8,128)}, f32[2,128,128]{2,1,0:T(8,128)}, f32[2,128,128]{2,1,0:T(8,128)}) custom-call(bf16[2,144,16,128]{3,2,1,0:T(8,128)(2,1)S(1)} %collective-permute-done.planes, bf16[144,128,128]{2,1,0:T(8,128)(2,1)} %place_first.1.before, ...), custom_call_target="tpu_custom_call", output_to_operand_aliasing={{0}: (1, {})} | custom-call | flops 600000 | bytes 3600000 | tf_op jit(solution)/shard_map/finish/pallas_call | solution.py:416
Async XLA Ops:
  4.3 32.5 %copy-start.6 = (s32[1,7]{1,0:T(1,128)S(1)}, s32[1,7]{1,0:T(1,128)}, u32[]{:S(2)}) copy-start(s32[1,7]{1,0:T(1,128)} %sel.1) | copy-start | bytes 88
  4.3 25.1 %all-to-all-start = ((s32[128,8,128]{2,1,0:T(8,128)}), s32[128,8,128]{2,1,0:T(8,128)S(1)}, u32[]{:S(2)}, u32[]{:S(2)}) async-start(s32[128,8,128]{2,1,0:T(8,128)} %bitcast.5), calls=%async_computation | async-start | bytes 1048576 | tf_op jit(solution)/shard_map/all_to_all | solution.py:440
  15.8 0.7 copy-start.7
  16.5 0.7 copy-start.8
  30.2 1.5 %copy-start.2 = (bf16[64,152,128]{2,1,0:T(8,128)(2,1)}, bf16[64,152,128]{2,1,0:T(8,128)(2,1)S(1)}, u32[]{:S(2)}) copy-start(bf16[64,152,128]{2,1,0:T(8,128)(2,1)S(1)} %get-tuple-element.25) | copy-start | bytes 7471108
  31.7 36.7 %all-to-all-start.1 = ((bf16[64,152,128]{2,1,0:T(8,128)(2,1)}), bf16[64,152,128]{2,1,0:T(8,128)(2,1)S(1)}, u32[]{:S(2)}, u32[]{:S(2)}) async-start(bf16[64,152,128]{2,1,0:T(8,128)(2,1)} %copy-done.2), calls=%async_computation.1 | async-start | bytes 4980736 | tf_op jit(solution)/shard_map/all_to_all | solution.py:444
  36.8 3.7 %copy-start = (f32[144,128,128]{2,1,0:T(8,128)S(1)}, f32[144,128,128]{2,1,0:T(8,128)}, u32[]{:S(2)}) copy-start(f32[144,128,128]{2,1,0:T(8,128)} %error.3) | copy-start | bytes 28311556
  40.4 2.3 %copy-start.1 = (bf16[144,128,128]{2,1,0:T(8,128)(2,1)S(1)}, bf16[144,128,128]{2,1,0:T(8,128)(2,1)}, u32[]{:S(2)}) copy-start(bf16[144,128,128]{2,1,0:T(8,128)(2,1)} %grad.3) | copy-start | bytes 14155780
  69.0 5.5 %collective-permute-start.1 = (bf16[2,144,16,128]{3,2,1,0:T(8,128)(2,1)S(1)}, bf16[2,144,16,128]{3,2,1,0:T(8,128)(2,1)S(1)}, u32[]{:S(2)}, u32[]{:S(2)}) collective-permute-start(bf16[2,144,16,128]{3,2,1,0:T(8,128)(2,1)S(1)} %get-tuple-element.29.first), channel_id=1, source_target_pairs={{0,1},{1,0},{2,3},{3,2},{4,5},{5,4},{6,7},{7,6},{8,9},{9,8},{10,11... | collective-permute-start | bytes 3538952 | tf_op jit(solution)/shard_map/ppermute | solution.py:435
  72.1 4.3 %collective-permute-start = (bf16[2,144,16,128]{3,2,1,0:T(8,128)(2,1)S(1)}, bf16[2,144,16,128]{3,2,1,0:T(8,128)(2,1)S(1)}, u32[]{:S(2)}, u32[]{:S(2)}) collective-permute-start(bf16[2,144,16,128]{3,2,1,0:T(8,128)(2,1)S(1)} %get-tuple-element.28.last), channel_id=1, source_target_pairs={{0,1},{1,0},{2,3},{3,2},{4,5},{5,4},{6,7},{7,6},{8,9},{9,8},{10,11... | collective-permute-start | bytes 3538952 | tf_op jit(solution)/shard_map/ppermute | solution.py:435
  72.2 4.2 %collective-permute-start.2 = (f32[2,64,128]{2,1,0:T(8,128)S(1)}, f32[2,64,128]{2,1,0:T(8,128)S(1)}, u32[]{:S(2)}, u32[]{:S(2)}) collective-permute-start(f32[2,64,128]{2,1,0:T(8,128)S(1)} %get-tuple-element.33), channel_id=1, source_target_pairs={{0,1},{1,0},{2,3},{3,2},{4,5},{5,4},{6,7},{7,6},{8,9},{9,8},{10,11... | collective-permute-start | bytes 196616 | tf_op jit(solution)/shard_map/ppermute | solution.py:435
  74.0 2.3 %copy-start.3 = (f32[2,128,128]{2,1,0:T(8,128)S(1)}, f32[2,128,128]{2,1,0:T(8,128)}, u32[]{:S(2)}) copy-start(f32[2,128,128]{2,1,0:T(8,128)} %master.3) | copy-start | bytes 393220
  74.0 2.3 %copy-start.4 = (f32[2,128,128]{2,1,0:T(8,128)S(1)}, f32[2,128,128]{2,1,0:T(8,128)}, u32[]{:S(2)}) copy-start(f32[2,128,128]{2,1,0:T(8,128)} %moment1.3) | copy-start | bytes 393220
  74.0 2.3 %copy-start.5 = (f32[2,128,128]{2,1,0:T(8,128)S(1)}, f32[2,128,128]{2,1,0:T(8,128)}, u32[]{:S(2)}) copy-start(f32[2,128,128]{2,1,0:T(8,128)} %moment2.3) | copy-start | bytes 393220

commit v4 on v2

--- a/solution.py
+++ b/solution.py
@@ -16,11 +16,13 @@
 N_COL = 8
 DEVICES = N_ROW * N_COL
 PLANE = N_ROW
+CHIPS = 4 * PLANE
 
 MSG = 8
 STATE_ROW = 4
 INFO_ROW = 7
 SCALE_LANE = 8
+RIDE = 8
 UNIT = 2.0**26
 STEPS = 32767.0
 ROOT_STEPS = 65535.0
@@ -201,11 +203,14 @@
     slot = (grid_row - row_start) + (grid_col - col_start)
     for s in range(OWNCAP):
         slot_map[:, s * BS : (s + 1) * BS] = jnp.where((owner == lane) & (slot == s), 1.0, 0.0).astype(BF16)
-    holder = lax.broadcasted_iota(I32, (DEVICES * OWNCAP, BS), 0)
+    holder = lax.broadcasted_iota(I32, (RIDE * CHIPS, BS), 0)
+    chip = holder // RIDE
     slot = holder % OWNCAP
-    holder = holder // OWNCAP
-    band_row = holder // N_COL
-    band_col = holder - band_row * N_COL
+    core = lax.axis_index("core")
+    band_row = chip % PLANE
+    at_z = lax.axis_index("z") + chip // PLANE
+    at_z = jnp.where(at_z >= 4, at_z - 4, at_z)
+    band_col = at_z * 2 + jnp.where(holder % 4 < OWNCAP, core, 1 - core)
     top = jnp.zeros_like(holder)
     end = jnp.zeros_like(holder)
     for k in range(N_ROW):
@@ -218,7 +223,7 @@
         right = jnp.where(band_col == k, cols_ref[k + 1], right)
     at_row = top + slot
     target = jnp.where((at_row < end) & (left < right), at_row * GC + left, -1)
-    lane = lax.broadcasted_iota(I32, (DEVICES * OWNCAP, BS), 1)
+    lane = lax.broadcasted_iota(I32, (RIDE * CHIPS, BS), 1)
     for part in range(2):
         block_map[:, part * BS : (part + 1) * BS] = jnp.where(target == lane + part * BS, 1.0, 0.0).astype(BF16)
     band_row = lax.axis_index("row")
@@ -238,7 +243,7 @@
         out_specs=[VMEM] * 3,
         out_shape=[
             jax.ShapeDtypeStruct((BLOCKS, OWNCAP * BS), BF16),
-            jax.ShapeDtypeStruct((OWNCAP * DEVICES, 2 * BS), BF16),
+            jax.ShapeDtypeStruct((RIDE * CHIPS, 2 * BS), BF16),
             jax.ShapeDtypeStruct((16, 2 * BS), BF16),
         ],
         compiler_params=PARAMS,
@@ -247,7 +252,7 @@
     )(row_bounds, col_bounds)
 
 
-def directions_kernel(got, slot_map, block_map, own_map, message, owned, flags):
+def directions_kernel(got, slot_map, block_map, own_map, message, across, flags):
     def rows(k):
         return got[pl.ds(k, DEVICES, stride=MSG), :]
 
@@ -285,12 +290,18 @@
 
     direction = adamw(totals, master, moment1, root2 * root2)[2]
     direction = jnp.where(tallies > 0.5, direction, 0.0).astype(BF16)
-    for i in range(PLANE):
-        message[i] = direction
-
     padded = jnp.concatenate([totals, jnp.zeros((2 * BS - BLOCKS, BS), F32)], axis=0)
     sums = jnp.dot(block_map[...], jnp.concatenate(three_terms(padded), axis=1), preferred_element_type=F32)
-    owned[...] = (sums[:, :BS] + sums[:, BS : 2 * BS]) + sums[:, 2 * BS :]
+    high, low, _ = three_terms((sums[:, :BS] + sums[:, BS : 2 * BS]) + sums[:, 2 * BS :])
+    term = lax.broadcasted_iota(I32, (RIDE * CHIPS, BS), 0) % RIDE < RIDE // 2
+    both = jnp.where(term, high.astype(F32), low.astype(F32)).astype(BF16)
+    for i in range(PLANE):
+        message[i, :BLOCKS] = direction
+        for n, away in enumerate((0, 1, 3)):
+            first = (away * PLANE + i) * RIDE
+            message[i, BLOCKS + n * RIDE : BLOCKS + (n + 1) * RIDE] = both[first : first + RIDE]
+    across[:BLOCKS] = direction
+    across[BLOCKS:] = both[2 * PLANE * RIDE : 3 * PLANE * RIDE]
 
     padded = jnp.concatenate([tallies, jnp.zeros((2 * BS - BLOCKS, BS), F32)], axis=0).astype(BF16)
     flags[...] = jnp.dot(own_map[...], padded, preferred_element_type=F32)
@@ -302,8 +313,8 @@
         in_specs=[VMEM] * 4,
         out_specs=[VMEM] * 3,
         out_shape=[
-            jax.ShapeDtypeStruct((PLANE, BLOCKS, BS), BF16),
-            jax.ShapeDtypeStruct((OWNCAP * DEVICES, BS), F32),
+            jax.ShapeDtypeStruct((PLANE, BLOCKS + 3 * RIDE, BS), BF16),
+            jax.ShapeDtypeStruct((BLOCKS + PLANE * RIDE, BS), BF16),
             jax.ShapeDtypeStruct((16, BS), F32),
         ],
         compiler_params=PARAMS,
@@ -315,84 +326,126 @@
 PITCH = BLOCKS + 1
 
 
-def turn_kernel(rows, out, scratch):
-    for chip in range(PLANE):
-        scratch[pl.ds(chip * PITCH, BLOCKS), :] = rows[chip].astype(F32)
-    for b in range(BLOCKS):
-        out[b] = scratch[pl.ds(b, PLANE, stride=PITCH), :].astype(BF16)
+PIECE = BLOCKS + RIDE
 
 
 def turn(rows):
-    return pl.pallas_call(
-        turn_kernel,
+    count = (rows.shape[1] - BLOCKS) // RIDE
+    pitch = rows.shape[1] + 1
+
+    def kernel(rows, *rest):
+        pieces, scratch = rest[:-1], rest[-1]
+        for chip in range(PLANE):
+            scratch[pl.ds(chip * pitch, pitch - 1), :] = rows[chip].astype(F32)
+
+        def tile(row):
+            return scratch[pl.ds(row, PLANE, stride=pitch), :].astype(BF16)
+
+        for b in range(BLOCKS):
+            turned = tile(b)
+            for piece in pieces:
+                piece[b] = turned
+        for n, piece in enumerate(pieces):
+            for t in range(RIDE):
+                piece[BLOCKS + t] = tile(BLOCKS + n * RIDE + t)
+
+    return pl.pallas_call(
+        kernel,
+        in_specs=[VMEM],
+        out_specs=[VMEM] * count,
+        out_shape=[jax.ShapeDtypeStruct((PIECE, PLANE, BS), BF16)] * count,
+        scratch_shapes=[pltpu.VMEM((PLANE * pitch, BS), F32)],
+        compiler_params=PARAMS,
+        cost_estimate=pl.CostEstimate(flops=600_000, bytes_accessed=2_000_000, transcendentals=0),
+        name="turn",
+    )(rows)
+
+
+def relay_kernel(got, message):
+    for i in range(PLANE):
+        message[i, :BLOCKS] = got[:BLOCKS]
+        message[i, BLOCKS:] = got[BLOCKS + i * RIDE : BLOCKS + (i + 1) * RIDE]
+
+
+def relay(got):
+    return pl.pallas_call(
+        relay_kernel,
         in_specs=[VMEM],
         out_specs=VMEM,
-        out_shape=jax.ShapeDtypeStruct((BLOCKS, PLANE, BS), BF16),
-        scratch_shapes=[pltpu.VMEM((PLANE * PITCH, BS), F32)],
+        out_shape=jax.ShapeDtypeStruct((PLANE, PIECE, BS), BF16),
         compiler_params=PARAMS,
-        cost_estimate=pl.CostEstimate(flops=600_000, bytes_accessed=1_200_000, transcendentals=0),
-        name="turn",
-    )(rows)
-
-
-def place(steps, pieces):
-    arrays = [a for piece in pieces for a in piece[2:]]
+        cost_estimate=pl.CostEstimate(flops=0, bytes_accessed=700_000, transcendentals=0),
+        name="relay",
+    )(got)
+
+
+def settle(pieces, flags, master, moment1, moment2, before):
+    arrays = [a for piece in pieces for a in piece[1:]]
+    aliased = list(before)
 
     def kernel(*refs):
-        inputs, out, sems = refs[: len(arrays)], refs[-2], refs[-1]
+        inputs, refs = refs[: len(arrays)], refs[len(arrays) :]
+        flags, master, moment1, moment2 = refs[:4]
+        refs = refs[4 + len(aliased) :]
+        steps, outs, new, sems, new_sems = refs[0], refs[1:4], refs[4], refs[5], refs[6]
         z, core = lax.axis_index("z"), lax.axis_index("core")
         copies = []
+        places = []
         for n, ref in enumerate(inputs):
-            first, away = pieces[n // 2][:2]
-            at = first_row(lax.rem(z + away, N_COL // 2), core if n % 2 == 0 else 1 - core)
-            target = out.at[pl.ds(first, ref.shape[0]), pl.ds(pl.multiple_of(at, PLANE), PLANE)]
-            copies.append(pltpu.make_async_copy(ref, target, sems.at[n]))
-        for copy in copies:
-            copy.start()
+            at = first_row(lax.rem(z + pieces[n // 2][0], 4), core if n % 2 == 0 else 1 - core)
+            rows = pl.ds(pl.multiple_of(at, PLANE), PLANE)
+            places.append(rows)
+            copies.append(pltpu.make_async_copy(ref.at[pl.ds(0, BLOCKS)], steps.at[:, rows], sems.at[n]))
+            copies[-1].start()
+        for n, ref in enumerate(inputs):
+            rows = places[n]
+            for s in range(OWNCAP):
+                tile = BLOCKS + n % 2 * OWNCAP + s
+                totals = ref[tile].astype(F32) + ref[tile + RIDE // 2].astype(F32)
+                old = [array[s, rows, :] for array in (master, moment1, moment2)]
+                changed = flags[s : s + 1] > 0.5
+                new1, new2, direction = adamw(totals, *old)
+                new[0, s, rows] = jnp.where(changed, old[0] - LEARN_RATE * direction, old[0])
+                new[1, s, rows] = jnp.where(changed, new1, old[1])
+                new[2, s, rows] = jnp.where(changed, new2, old[2])
+        for n in range(len(inputs)):
+            rows = places[n]
+            for array in range(3):
+                for s in range(OWNCAP):
+                    copies.append(
+                        pltpu.make_async_copy(
+                            new.at[array, s, rows], outs[array].at[s, rows], new_sems.at[n, array, s]
+                        )
+                    )
+                    copies[-1].start()
         for copy in copies:
             copy.wait()
 
+    slots = jax.ShapeDtypeStruct((OWNCAP, BS, BS), F32)
     return pl.pallas_call(
         kernel,
-        in_specs=[VMEM] * len(arrays) + ([] if steps is None else [HBM]),
-        out_specs=HBM,
-        out_shape=jax.ShapeDtypeStruct((BLOCKS, BS, BS), BF16),
-        scratch_shapes=[pltpu.SemaphoreType.DMA((len(arrays),))],
-        input_output_aliases={} if steps is None else {len(arrays): 0},
+        in_specs=[VMEM] * (len(arrays) + 4) + [HBM] * len(aliased),
+        out_specs=[HBM] * 4,
+        out_shape=[jax.ShapeDtypeStruct((BLOCKS, BS, BS), BF16), slots, slots, slots],
+        scratch_shapes=[
+            pltpu.VMEM((3, OWNCAP, BS, BS), F32),
+            pltpu.SemaphoreType.DMA((len(arrays),)),
+            pltpu.SemaphoreType.DMA((len(arrays), 3, OWNCAP)),
+        ],
+        input_output_aliases={len(arrays) + 4 + n: n for n in range(len(aliased))},
         compiler_params=PARAMS,
-        cost_estimate=pl.CostEstimate(flops=0, bytes_accessed=2_400_000, transcendentals=0),
-        name="place",
-    )(*arrays, *([] if steps is None else [steps]))
-
-
-def update_kernel(owned, flags, master, moment1, moment2, master_out, moment1_out, moment2_out, totals):
-    for s in range(OWNCAP):
-        for col in range(N_COL):
-            at = first_row(col // 2, col % 2)
-            totals[s, at : at + PLANE] = owned[pl.ds(col * OWNCAP + s, PLANE, stride=N_COL * OWNCAP), :]
-        changed = flags[s : s + 1] > 0.5
-        new1, new2, direction = adamw(totals[s], master[s], moment1[s], moment2[s])
-        master_out[s] = jnp.where(changed, master[s] - LEARN_RATE * direction, master[s])
-        moment1_out[s] = jnp.where(changed, new1, moment1[s])
-        moment2_out[s] = jnp.where(changed, new2, moment2[s])
-
-
-def update(owned, flags, master, moment1, moment2):
-    slots = jax.ShapeDtypeStruct((OWNCAP, BS, BS), F32)
-    return pl.pallas_call(
-        update_kernel,
-        in_specs=[VMEM] * 5,
-        out_specs=[VMEM] * 3,
-        out_shape=[slots] * 3,
-        scratch_shapes=[pltpu.VMEM((OWNCAP, BS, BS), F32)],
-        compiler_params=PARAMS,
-        cost_estimate=pl.CostEstimate(flops=600_000, bytes_accessed=900_000, transcendentals=33_000),
-        name="update",
-    )(owned, flags, master, moment1, moment2)
+        cost_estimate=pl.CostEstimate(flops=600_000, bytes_accessed=2_400_000, transcendentals=33_000),
+        name="settle",
+    )(*arrays, flags, master, moment1, moment2, *aliased)
 
 
 RIGHT = [(i, (i + 1) % 4) for i in range(4)]
 LEFT = [(i, (i + 3) % 4) for i in range(4)]
+ACROSS = [(i, (i + 2) % 4) for i in range(4)]
+
+
+def swap(piece):
+    return lax.ppermute(piece, "core", [(0, 1), (1, 0)])
 
 
 def local(grad, error, sel_blocks, row_bounds, col_bounds, master, moment1, moment2):
@@ -401,30 +454,32 @@
     slot_map, block_map, own_map = maps(row_bounds, col_bounds)
     error_out = feedback(sel_blocks, grad, error, 0, None)
     got, error_out = lax.optimization_barrier((got, error_out))
-    message, owned, flags = directions(got, slot_map, block_map, own_map)
+    message, across, flags = directions(got, slot_map, block_map, own_map)
+
+    def exchange(message):
+        rows = message.shape[1]
+        got = lax.all_to_all(message.reshape(PLANE * rows, BS), "row", split_axis=0, concat_axis=0, tiled=True)
+        return got.reshape(PLANE, rows, BS)
 
     message, error_out = lax.optimization_barrier((message, error_out))
-    plane = lax.all_to_all(message.reshape(PLANE * BLOCKS, BS), "row", split_axis=0, concat_axis=0, tiled=True)
+    plane = exchange(message)
+    far_message = relay(lax.ppermute(across, "z", ACROSS))
     error_out = feedback(sel_blocks, grad, error, 1, error_out)
-    plane, error_out = lax.optimization_barrier((plane, error_out))
-    mine = turn(plane.reshape(PLANE, BLOCKS, BS))
-    mine, owned = lax.optimization_barrier((mine, owned))
-
-    def swap(piece):
-        return lax.ppermute(piece, "core", [(0, 1), (1, 0)])
-
-    half = BLOCKS // 2
-    before = lax.ppermute(mine, "z", RIGHT)
-    after = lax.ppermute(mine, "z", LEFT)
+    plane, far_message, error_out = lax.optimization_barrier((plane, far_message, error_out))
+    mine, right, left = turn(plane)
+
+    before = lax.ppermute(right, "z", RIGHT)
+    after = lax.ppermute(left, "z", LEFT)
     mine_too = swap(mine)
-    owned = lax.all_to_all(owned, ("row", "z", "core"), split_axis=0, concat_axis=0, tiled=True)
-    before, after, mine_too, owned = lax.optimization_barrier((before, after, mine_too, owned))
-    far_first = lax.ppermute(before[:half], "z", RIGHT)
-    far_last = lax.ppermute(after[half:], "z", LEFT)
-    steps = place(None, [(0, 0, mine, mine_too), (0, 3, before, swap(before)), (0, 1, after, swap(after))])
-    states = update(owned, flags, master, moment1, moment2)
-    far_first, far_last, steps, states = lax.optimization_barrier((far_first, far_last, steps, states))
-    steps = place(steps, [(0, 2, far_first, swap(far_first)), (half, 2, far_last, swap(far_last))])
+    far_message, mine = lax.optimization_barrier((far_message, mine))
+    far_plane = exchange(far_message)
+    outs = settle([(0, mine, mine_too)], flags, master, moment1, moment2, ())
+    before, after, far_plane, outs = lax.optimization_barrier((before, after, far_plane, outs))
+    (far,) = turn(far_plane)
+    before_too, after_too, far_too = swap(before), swap(after), swap(far)
+    outs = settle([(3, before, before_too), (1, after, after_too)], flags, master, moment1, moment2, outs)
+    far_too, outs = lax.optimization_barrier((far_too, outs))
+    steps, *states = settle([(2, far, far_too)], flags, master, moment1, moment2, outs)
     return (error_out, *states, steps)
 
 

time: 81.7 us -> 76 us (0.930)
  blocking collectives: 17.8 us -> 0 us
  starting transfers between devices: 22.3 us -> 27.7 us
  Pallas kernels: 22.6 us -> 26.6 us
  waiting for transfers between devices: 16.3 us -> 19.1 us
    all_to_all x1 -> x0, blocking collectives: 17.8 us -> none  [local(): lax.all_to_all(owned, ('row', 'z', 'core'), split_axis=0, concat_axis=0,...]
    all_to_all x1 -> x2, waiting for transfers between devices: 4.64 us -> 12.5 us  [exchange(): lax.all_to_all(message.reshape(PLANE * rows, BS), 'row', split_axis=0, co...]
    ppermute x4 -> x3, waiting for transfers between devices: 5.03 us -> 0.01 us  [the longest x1 0.01 us: local(): far_message = relay(lax.ppermute(across, 'z', ACROSS))]
    pallas_call x4 -> x6, Pallas kernels: 3.9 us -> 7.55 us  [the longest x3 5.18 us: settle(): pl.pallas_call(kernel, in_specs=[VMEM] * (len(arrays) + 4) + [HBM] * len(...]
    all_to_all x1 -> x2, starting transfers between devices: 3.58 us -> 7.19 us  [exchange(): lax.all_to_all(message.reshape(PLANE * rows, BS), 'row', split_axis=0, co...]
    ppermute x4 -> x3, starting transfers between devices: 3.01 us -> 4.34 us  [the longest x1 2.56 us: local(): after = lax.ppermute(left, 'z', LEFT)]
    ppermute x5 -> x4, starting transfers between devices: 4.25 us -> 4.65 us  [swap(): return lax.ppermute(piece, 'core', [(0, 1), (1, 0)])]
    ppermute x5 -> x4, waiting for transfers between devices: 1.63 us -> 1.83 us  [swap(): return lax.ppermute(piece, 'core', [(0, 1), (1, 0)])]
  transfers between devices with their start and end apart: 11 -> 10, of which waited for: 6 -> 5; matrix products, arithmetic and copies ran while one was open for 0% -> 0% of each run, Pallas kernels for 20% -> 25%
where the time goes in v4:
time: 76 us; the launch traced here: 75.4 us
  starting transfers between devices  27.7 us (36%)
  Pallas kernels  26.6 us (35%)
  waiting for transfers between devices  19.1 us (25%)
  local copies, waits for them, and re-layouts  1.32 us (2%)
  between operations  0.77 us (1%)
    pallas_call x2, Pallas kernels, feedback(): pl.pallas_call(kernel, in_specs=[SMEM] + [HBM] * 2 + [HBM] * len(more), o...  12.5 us
    all_to_all x2, waiting for transfers between devices, exchange(): lax.all_to_all(message.reshape(PLANE * rows, BS), 'row', split_axis=0, co...  12.5 us
    all_to_all x1, starting transfers between devices, local(): lax.all_to_all(send, ('row', 'z', 'core'), split_axis=0, concat_axis=0, t...  11.5 us
    all_to_all x2, starting transfers between devices, exchange(): lax.all_to_all(message.reshape(PLANE * rows, BS), 'row', split_axis=0, co...  7.19 us
    pallas_call x3, Pallas kernels, settle(): pl.pallas_call(kernel, in_specs=[VMEM] * (len(arrays) + 4) + [HBM] * len(...  5.18 us
    all_to_all x1, waiting for transfers between devices, local(): lax.all_to_all(send, ('row', 'z', 'core'), split_axis=0, concat_axis=0, t...  4.74 us
    ppermute x4, starting transfers between devices, swap(): return lax.ppermute(piece, 'core', [(0, 1), (1, 0)])  4.65 us
    pallas_call x1, Pallas kernels, pack(): pl.pallas_call(pack_kernel, in_specs=[HBM] * 6, out_specs=VMEM, out_shape...  3.63 us
  transfers between devices with their start and end apart: 10, of which 5 were waited for; matrix products, arithmetic and copies ran while one was open for 0% of the time, Pallas kernels for 25%

profile of v4, /device:TPU:1, one launch (start us, length us, event | category | flops | bytes accessed | tf_op | source)
XLA Modules:
  0.0 75.4 jit_solution(7099947646119364552)
XLA Ops:
  0.6 3.6 %pack_rows.1 = s32[1024,128]{1,0:T(8,128)} custom-call(s32[1,7]{1,0:T(1,128)} %refs_0_.3, bf16[144,128,128]{2,1,0:T(8,128)(2,1)} %refs_1_.3, f32[144,128,128]{2,1,0:T(8,128)} %refs_2_.3, f32[2,128,128]{2,1,0:T(8,128)} %refs_3_.3, f32[2,128,128]{2,1,0:T(8,128)} %refs_4_.3, f32[2,128,128]{2,1,0:T(8,128)} %refs_5_.5), custom_call_target="tpu_custom_call" | custom-call | flops 200000 | bytes 2200000 | tf_op jit(solution)/shard_map/pack_rows/pallas_call | solution.py:132
  4.3 11.5 %all-to-all-start = ((s32[128,8,128]{2,1,0:T(8,128)}), s32[128,8,128]{2,1,0:T(8,128)S(1)}, u32[]{:S(2)}, u32[]{:S(2)}) async-start(s32[128,8,128]{2,1,0:T(8,128)} %bitcast.3), calls=%async_computation | async-start | bytes 1048576 | tf_op jit(solution)/shard_map/all_to_all | solution.py:453
  15.8 0.0 copy-start.3
  15.8 0.6 copy-done.3
  16.4 0.0 copy-start.4
  16.4 0.7 copy-done.4
  17.1 1.3 %slot_maps.1 = (bf16[144,256]{1,0:T(8,128)(2,1)S(1)}, bf16[512,256]{1,0:T(8,128)(2,1)S(1)}, bf16[16,256]{1,0:T(8,128)(2,1)S(1)}) custom-call(s32[17]{0:T(128)S(1)} %copy-done.3, s32[9]{0:T(128)S(1)} %copy-done.4), custom_call_target="tpu_custom_call" | custom-call | flops 500000 | bytes 300000 | tf_op jit(solution)/shard_map/slot_maps/pallas_call | solution.py:240
  18.4 6.3 %error_feedback.2.refs_3_ = f32[144,128,128]{2,1,0:T(8,128)} custom-call(s32[1,7]{1,0:T(1,128)} %refs_0_.3, bf16[144,128,128]{2,1,0:T(8,128)(2,1)} %refs_1_.3, f32[144,128,128]{2,1,0:T(8,128)} %refs_2_.3), custom_call_target="tpu_custom_call" | custom-call | flops 2500000 | bytes 11800000 | tf_op jit(solution)/shard_map/error_feedback/pallas_call | solution.py:183
  24.6 4.7 %all-to-all-done = s32[128,8,128]{2,1,0:T(8,128)S(1)} async-done(((s32[128,8,128]{2,1,0:T(8,128)}), s32[128,8,128]{2,1,0:T(8,128)S(1)}, u32[]{:S(2)}, u32[]{:S(2)}) %all-to-all-start) | async-done | bytes 524320 | tf_op jit(solution)/shard_map/all_to_all | solution.py:453
  29.4 1.6 %directions.1 = (bf16[16,168,128]{2,1,0:T(8,128)(2,1)}, bf16[272,128]{1,0:T(8,128)(2,1)S(1)}, f32[16,128]{1,0:T(8,128)S(1)}) custom-call(s32[1024,128]{1,0:T(8,128)S(1)} %bitcast.2, bf16[144,256]{1,0:T(8,128)(2,1)S(1)} %get-tuple-element.48.slot_map, bf16[512,256]{1,0:T(8,128)(2,1)S(1)} %get-tuple-element.49.block_map, ...), custom_call_target="tpu_custom_call" | custom-call | flops 200000000 | bytes 2000000 | tf_op jit(solution)/shard_map/directions/pallas_call | solution.py:311
  31.0 3.6 %all-to-all-start.1 = ((bf16[16,168,128]{2,1,0:T(8,128)(2,1)}), bf16[16,168,128]{2,1,0:T(8,128)(2,1)S(1)}, u32[]{:S(2)}, u32[]{:S(2)}) async-start(bf16[16,168,128]{2,1,0:T(8,128)(2,1)} %get-tuple-element.53), calls=%async_computation.1 | async-start | bytes 1376256 | tf_op jit(solution)/shard_map/all_to_all | solution.py:461
  34.6 0.0 copy-start
  34.6 0.0 copy-start.1
  34.6 0.0 copy-start.2
  34.6 1.7 %collective-permute-start = (bf16[272,128]{1,0:T(8,128)(2,1)S(1)}, bf16[272,128]{1,0:T(8,128)(2,1)S(1)}, u32[]{:S(2)}, u32[]{:S(2)}) collective-permute-start(bf16[272,128]{1,0:T(8,128)(2,1)S(1)} %get-tuple-element.54), channel_id=1, source_target_pairs={{0,4},{2,6},{4,0},{6,2},{1,5},{3,7},{5,1},{7,3},{8,12},{10,14},{12... | collective-permute-start | bytes 208904 | tf_op jit(solution)/shard_map/ppermute | solution.py:466
  36.3 6.3 %error_feedback.3 = f32[144,128,128]{2,1,0:T(8,128)} custom-call(s32[1,7]{1,0:T(1,128)} %refs_0_.3, bf16[144,128,128]{2,1,0:T(8,128)(2,1)} %refs_1_.3, f32[144,128,128]{2,1,0:T(8,128)} %refs_2_.3, f32[144,128,128]{2,1,0:T(8,128)} %error_feedback.2.refs_3_), custom_call_target="tpu_custom_call", output_to_operand_aliasing={{}: (3, {})} | custom-call | flops 2500000 | bytes 11800000 | tf_op jit(solution)/shard_map/error_feedback/pallas_call | solution.py:183
  42.5 0.0 collective-permute-done.got
  42.5 0.9 %relay.1 = bf16[16,152,128]{2,1,0:T(8,128)(2,1)} custom-call(bf16[272,128]{1,0:T(8,128)(2,1)S(1)} %collective-permute-done.got), custom_call_target="tpu_custom_call" | custom-call | bytes 700000 | tf_op jit(solution)/shard_map/relay/pallas_call | solution.py:371
  43.5 2.9 %all-to-all-done.1.rows = bf16[16,168,128]{2,1,0:T(8,128)(2,1)S(1)} async-done(((bf16[16,168,128]{2,1,0:T(8,128)(2,1)}), bf16[16,168,128]{2,1,0:T(8,128)(2,1)S(1)}, u32[]{:S(2)}, u32[]{:S(2)}) %all-to-all-start.1) | async-done | bytes 688160 | tf_op jit(solution)/shard_map/all_to_all | solution.py:461
  46.4 1.3 %turn.2 = (bf16[152,16,128]{2,1,0:T(8,128)(2,1)S(1)}, bf16[152,16,128]{2,1,0:T(8,128)(2,1)}, bf16[152,16,128]{2,1,0:T(8,128)(2,1)}) custom-call(bf16[16,168,128]{2,1,0:T(8,128)(2,1)S(1)} %all-to-all-done.1.rows), custom_call_target="tpu_custom_call" | custom-call | flops 600000 | bytes 2000000 | tf_op jit(solution)/shard_map/turn/pallas_call | solution.py:352
  47.7 2.4 %collective-permute-start.3 = (bf16[152,16,128]{2,1,0:T(8,128)(2,1)S(1)}, bf16[152,16,128]{2,1,0:T(8,128)(2,1)}, u32[]{:S(2)}, u32[]{:S(2)}) collective-permute-start(bf16[152,16,128]{2,1,0:T(8,128)(2,1)S(1)} %get-tuple-element.63.refs_0_), channel_id=1, source_target_pairs={{0,1},{1,0},{2,3},{3,2},{4,5},{5,4},{6,7},{7,6},{8,9},{9,8},{10,11... | collective-permute-start | bytes 1867784 | tf_op jit(solution)/shard_map/ppermute | solution.py:448
  50.1 0.1 collective-permute-start.1
  50.2 2.6 %collective-permute-start.2 = (bf16[152,16,128]{2,1,0:T(8,128)(2,1)}, bf16[152,16,128]{2,1,0:T(8,128)(2,1)S(1)}, u32[]{:S(2)}, u32[]{:S(2)}) collective-permute-start(bf16[152,16,128]{2,1,0:T(8,128)(2,1)} %get-tuple-element.59), channel_id=1, source_target_pairs={{0,6},{2,0},{4,2},{6,4},{1,7},{3,1},{5,3},{7,5},{8,14},{10,8},{12,... | collective-permute-start | bytes 1867784 | tf_op jit(solution)/shard_map/ppermute | solution.py:472
  52.8 3.6 %all-to-all-start.2 = ((bf16[16,152,128]{2,1,0:T(8,128)(2,1)}), bf16[16,152,128]{2,1,0:T(8,128)(2,1)S(1)}, u32[]{:S(2)}, u32[]{:S(2)}) async-start(bf16[16,152,128]{2,1,0:T(8,128)(2,1)} %relay.1), calls=%async_computation.2 | async-start | bytes 1245184 | tf_op jit(solution)/shard_map/all_to_all | solution.py:461
  56.4 0.0 collective-permute-done.3.refs_1_
  56.4 0.0 copy-done
  56.4 0.0 copy-done.1
  56.4 0.0 copy-done.2
  56.4 2.2 %settle.3 = (bf16[144,128,128]{2,1,0:T(8,128)(2,1)}, f32[2,128,128]{2,1,0:T(8,128)}, f32[2,128,128]{2,1,0:T(8,128)}, f32[2,128,128]{2,1,0:T(8,128)}) custom-call(bf16[152,16,128]{2,1,0:T(8,128)(2,1)S(1)} %get-tuple-element.63.refs_0_, bf16[152,16,128]{2,1,0:T(8,128)(2,1)} %collective-permute-done.3.refs_1_, f32[16,128]{1,0:T(8,128)S(1)} %get-tuple-element.64.refs_2_.refs_4_, ...), custom_call_target="tpu_custom_call" | custom-call | flops 600000 | bytes 2400000 | tf_op jit(solution)/shard_map/settle/pallas_call | solution.py:425
  58.7 9.5 %all-to-all-done.2.rows = bf16[16,152,128]{2,1,0:T(8,128)(2,1)S(1)} async-done(((bf16[16,152,128]{2,1,0:T(8,128)(2,1)}), bf16[16,152,128]{2,1,0:T(8,128)(2,1)S(1)}, u32[]{:S(2)}, u32[]{:S(2)}) %all-to-all-start.2) | async-done | bytes 622624 | tf_op jit(solution)/shard_map/all_to_all | solution.py:461
  68.2 0.0 collective-permute-done.1.refs_0_
  68.2 0.0 collective-permute-done.2.refs_2_
  68.2 1.7 %collective-permute-start.5 = (bf16[152,16,128]{2,1,0:T(8,128)(2,1)S(1)}, bf16[152,16,128]{2,1,0:T(8,128)(2,1)S(1)}, u32[]{:S(2)}, u32[]{:S(2)}) collective-permute-start(bf16[152,16,128]{2,1,0:T(8,128)(2,1)S(1)} %collective-permute-done.1.refs_0_), channel_id=1, source_target_pairs={{0,1},{1,0},{2,3},{3,2},{4,5},{5,4},{6,7},{7,6},{8,9},{9,8},{10,11... | collective-permute-start | bytes 1867784 | tf_op jit(solution)/shard_map/ppermute | solution.py:448
  69.9 0.1 collective-permute-start.6
  70.0 0.1 turn.3.refs_0_
  70.1 0.5 collective-permute-start.4
  70.6 0.9 %collective-permute-done.5.refs_1_ = bf16[152,16,128]{2,1,0:T(8,128)(2,1)S(1)} collective-permute-done((bf16[152,16,128]{2,1,0:T(8,128)(2,1)S(1)}, bf16[152,16,128]{2,1,0:T(8,128)(2,1)S(1)}, u32[]{:S(2)}, u32[]{:S(2)}) %collective-permute-start.5) | collective-permute-done | bytes 622624 | tf_op jit(solution)/shard_map/ppermute | solution.py:448
  71.6 0.9 %collective-permute-done.6.refs_3_ = bf16[152,16,128]{2,1,0:T(8,128)(2,1)S(1)} collective-permute-done((bf16[152,16,128]{2,1,0:T(8,128)(2,1)S(1)}, bf16[152,16,128]{2,1,0:T(8,128)(2,1)S(1)}, u32[]{:S(2)}, u32[]{:S(2)}) %collective-permute-start.6) | collective-permute-done | bytes 622624 | tf_op jit(solution)/shard_map/ppermute | solution.py:448
  72.4 1.8 %settle.4 = (bf16[144,128,128]{2,1,0:T(8,128)(2,1)}, f32[2,128,128]{2,1,0:T(8,128)}, f32[2,128,128]{2,1,0:T(8,128)}, f32[2,128,128]{2,1,0:T(8,128)}) custom-call(bf16[152,16,128]{2,1,0:T(8,128)(2,1)S(1)} %collective-permute-done.1.refs_0_, ...), custom_call_target="tpu_custom_call", output_to_operand_aliasing={{0}: (8, {}), {1}: (9, {}), {2}: (10, {}), {3}: (11, {})} | custom-call | flops 600000 | bytes 2400000 | tf_op jit(solution)/shard_map/settle/pallas_call | solution.py:425
  74.2 0.0 collective-permute-done.4.refs_1_
  74.2 1.2 %settle.5 = (bf16[144,128,128]{2,1,0:T(8,128)(2,1)}, f32[2,128,128]{2,1,0:T(8,128)}, f32[2,128,128]{2,1,0:T(8,128)}, f32[2,128,128]{2,1,0:T(8,128)}) custom-call(bf16[152,16,128]{2,1,0:T(8,128)(2,1)S(1)} %turn.3.refs_0_, ...), custom_call_target="tpu_custom_call", output_to_operand_aliasing={{0}: (6, {}), {1}: (7, {}), {2}: (8, {}), {3}: (9, {})} | custom-call | flops 600000 | bytes 2400000 | tf_op jit(solution)/shard_map/settle/pallas_call | solution.py:425
Async XLA Ops:
  4.3 25.1 %all-to-all-start = ((s32[128,8,128]{2,1,0:T(8,128)}), s32[128,8,128]{2,1,0:T(8,128)S(1)}, u32[]{:S(2)}, u32[]{:S(2)}) async-start(s32[128,8,128]{2,1,0:T(8,128)} %bitcast.3), calls=%async_computation | async-start | bytes 1048576 | tf_op jit(solution)/shard_map/all_to_all | solution.py:453
  15.8 0.7 copy-start.3
  16.4 0.7 copy-start.4
  31.0 15.4 %all-to-all-start.1 = ((bf16[16,168,128]{2,1,0:T(8,128)(2,1)}), bf16[16,168,128]{2,1,0:T(8,128)(2,1)S(1)}, u32[]{:S(2)}, u32[]{:S(2)}) async-start(bf16[16,168,128]{2,1,0:T(8,128)(2,1)} %get-tuple-element.53), calls=%async_computation.1 | async-start | bytes 1376256 | tf_op jit(solution)/shard_map/all_to_all | solution.py:461
  34.6 21.8 %copy-start = (f32[2,128,128]{2,1,0:T(8,128)S(1)}, f32[2,128,128]{2,1,0:T(8,128)}, u32[]{:S(2)}) copy-start(f32[2,128,128]{2,1,0:T(8,128)} %refs_3_.3) | copy-start | bytes 393220
  34.6 21.8 %copy-start.1 = (f32[2,128,128]{2,1,0:T(8,128)S(1)}, f32[2,128,128]{2,1,0:T(8,128)}, u32[]{:S(2)}) copy-start(f32[2,128,128]{2,1,0:T(8,128)} %refs_4_.3) | copy-start | bytes 393220
  34.6 21.8 %copy-start.2 = (f32[2,128,128]{2,1,0:T(8,128)S(1)}, f32[2,128,128]{2,1,0:T(8,128)}, u32[]{:S(2)}) copy-start(f32[2,128,128]{2,1,0:T(8,128)} %refs_5_.5) | copy-start | bytes 393220
  34.6 7.9 %collective-permute-start = (bf16[272,128]{1,0:T(8,128)(2,1)S(1)}, bf16[272,128]{1,0:T(8,128)(2,1)S(1)}, u32[]{:S(2)}, u32[]{:S(2)}) collective-permute-start(bf16[272,128]{1,0:T(8,128)(2,1)S(1)} %get-tuple-element.54), channel_id=1, source_target_pairs={{0,4},{2,6},{4,0},{6,2},{1,5},{3,7},{5,1},{7,3},{8,12},{10,14},{12... | collective-permute-start | bytes 208904 | tf_op jit(solution)/shard_map/ppermute | solution.py:466
  47.7 8.7 %collective-permute-start.3 = (bf16[152,16,128]{2,1,0:T(8,128)(2,1)S(1)}, bf16[152,16,128]{2,1,0:T(8,128)(2,1)}, u32[]{:S(2)}, u32[]{:S(2)}) collective-permute-start(bf16[152,16,128]{2,1,0:T(8,128)(2,1)S(1)} %get-tuple-element.63.refs_0_), channel_id=1, source_target_pairs={{0,1},{1,0},{2,3},{3,2},{4,5},{5,4},{6,7},{7,6},{8,9},{9,8},{10,11... | collective-permute-start | bytes 1867784 | tf_op jit(solution)/shard_map/ppermute | solution.py:448
  50.1 18.1 %collective-permute-start.1 = (bf16[152,16,128]{2,1,0:T(8,128)(2,1)}, bf16[152,16,128]{2,1,0:T(8,128)(2,1)S(1)}, u32[]{:S(2)}, u32[]{:S(2)}) collective-permute-start(bf16[152,16,128]{2,1,0:T(8,128)(2,1)} %get-tuple-element.58), channel_id=1, source_target_pairs={{0,2},{2,4},{4,6},{6,0},{1,3},{3,5},{5,7},{7,1},{8,10},{10,12},{12... | collective-permute-start | bytes 1867784 | tf_op jit(solution)/shard_map/ppermute | solution.py:471
  50.2 18.0 %collective-permute-start.2 = (bf16[152,16,128]{2,1,0:T(8,128)(2,1)}, bf16[152,16,128]{2,1,0:T(8,128)(2,1)S(1)}, u32[]{:S(2)}, u32[]{:S(2)}) collective-permute-start(bf16[152,16,128]{2,1,0:T(8,128)(2,1)} %get-tuple-element.59), channel_id=1, source_target_pairs={{0,6},{2,0},{4,2},{6,4},{1,7},{3,1},{5,3},{7,5},{8,14},{10,8},{12,... | collective-permute-start | bytes 1867784 | tf_op jit(solution)/shard_map/ppermute | solution.py:472
  52.8 15.4 %all-to-all-start.2 = ((bf16[16,152,128]{2,1,0:T(8,128)(2,1)}), bf16[16,152,128]{2,1,0:T(8,128)(2,1)S(1)}, u32[]{:S(2)}, u32[]{:S(2)}) async-start(bf16[16,152,128]{2,1,0:T(8,128)(2,1)} %relay.1), calls=%async_computation.2 | async-start | bytes 1245184 | tf_op jit(solution)/shard_map/all_to_all | solution.py:461
  68.2 3.4 %collective-permute-start.5 = (bf16[152,16,128]{2,1,0:T(8,128)(2,1)S(1)}, bf16[152,16,128]{2,1,0:T(8,128)(2,1)S(1)}, u32[]{:S(2)}, u32[]{:S(2)}) collective-permute-start(bf16[152,16,128]{2,1,0:T(8,128)(2,1)S(1)} %collective-permute-done.1.refs_0_), channel_id=1, source_target_pairs={{0,1},{1,0},{2,3},{3,2},{4,5},{5,4},{6,7},{7,6},{8,9},{9,8},{10,11... | collective-permute-start | bytes 1867784 | tf_op jit(solution)/shard_map/ppermute | solution.py:448
  69.9 2.6 %collective-permute-start.6 = (bf16[152,16,128]{2,1,0:T(8,128)(2,1)S(1)}, bf16[152,16,128]{2,1,0:T(8,128)(2,1)S(1)}, u32[]{:S(2)}, u32[]{:S(2)}) collective-permute-start(bf16[152,16,128]{2,1,0:T(8,128)(2,1)S(1)} %collective-permute-done.2.refs_2_), channel_id=1, source_target_pairs={{0,1},{1,0},{2,3},{3,2},{4,5},{5,4},{6,7},{7,6},{8,9},{9,8},{10,11... | collective-permute-start | bytes 1867784 | tf_op jit(solution)/shard_map/ppermute | solution.py:448
  70.1 4.1 %collective-permute-start.4 = (bf16[152,16,128]{2,1,0:T(8,128)(2,1)S(1)}, bf16[152,16,128]{2,1,0:T(8,128)(2,1)S(1)}, u32[]{:S(2)}, u32[]{:S(2)}) collective-permute-start(bf16[152,16,128]{2,1,0:T(8,128)(2,1)S(1)} %turn.3.refs_0_), channel_id=1, source_target_pairs={{0,1},{1,0},{2,3},{3,2},{4,5},{5,4},{6,7},{7,6},{8,9},{9,8},{10,11... | collective-permute-start | bytes 1867784 | tf_op jit(solution)/shard_map/ppermute | solution.py:448

commit v5 on v4

--- a/solution.py
+++ b/solution.py
@@ -474,9 +474,10 @@
     far_message, mine = lax.optimization_barrier((far_message, mine))
     far_plane = exchange(far_message)
     outs = settle([(0, mine, mine_too)], flags, master, moment1, moment2, ())
-    before, after, far_plane, outs = lax.optimization_barrier((before, after, far_plane, outs))
+    before, after, outs = lax.optimization_barrier((before, after, outs))
+    before_too, after_too = swap(before), swap(after)
     (far,) = turn(far_plane)
-    before_too, after_too, far_too = swap(before), swap(after), swap(far)
+    far_too = swap(far)
     outs = settle([(3, before, before_too), (1, after, after_too)], flags, master, moment1, moment2, outs)
     far_too, outs = lax.optimization_barrier((far_too, outs))
     steps, *states = settle([(2, far, far_too)], flags, master, moment1, moment2, outs)

time: 76 us -> 75.4 us (level)
  waiting for transfers between devices: 19.1 us -> 17 us
  Pallas kernels: 26.6 us -> 27.6 us
    all_to_all x2, waiting for transfers between devices: 12.5 us -> 3.17 us  [exchange(): lax.all_to_all(message.reshape(PLANE * rows, BS), 'row', split_axis=0, co...]
    ppermute x1, waiting for transfers between devices: 0.01 us -> 8.52 us  [local(): before = lax.ppermute(right, 'z', RIGHT)]
    ppermute x4, waiting for transfers between devices: 1.83 us -> 0.56 us  [swap(): return lax.ppermute(piece, 'core', [(0, 1), (1, 0)])]
    pallas_call x3, Pallas kernels: 5.18 us -> 6.23 us  [settle(): pl.pallas_call(kernel, in_specs=[VMEM] * (len(arrays) + 4) + [HBM] * len(...]
  transfers between devices with their start and end apart: 10 -> 10, of which waited for: 5 -> 6; matrix products, arithmetic and copies ran while one was open for 0% -> 0% of each run, Pallas kernels for 25% -> 27%
where the time goes in v5:
time: 75.4 us; the launch traced here: 74.7 us
  starting transfers between devices  27.9 us (37%)
  Pallas kernels  27.6 us (37%)
  waiting for transfers between devices  17 us (23%)
  local copies, waits for them, and re-layouts  1.32 us (2%)
  between operations  0.77 us (1%)
    pallas_call x2, Pallas kernels, feedback(): pl.pallas_call(kernel, in_specs=[SMEM] + [HBM] * 2 + [HBM] * len(more), o...  12.5 us
    all_to_all x1, starting transfers between devices, local(): lax.all_to_all(send, ('row', 'z', 'core'), split_axis=0, concat_axis=0, t...  11.5 us
    ppermute x1, waiting for transfers between devices, local(): before = lax.ppermute(right, 'z', RIGHT)  8.52 us
    all_to_all x2, starting transfers between devices, exchange(): lax.all_to_all(message.reshape(PLANE * rows, BS), 'row', split_axis=0, co...  7.19 us
    pallas_call x3, Pallas kernels, settle(): pl.pallas_call(kernel, in_specs=[VMEM] * (len(arrays) + 4) + [HBM] * len(...  6.23 us
    ppermute x4, starting transfers between devices, swap(): return lax.ppermute(piece, 'core', [(0, 1), (1, 0)])  4.92 us
    all_to_all x1, waiting for transfers between devices, local(): lax.all_to_all(send, ('row', 'z', 'core'), split_axis=0, concat_axis=0, t...  4.74 us
    pallas_call x1, Pallas kernels, pack(): pl.pallas_call(pack_kernel, in_specs=[HBM] * 6, out_specs=VMEM, out_shape...  3.63 us
  transfers between devices with their start and end apart: 10, of which 6 were waited for; matrix products, arithmetic and copies ran while one was open for 0% of the time, Pallas kernels for 27%

profile of v5, /device:TPU:1, one launch (start us, length us, event | category | flops | bytes accessed | tf_op | source)
XLA Modules:
  0.0 74.7 jit_solution(4644583410075014444)
XLA Ops:
  0.6 3.6 %pack_rows.1 = s32[1024,128]{1,0:T(8,128)} custom-call(s32[1,7]{1,0:T(1,128)} %refs_0_.3, bf16[144,128,128]{2,1,0:T(8,128)(2,1)} %refs_1_.3, f32[144,128,128]{2,1,0:T(8,128)} %refs_2_.3, f32[2,128,128]{2,1,0:T(8,128)} %refs_3_.3, f32[2,128,128]{2,1,0:T(8,128)} %refs_4_.3, f32[2,128,128]{2,1,0:T(8,128)} %refs_5_.5), custom_call_target="tpu_custom_call" | custom-call | flops 200000 | bytes 2200000 | tf_op jit(solution)/shard_map/pack_rows/pallas_call | solution.py:132
  4.3 11.5 %all-to-all-start = ((s32[128,8,128]{2,1,0:T(8,128)}), s32[128,8,128]{2,1,0:T(8,128)S(1)}, u32[]{:S(2)}, u32[]{:S(2)}) async-start(s32[128,8,128]{2,1,0:T(8,128)} %bitcast.3), calls=%async_computation | async-start | bytes 1048576 | tf_op jit(solution)/shard_map/all_to_all | solution.py:453
  15.8 0.0 copy-start.3
  15.8 0.6 copy-done.3
  16.4 0.0 copy-start.4
  16.4 0.7 copy-done.4
  17.1 1.3 %slot_maps.1 = (bf16[144,256]{1,0:T(8,128)(2,1)S(1)}, bf16[512,256]{1,0:T(8,128)(2,1)S(1)}, bf16[16,256]{1,0:T(8,128)(2,1)S(1)}) custom-call(s32[17]{0:T(128)S(1)} %copy-done.3, s32[9]{0:T(128)S(1)} %copy-done.4), custom_call_target="tpu_custom_call" | custom-call | flops 500000 | bytes 300000 | tf_op jit(solution)/shard_map/slot_maps/pallas_call | solution.py:240
  18.4 6.3 %error_feedback.2.refs_3_ = f32[144,128,128]{2,1,0:T(8,128)} custom-call(s32[1,7]{1,0:T(1,128)} %refs_0_.3, bf16[144,128,128]{2,1,0:T(8,128)(2,1)} %refs_1_.3, f32[144,128,128]{2,1,0:T(8,128)} %refs_2_.3), custom_call_target="tpu_custom_call" | custom-call | flops 2500000 | bytes 11800000 | tf_op jit(solution)/shard_map/error_feedback/pallas_call | solution.py:183
  24.6 4.7 %all-to-all-done = s32[128,8,128]{2,1,0:T(8,128)S(1)} async-done(((s32[128,8,128]{2,1,0:T(8,128)}), s32[128,8,128]{2,1,0:T(8,128)S(1)}, u32[]{:S(2)}, u32[]{:S(2)}) %all-to-all-start) | async-done | bytes 524320 | tf_op jit(solution)/shard_map/all_to_all | solution.py:453
  29.4 1.6 %directions.1 = (bf16[16,168,128]{2,1,0:T(8,128)(2,1)}, bf16[272,128]{1,0:T(8,128)(2,1)S(1)}, f32[16,128]{1,0:T(8,128)S(1)}) custom-call(s32[1024,128]{1,0:T(8,128)S(1)} %bitcast.2, bf16[144,256]{1,0:T(8,128)(2,1)S(1)} %get-tuple-element.47.slot_map, bf16[512,256]{1,0:T(8,128)(2,1)S(1)} %get-tuple-element.48.block_map, ...), custom_call_target="tpu_custom_call" | custom-call | flops 200000000 | bytes 2000000 | tf_op jit(solution)/shard_map/directions/pallas_call | solution.py:311
  31.0 3.6 %all-to-all-start.1 = ((bf16[16,168,128]{2,1,0:T(8,128)(2,1)}), bf16[16,168,128]{2,1,0:T(8,128)(2,1)S(1)}, u32[]{:S(2)}, u32[]{:S(2)}) async-start(bf16[16,168,128]{2,1,0:T(8,128)(2,1)} %get-tuple-element.52), calls=%async_computation.1 | async-start | bytes 1376256 | tf_op jit(solution)/shard_map/all_to_all | solution.py:461
  34.6 0.0 copy-start
  34.6 0.0 copy-start.1
  34.6 0.0 copy-start.2
  34.6 1.7 %collective-permute-start = (bf16[272,128]{1,0:T(8,128)(2,1)S(1)}, bf16[272,128]{1,0:T(8,128)(2,1)S(1)}, u32[]{:S(2)}, u32[]{:S(2)}) collective-permute-start(bf16[272,128]{1,0:T(8,128)(2,1)S(1)} %get-tuple-element.53), channel_id=1, source_target_pairs={{0,4},{2,6},{4,0},{6,2},{1,5},{3,7},{5,1},{7,3},{8,12},{10,14},{12... | collective-permute-start | bytes 208904 | tf_op jit(solution)/shard_map/ppermute | solution.py:466
  36.3 6.3 %error_feedback.3 = f32[144,128,128]{2,1,0:T(8,128)} custom-call(s32[1,7]{1,0:T(1,128)} %refs_0_.3, bf16[144,128,128]{2,1,0:T(8,128)(2,1)} %refs_1_.3, f32[144,128,128]{2,1,0:T(8,128)} %refs_2_.3, f32[144,128,128]{2,1,0:T(8,128)} %error_feedback.2.refs_3_), custom_call_target="tpu_custom_call", output_to_operand_aliasing={{}: (3, {})} | custom-call | flops 2500000 | bytes 11800000 | tf_op jit(solution)/shard_map/error_feedback/pallas_call | solution.py:183
  42.5 0.0 collective-permute-done.got
  42.5 0.9 %relay.1 = bf16[16,152,128]{2,1,0:T(8,128)(2,1)} custom-call(bf16[272,128]{1,0:T(8,128)(2,1)S(1)} %collective-permute-done.got), custom_call_target="tpu_custom_call" | custom-call | bytes 700000 | tf_op jit(solution)/shard_map/relay/pallas_call | solution.py:371
  43.5 2.9 %all-to-all-done.1.rows = bf16[16,168,128]{2,1,0:T(8,128)(2,1)S(1)} async-done(((bf16[16,168,128]{2,1,0:T(8,128)(2,1)}), bf16[16,168,128]{2,1,0:T(8,128)(2,1)S(1)}, u32[]{:S(2)}, u32[]{:S(2)}) %all-to-all-start.1) | async-done | bytes 688160 | tf_op jit(solution)/shard_map/all_to_all | solution.py:461
  46.4 1.3 %turn.2 = (bf16[152,16,128]{2,1,0:T(8,128)(2,1)S(1)}, bf16[152,16,128]{2,1,0:T(8,128)(2,1)}, bf16[152,16,128]{2,1,0:T(8,128)(2,1)}) custom-call(bf16[16,168,128]{2,1,0:T(8,128)(2,1)S(1)} %all-to-all-done.1.rows), custom_call_target="tpu_custom_call" | custom-call | flops 600000 | bytes 2000000 | tf_op jit(solution)/shard_map/turn/pallas_call | solution.py:352
  47.7 2.4 %collective-permute-start.4 = (bf16[152,16,128]{2,1,0:T(8,128)(2,1)S(1)}, bf16[152,16,128]{2,1,0:T(8,128)(2,1)}, u32[]{:S(2)}, u32[]{:S(2)}) collective-permute-start(bf16[152,16,128]{2,1,0:T(8,128)(2,1)S(1)} %get-tuple-element.62.refs_0_), channel_id=1, source_target_pairs={{0,1},{1,0},{2,3},{3,2},{4,5},{5,4},{6,7},{7,6},{8,9},{9,8},{10,11... | collective-permute-start | bytes 1867784 | tf_op jit(solution)/shard_map/ppermute | solution.py:448
  50.1 0.1 collective-permute-start.2
  50.2 2.6 %collective-permute-start.3 = (bf16[152,16,128]{2,1,0:T(8,128)(2,1)}, bf16[152,16,128]{2,1,0:T(8,128)(2,1)S(1)}, u32[]{:S(2)}, u32[]{:S(2)}) collective-permute-start(bf16[152,16,128]{2,1,0:T(8,128)(2,1)} %get-tuple-element.61), channel_id=1, source_target_pairs={{0,6},{2,0},{4,2},{6,4},{1,7},{3,1},{5,3},{7,5},{8,14},{10,8},{12,... | collective-permute-start | bytes 1867784 | tf_op jit(solution)/shard_map/ppermute | solution.py:472
  52.8 3.6 %all-to-all-start.2 = ((bf16[16,152,128]{2,1,0:T(8,128)(2,1)}), bf16[16,152,128]{2,1,0:T(8,128)(2,1)S(1)}, u32[]{:S(2)}, u32[]{:S(2)}) async-start(bf16[16,152,128]{2,1,0:T(8,128)(2,1)} %relay.1), calls=%async_computation.2 | async-start | bytes 1245184 | tf_op jit(solution)/shard_map/all_to_all | solution.py:461
  56.4 0.0 collective-permute-done.4.refs_1_
  56.4 0.0 copy-done
  56.4 0.0 copy-done.1
  56.4 0.0 copy-done.2
  56.4 2.2 %settle.3 = (bf16[144,128,128]{2,1,0:T(8,128)(2,1)}, f32[2,128,128]{2,1,0:T(8,128)}, f32[2,128,128]{2,1,0:T(8,128)}, f32[2,128,128]{2,1,0:T(8,128)}) custom-call(bf16[152,16,128]{2,1,0:T(8,128)(2,1)S(1)} %get-tuple-element.62.refs_0_, bf16[152,16,128]{2,1,0:T(8,128)(2,1)} %collective-permute-done.4.refs_1_, f32[16,128]{1,0:T(8,128)S(1)} %get-tuple-element.63.refs_2_.refs_4_, ...), custom_call_target="tpu_custom_call" | custom-call | flops 600000 | bytes 2400000 | tf_op jit(solution)/shard_map/settle/pallas_call | solution.py:425
  58.7 8.5 %collective-permute-done.2.refs_0_ = bf16[152,16,128]{2,1,0:T(8,128)(2,1)S(1)} collective-permute-done((bf16[152,16,128]{2,1,0:T(8,128)(2,1)}, bf16[152,16,128]{2,1,0:T(8,128)(2,1)S(1)}, u32[]{:S(2)}, u32[]{:S(2)}) %collective-permute-start.2) | collective-permute-done | bytes 622624 | tf_op jit(solution)/shard_map/ppermute | solution.py:471
  67.2 0.0 collective-permute-done.3.refs_2_
  67.2 0.8 %collective-permute-start.5 = (bf16[152,16,128]{2,1,0:T(8,128)(2,1)S(1)}, bf16[152,16,128]{2,1,0:T(8,128)(2,1)S(1)}, u32[]{:S(2)}, u32[]{:S(2)}) collective-permute-start(bf16[152,16,128]{2,1,0:T(8,128)(2,1)S(1)} %collective-permute-done.2.refs_0_), channel_id=1, source_target_pairs={{0,1},{1,0},{2,3},{3,2},{4,5},{5,4},{6,7},{7,6},{8,9},{9,8},{10,11... | collective-permute-start | bytes 1867784 | tf_op jit(solution)/shard_map/ppermute | solution.py:448
  68.0 0.0 collective-permute-start.6
  68.0 0.2 all-to-all-done.2.rows
  68.2 0.1 turn.3.refs_0_
  68.4 1.8 %collective-permute-start.1 = (bf16[152,16,128]{2,1,0:T(8,128)(2,1)S(1)}, bf16[152,16,128]{2,1,0:T(8,128)(2,1)S(1)}, u32[]{:S(2)}, u32[]{:S(2)}) collective-permute-start(bf16[152,16,128]{2,1,0:T(8,128)(2,1)S(1)} %turn.3.refs_0_), channel_id=1, source_target_pairs={{0,1},{1,0},{2,3},{3,2},{4,5},{5,4},{6,7},{7,6},{8,9},{9,8},{10,11... | collective-permute-start | bytes 1867784 | tf_op jit(solution)/shard_map/ppermute | solution.py:448
  70.1 0.4 collective-permute-done.5.refs_1_
  70.5 0.2 collective-permute-done.6.refs_3_
  70.7 2.8 %settle.4 = (bf16[144,128,128]{2,1,0:T(8,128)(2,1)}, f32[2,128,128]{2,1,0:T(8,128)}, f32[2,128,128]{2,1,0:T(8,128)}, f32[2,128,128]{2,1,0:T(8,128)}) custom-call(bf16[152,16,128]{2,1,0:T(8,128)(2,1)S(1)} %collective-permute-done.2.refs_0_, ...), custom_call_target="tpu_custom_call", output_to_operand_aliasing={{0}: (8, {}), {1}: (9, {}), {2}: (10, {}), {3}: (11, {})} | custom-call | flops 600000 | bytes 2400000 | tf_op jit(solution)/shard_map/settle/pallas_call | solution.py:425
  73.5 0.0 collective-permute-done.1.refs_1_
  73.5 1.2 %settle.5 = (bf16[144,128,128]{2,1,0:T(8,128)(2,1)}, f32[2,128,128]{2,1,0:T(8,128)}, f32[2,128,128]{2,1,0:T(8,128)}, f32[2,128,128]{2,1,0:T(8,128)}) custom-call(bf16[152,16,128]{2,1,0:T(8,128)(2,1)S(1)} %turn.3.refs_0_, ...), custom_call_target="tpu_custom_call", output_to_operand_aliasing={{0}: (6, {}), {1}: (7, {}), {2}: (8, {}), {3}: (9, {})} | custom-call | flops 600000 | bytes 2400000 | tf_op jit(solution)/shard_map/settle/pallas_call | solution.py:425
Async XLA Ops:
  4.3 25.1 %all-to-all-start = ((s32[128,8,128]{2,1,0:T(8,128)}), s32[128,8,128]{2,1,0:T(8,128)S(1)}, u32[]{:S(2)}, u32[]{:S(2)}) async-start(s32[128,8,128]{2,1,0:T(8,128)} %bitcast.3), calls=%async_computation | async-start | bytes 1048576 | tf_op jit(solution)/shard_map/all_to_all | solution.py:453
  15.8 0.7 copy-start.3
  16.4 0.7 copy-start.4
  31.0 15.4 %all-to-all-start.1 = ((bf16[16,168,128]{2,1,0:T(8,128)(2,1)}), bf16[16,168,128]{2,1,0:T(8,128)(2,1)S(1)}, u32[]{:S(2)}, u32[]{:S(2)}) async-start(bf16[16,168,128]{2,1,0:T(8,128)(2,1)} %get-tuple-element.52), calls=%async_computation.1 | async-start | bytes 1376256 | tf_op jit(solution)/shard_map/all_to_all | solution.py:461
  34.6 21.8 %copy-start = (f32[2,128,128]{2,1,0:T(8,128)S(1)}, f32[2,128,128]{2,1,0:T(8,128)}, u32[]{:S(2)}) copy-start(f32[2,128,128]{2,1,0:T(8,128)} %refs_3_.3) | copy-start | bytes 393220
  34.6 21.8 %copy-start.1 = (f32[2,128,128]{2,1,0:T(8,128)S(1)}, f32[2,128,128]{2,1,0:T(8,128)}, u32[]{:S(2)}) copy-start(f32[2,128,128]{2,1,0:T(8,128)} %refs_4_.3) | copy-start | bytes 393220
  34.6 21.8 %copy-start.2 = (f32[2,128,128]{2,1,0:T(8,128)S(1)}, f32[2,128,128]{2,1,0:T(8,128)}, u32[]{:S(2)}) copy-start(f32[2,128,128]{2,1,0:T(8,128)} %refs_5_.5) | copy-start | bytes 393220
  34.6 7.9 %collective-permute-start = (bf16[272,128]{1,0:T(8,128)(2,1)S(1)}, bf16[272,128]{1,0:T(8,128)(2,1)S(1)}, u32[]{:S(2)}, u32[]{:S(2)}) collective-permute-start(bf16[272,128]{1,0:T(8,128)(2,1)S(1)} %get-tuple-element.53), channel_id=1, source_target_pairs={{0,4},{2,6},{4,0},{6,2},{1,5},{3,7},{5,1},{7,3},{8,12},{10,14},{12... | collective-permute-start | bytes 208904 | tf_op jit(solution)/shard_map/ppermute | solution.py:466
  47.7 8.7 %collective-permute-start.4 = (bf16[152,16,128]{2,1,0:T(8,128)(2,1)S(1)}, bf16[152,16,128]{2,1,0:T(8,128)(2,1)}, u32[]{:S(2)}, u32[]{:S(2)}) collective-permute-start(bf16[152,16,128]{2,1,0:T(8,128)(2,1)S(1)} %get-tuple-element.62.refs_0_), channel_id=1, source_target_pairs={{0,1},{1,0},{2,3},{3,2},{4,5},{5,4},{6,7},{7,6},{8,9},{9,8},{10,11... | collective-permute-start | bytes 1867784 | tf_op jit(solution)/shard_map/ppermute | solution.py:448
  50.1 17.1 %collective-permute-start.2 = (bf16[152,16,128]{2,1,0:T(8,128)(2,1)}, bf16[152,16,128]{2,1,0:T(8,128)(2,1)S(1)}, u32[]{:S(2)}, u32[]{:S(2)}) collective-permute-start(bf16[152,16,128]{2,1,0:T(8,128)(2,1)} %get-tuple-element.60), channel_id=1, source_target_pairs={{0,2},{2,4},{4,6},{6,0},{1,3},{3,5},{5,7},{7,1},{8,10},{10,12},{12... | collective-permute-start | bytes 1867784 | tf_op jit(solution)/shard_map/ppermute | solution.py:471
  50.2 17.0 %collective-permute-start.3 = (bf16[152,16,128]{2,1,0:T(8,128)(2,1)}, bf16[152,16,128]{2,1,0:T(8,128)(2,1)S(1)}, u32[]{:S(2)}, u32[]{:S(2)}) collective-permute-start(bf16[152,16,128]{2,1,0:T(8,128)(2,1)} %get-tuple-element.61), channel_id=1, source_target_pairs={{0,6},{2,0},{4,2},{6,4},{1,7},{3,1},{5,3},{7,5},{8,14},{10,8},{12,... | collective-permute-start | bytes 1867784 | tf_op jit(solution)/shard_map/ppermute | solution.py:472
  52.8 15.4 %all-to-all-start.2 = ((bf16[16,152,128]{2,1,0:T(8,128)(2,1)}), bf16[16,152,128]{2,1,0:T(8,128)(2,1)S(1)}, u32[]{:S(2)}, u32[]{:S(2)}) async-start(bf16[16,152,128]{2,1,0:T(8,128)(2,1)} %relay.1), calls=%async_computation.2 | async-start | bytes 1245184 | tf_op jit(solution)/shard_map/all_to_all | solution.py:461
  67.2 3.3 %collective-permute-start.5 = (bf16[152,16,128]{2,1,0:T(8,128)(2,1)S(1)}, bf16[152,16,128]{2,1,0:T(8,128)(2,1)S(1)}, u32[]{:S(2)}, u32[]{:S(2)}) collective-permute-start(bf16[152,16,128]{2,1,0:T(8,128)(2,1)S(1)} %collective-permute-done.2.refs_0_), channel_id=1, source_target_pairs={{0,1},{1,0},{2,3},{3,2},{4,5},{5,4},{6,7},{7,6},{8,9},{9,8},{10,11... | collective-permute-start | bytes 1867784 | tf_op jit(solution)/shard_map/ppermute | solution.py:448
  68.0 2.7 %collective-permute-start.6 = (bf16[152,16,128]{2,1,0:T(8,128)(2,1)S(1)}, bf16[152,16,128]{2,1,0:T(8,128)(2,1)}, u32[]{:S(2)}, u32[]{:S(2)}) collective-permute-start(bf16[152,16,128]{2,1,0:T(8,128)(2,1)S(1)} %collective-permute-done.3.refs_2_), channel_id=1, source_target_pairs={{0,1},{1,0},{2,3},{3,2},{4,5},{5,4},{6,7},{7,6},{8,9},{9,8},{10,11... | collective-permute-start | bytes 1867784 | tf_op jit(solution)/shard_map/ppermute | solution.py:448
  68.4 5.1 %collective-permute-start.1 = (bf16[152,16,128]{2,1,0:T(8,128)(2,1)S(1)}, bf16[152,16,128]{2,1,0:T(8,128)(2,1)S(1)}, u32[]{:S(2)}, u32[]{:S(2)}) collective-permute-start(bf16[152,16,128]{2,1,0:T(8,128)(2,1)S(1)} %turn.3.refs_0_), channel_id=1, source_target_pairs={{0,1},{1,0},{2,3},{3,2},{4,5},{5,4},{6,7},{7,6},{8,9},{9,8},{10,11... | collective-permute-start | bytes 1867784 | tf_op jit(solution)/shard_map/ppermute | solution.py:448
